TPU v7x, 32 devices: a whole 2x2x4 slice. The times are simulated.
32 devices in a mesh: dp: 16 (over z, x, core), mp: 2 (over y).
Axes of the slice: x: 2, y: 2, z: 4, core: 2. Of those that a mesh axis runs over, the one named last changes fastest.
Arguments:
- frames_in: bfloat16 [8, 4096, 1024], P('mp', 'dp'), may hold values from -6 to 6
- delays: int32 [8], P('mp'), may hold values from 1 to 2, as said below
- item_bounds: int32 [2], replicated, may hold values from 1 to 4095, as said below
- attn_gain: float32 [8, 1024], P('mp'), may hold values from 0.1 to 1.9
- ffn_gain: float32 [8, 1024], P('mp'), may hold values from 0.1 to 1.9
- w_qkv: bfloat16 [8, 3, 1024, 1024], P(None, None, None, 'mp'), may hold values from -0.1875 to 0.1875
- w_out: bfloat16 [8, 1024, 1024], P(None, None, 'mp'), may hold values from -0.375 to 0.375
- w_gate_up: bfloat16 [8, 2, 1024, 2816], P(None, None, None, 'mp'), may hold values from -0.1875 to 0.1875
- w_down: bfloat16 [8, 1024, 2816], P(None, None, 'mp'), may hold values from -0.15625 to 0.15625
- cotangent: bfloat16 [8, 4096, 1024], P('mp', 'dp'), may hold values from -6 to 6
Outputs:
- mixed: bfloat16 [8, 4096, 1024], P('mp', 'dp')
- input_grad: float32 [8, 4096, 1024], P('mp', 'dp')
- attn_gain_grad: float32 [8, 1024], P('mp', 'dp')
- ffn_gain_grad: float32 [8, 1024], P('mp', 'dp')
- qkv_grad: float32 [8, 3, 1024, 1024], P(None, None, 'dp', 'mp')
- out_grad: float32 [8, 1024, 1024], P(None, 'dp', 'mp')
- gate_up_grad: float32 [8, 2, 1024, 2816], P(None, None, 'dp', 'mp')
- down_grad: float32 [8, 1024, 2816], P(None, 'dp', 'mp')
Inputs may be any that keep to these rules, and one draw needn't show every extreme that they name: Each position is delayed by 1 or 2 frames, and both delays occur. item_bounds[0] lies among the first 256 frames and item_bounds[1] among the last 256; items begin at frame 0 and at each bound.
All inputs are finite; a program needn't handle non-finite values.
Results may differ from a plain program's by a relative error of at most 0.012.
Values may be sent and summed in bfloat16 or wider, within the bound.
A program may use at most 640 MiB of HBM per device.

v0:
```python
import jax
import jax.numpy as jnp
from jax import lax
from jax.sharding import PartitionSpec as P

HD = 64


epsilon = 1e-05


def shifted_2(block, axis, distance):
    devices = range(lax.axis_size(axis))
    route = [(i - distance, i) for i in devices if i - distance in devices]
    return lax.ppermute(block, axis, route)


def normalize(values, gain):
    scale = lax.rsqrt(jnp.mean(values * values, axis=-1, keepdims=True) + epsilon)
    return (values * scale * gain[:, None, :], scale)


def norm_back(values, scale, gain, upstream):
    gained = gain[:, None, :] * upstream
    gain_grad = jnp.sum(upstream * values * scale, axis=1)
    value_grad = scale * gained - values * (scale * scale * scale) * jnp.mean(
        gained * values, axis=-1, keepdims=True
    )
    return (value_grad, gain_grad)


def gated_back(d_hidden, gate, up_part):
    sigma = jax.nn.sigmoid(gate)
    d_gate = d_hidden * up_part * sigma * (1.0 + gate * (1.0 - sigma))
    d_up = d_hidden * gate * sigma
    return jnp.stack([d_gate, d_up], axis=1).astype(jnp.bfloat16)


def local(
    frames_in, delays, item_bounds, attn_gain, ffn_gain, w_qkv, w_out, w_gate_up, w_down, cotangent
):
    local_pos, local_frames, model_width = frames_in.shape
    positions = w_qkv.shape[0]
    head_width = w_qkv.shape[3]
    local_heads = head_width // HD
    frame_ids = lax.axis_index("dp") * local_frames + jnp.arange(local_frames, dtype=jnp.int32)
    earlier = shifted_2(frames_in[:, local_frames - 2 :, :], "dp", 1)
    padded = jnp.concatenate([earlier, frames_in], axis=1)

    def take_frames(frame_row, shift_lag):
        return lax.dynamic_slice_in_dim(frame_row, 2 - shift_lag, local_frames, 0)

    shifted = jax.vmap(take_frames)(padded, delays)
    item_start = jnp.where(
        frame_ids >= item_bounds[1],
        item_bounds[1],
        jnp.where(frame_ids >= item_bounds[0], item_bounds[0], 0),
    )
    usable = frame_ids[None, :] - delays[:, None] >= item_start[None, :]
    resid = jnp.where(usable[:, :, None], shifted.astype(jnp.float32), 0.0)
    normed_a, scale_a = normalize(resid, attn_gain)
    normed_all = lax.all_gather(normed_a.astype(jnp.bfloat16), "mp", axis=0, tiled=True)
    qkv = jnp.einsum(
        "pfd,pcde->pcfe", normed_all, w_qkv, preferred_element_type=jnp.float32
    ).astype(jnp.bfloat16)
    split = qkv.reshape(positions, 3, local_frames, local_heads, HD)
    queries, key_rows, values = (split[:, 0], split[:, 1], split[:, 2])
    scores = (
        jnp.einsum("ifhe,jfhe->fhij", queries, key_rows, preferred_element_type=jnp.float32) * 0.125
    )
    causal = jnp.tril(jnp.ones((positions, positions), dtype=bool))
    scores = jnp.where(causal, scores, -1e30)
    probs = jax.nn.softmax(scores, axis=-1)
    probs_low = probs.astype(jnp.bfloat16)
    context = jnp.einsum("fhij,jfhe->ifhe", probs_low, values, preferred_element_type=jnp.float32)
    context = context.astype(jnp.bfloat16).reshape(positions, local_frames, head_width)
    weight_rows = w_out
    middle = resid + lax.psum_scatter(
        jnp.einsum("pfe,pde->pfd", context, weight_rows, preferred_element_type=jnp.float32),
        "mp",
        scatter_dimension=0,
        tiled=True,
    )
    normed_f, scale_f = normalize(middle, ffn_gain)
    normed_f_low = normed_f.astype(jnp.bfloat16)
    grad_in = cotangent.astype(jnp.float32)
    normed_f_all = lax.all_gather(normed_f_low, "mp", axis=0, tiled=True)
    gate_up = jnp.einsum(
        "pfd,pcdh->pcfh", normed_f_all, w_gate_up, preferred_element_type=jnp.float32
    )
    hidden = (jax.nn.silu(gate_up[:, 0]) * gate_up[:, 1]).astype(jnp.bfloat16)
    weight_rows = w_down
    mixed = (
        middle
        + lax.psum_scatter(
            jnp.einsum("pfh,pdh->pfd", hidden, weight_rows, preferred_element_type=jnp.float32),
            "mp",
            scatter_dimension=0,
            tiled=True,
        )
    ).astype(jnp.bfloat16)
    cotangent_all = lax.all_gather(cotangent, "mp", axis=0, tiled=True)
    d_hidden = jnp.einsum("pfd,pdh->pfh", cotangent_all, w_down, preferred_element_type=jnp.float32)
    down_local = jnp.einsum(
        "pfd,pfh->pdh", cotangent_all, hidden, preferred_element_type=jnp.float32
    )
    d_gate_up = gated_back(d_hidden, gate_up[:, 0], gate_up[:, 1])
    gate_up_local = jnp.einsum(
        "pfd,pcfh->pcdh", normed_f_all, d_gate_up, preferred_element_type=jnp.float32
    )
    grad_rows = d_gate_up
    weight_rows = w_gate_up
    d_normed_f = lax.psum_scatter(
        jnp.einsum("pcfh,pcdh->pfd", grad_rows, weight_rows, preferred_element_type=jnp.float32),
        "mp",
        scatter_dimension=0,
        tiled=True,
    )
    middle_grad, ffn_gain_local = norm_back(middle, scale_f, ffn_gain, d_normed_f)
    d_middle = grad_in + middle_grad
    d_middle_all = lax.all_gather(d_middle.astype(jnp.bfloat16), "mp", axis=0, tiled=True)
    out_local = jnp.einsum(
        "pfd,pfe->pde", d_middle_all, context, preferred_element_type=jnp.float32
    )
    d_context = jnp.einsum(
        "pfd,pde->pfe", d_middle_all, w_out, preferred_element_type=jnp.float32
    ).astype(jnp.bfloat16)
    d_context = d_context.reshape(positions, local_frames, local_heads, HD)
    d_probs = jnp.einsum("ifhe,jfhe->fhij", d_context, values, preferred_element_type=jnp.float32)
    d_values = jnp.einsum(
        "fhij,ifhe->jfhe", probs_low, d_context, preferred_element_type=jnp.float32
    )
    d_scores = (probs * (d_probs - jnp.sum(probs * d_probs, axis=-1, keepdims=True))).astype(
        jnp.bfloat16
    )
    d_queries = (
        jnp.einsum("fhij,jfhe->ifhe", d_scores, key_rows, preferred_element_type=jnp.float32)
        * 0.125
    )
    d_keys = (
        jnp.einsum("fhij,ifhe->jfhe", d_scores, queries, preferred_element_type=jnp.float32) * 0.125
    )
    d_qkv = (
        jnp.stack([d_queries, d_keys, d_values], axis=1)
        .reshape(positions, 3, local_frames, head_width)
        .astype(jnp.bfloat16)
    )
    qkv_local = jnp.einsum("pfd,pcfe->pcde", normed_all, d_qkv, preferred_element_type=jnp.float32)
    grad_rows = d_qkv
    weight_rows = w_qkv
    d_normed_a = lax.psum_scatter(
        jnp.einsum("pcfe,pcde->pfd", grad_rows, weight_rows, preferred_element_type=jnp.float32),
        "mp",
        scatter_dimension=0,
        tiled=True,
    )
    resid_grad, attn_gain_local = norm_back(resid, scale_a, attn_gain, d_normed_a)
    d_resid = d_middle + resid_grad
    spread = jnp.where(usable[:, :, None], d_resid, 0.0)

    def place_frames(frame_row, shift_lag):
        blank = jnp.zeros((local_frames + 2, model_width), jnp.float32)
        return lax.dynamic_update_slice_in_dim(blank, frame_row, 2 - shift_lag, 0)

    placed = jax.vmap(place_frames)(spread, delays)
    returned = shifted_2(placed[:, :2, :], "dp", -1)
    input_grad = placed[:, 2:, :] + jnp.pad(returned, ((0, 0), (local_frames - 2, 0), (0, 0)))
    qkv_grad, out_grad, gate_up_grad, down_grad, attn_gain_grad, ffn_gain_grad = (
        lax.psum_scatter(qkv_local, "dp", scatter_dimension=2, tiled=True),
        lax.psum_scatter(out_local, "dp", scatter_dimension=1, tiled=True),
        lax.psum_scatter(gate_up_local, "dp", scatter_dimension=2, tiled=True),
        lax.psum_scatter(down_local, "dp", scatter_dimension=1, tiled=True),
        lax.psum_scatter(attn_gain_local, "dp", scatter_dimension=1, tiled=True),
        lax.psum_scatter(ffn_gain_local, "dp", scatter_dimension=1, tiled=True),
    )
    return (
        mixed,
        input_grad,
        attn_gain_grad,
        ffn_gain_grad,
        qkv_grad,
        out_grad,
        gate_up_grad,
        down_grad,
    )


def solution(mesh):
    placed = (
        P("mp", "dp", None),
        P("mp"),
        P(),
        P("mp", None),
        P("mp", None),
        P(None, None, None, "mp"),
        P(None, None, "mp"),
        P(None, None, None, "mp"),
        P(None, None, "mp"),
        P("mp", "dp", None),
    )
    return jax.shard_map(
        local,
        mesh=mesh,
        in_specs=placed,
        out_specs=(
            P("mp", "dp", None),
            P("mp", "dp", None),
            P("mp", "dp"),
            P("mp", "dp"),
            P(None, None, "dp", "mp"),
            P(None, "dp", "mp"),
            P(None, None, "dp", "mp"),
            P(None, "dp", "mp"),
        ),
        check_vma=False,
    )
```

profile of v0, /device:TPU:0, one launch (start us, length us, event | category | flops | bytes accessed | tf_op | source)
XLA Modules:
  0.0 2982.2 jit_solution(2487931754177593051)
XLA Ops:
  15.9 3.5 pad_maximum_fusion.4
  19.4 12.4 while.2
  36.1 58.9 %all-gather.5.cloned.1.call-done = bf16[8,256,1024]{2,1,0:T(8,128)(2,1)} async-done(((bf16[4,256,1024]{2,1,0:T(8,128)(2,1)}), bf16[8,256,1024]{2,1,0:T(8,128)(2,1)}) %all-gather.5.cloned.1.call-update) | async-done | bytes 4194320 | tf_op jit(solution)/shard_map/all_gather | solution.py:62
  95.0 17.5 convert_bitcast_fusion
  112.5 8.6 copy.66
  121.1 5.8 fusion.51
  126.9 7.5 copy.114
  134.4 7.4 copy.113
  141.8 7.5 copy.115
  149.3 5.8 fusion.16
  155.1 6.9 fusion.53
  161.9 8.7 convert_bitcast_fusion.2
  170.7 5.9 copy.71
  176.6 9.7 fusion.54
  186.4 99.3 %reduce-scatter.15.cloned.1.call-done = f32[4,256,1024]{2,1,0:T(8,128)} async-done(((f32[8,256,1024]{2,1,0:T(8,128)}), f32[4,256,1024]{2,1,0:T(8,128)}) %reduce-scatter.15.cloned.1.call-update) | async-done | bytes 4194320 | tf_op jit(solution)/shard_map/reduce_scatter | solution.py:78
  293.3 56.3 %all-gather.7.cloned.1.call-done = bf16[8,256,1024]{2,1,0:T(8,128)(2,1)} async-done(((bf16[4,256,1024]{2,1,0:T(8,128)(2,1)}), bf16[8,256,1024]{2,1,0:T(8,128)(2,1)}) %all-gather.7.cloned.1.call-update) | async-done | bytes 4194320 | tf_op jit(solution)/shard_map/all_gather | solution.py:87
  349.6 27.5 convolution_bitcast_fusion.3
  377.1 30.8 %all-gather.9.cloned.1.call-done = bf16[8,256,1024]{2,1,0:T(8,128)(2,1)} async-done(((bf16[4,256,1024]{2,1,0:T(8,128)(2,1)}), bf16[8,256,1024]{2,1,0:T(8,128)(2,1)}) %all-gather.9.cloned.1.call-update) | async-done | bytes 4194320 | tf_op jit(solution)/shard_map/all_gather | solution.py:102
  407.9 26.1 fusion.6
  434.0 23.9 fusion.31
  457.9 99.3 %reduce-scatter.19.cloned.1.call-done = f32[4,256,1024]{2,1,0:T(8,128)} async-done(((f32[8,256,1024]{2,1,0:T(8,128)}), f32[4,256,1024]{2,1,0:T(8,128)}) %reduce-scatter.19.cloned.1.call-update) | async-done | bytes 4194320 | tf_op jit(solution)/shard_map/reduce_scatter | solution.py:113
  557.3 4.7 multiply_reduce_fusion.1
  565.6 56.9 %all-gather.11.cloned.1.call-done = bf16[8,256,1024]{2,1,0:T(8,128)(2,1)} async-done(((bf16[4,256,1024]{2,1,0:T(8,128)(2,1)}), bf16[8,256,1024]{2,1,0:T(8,128)(2,1)}) %all-gather.11.cloned.1.call-update) | async-done | bytes 4194320 | tf_op jit(solution)/shard_map/all_gather | solution.py:121
  622.4 8.3 convolution_convert_fusion
  630.7 3.2 copy.75
  634.0 6.7 copy.76
  640.6 9.0 convert_bitcast_fusion.1
  649.6 10.0 multiply_reduce_fusion
  659.6 7.3 multiply_convert_fusion.5
  667.0 4.3 fusion.8
  671.3 4.2 fusion.7
  675.5 5.1 copy.81
  683.0 5.0 copy.78
  688.0 6.0 copy.79
  693.9 3.9 copy.83
  700.2 25.6 convolution_bitcast_fusion.4
  725.9 16.2 fusion.55
  743.3 81.9 %reduce-scatter.21.cloned.1.call-done = f32[4,256,1024]{2,1,0:T(8,128)} async-done(((f32[8,256,1024]{2,1,0:T(8,128)}), f32[4,256,1024]{2,1,0:T(8,128)}) %reduce-scatter.21.cloned.1.call-update) | async-done | bytes 4194320 | tf_op jit(solution)/shard_map/reduce_scatter | solution.py:151
  825.3 3.7 multiply_reduce_fusion.2
  830.1 21.0 convolution_bitcast_fusion.1
  851.1 49.3 %copy.93 = f32[8,1024,1408]{2,0,1:T(8,128)} copy(f32[8,1024,1408]{1,2,0:T(8,128)} %convolution_bitcast_fusion.1) | data formatting | bytes 92274688 | tf_op jit(solution)/shard_map/pfd,pfh->pdh/dot_general | solution.py:104
  902.0 21.0 convolution_bitcast_fusion.2
  923.0 49.8 %copy.87 = f32[8,3,1024,512]{3,0,1,2:T(8,128)} copy(f32[8,3,1024,512]{2,3,1,0:T(8,128)} %convolution_bitcast_fusion.2) | data formatting | bytes 100663296 | tf_op jit(solution)/shard_map/pfd,pcfe->pcde/transpose | solution.py:148
  972.8 37.1 %convolution_bitcast_fusion = f32[8,2,1024,1408]{2,3,1,0:T(8,128)} fusion(bf16[8,256,1024]{2,1,0:T(8,128)(2,1)} %all-gather.7.cloned.1.call-done, bf16[8,1,256,1408]{3,2,0,1:T(8,128)(2,1)} %get-tuple-element.100, bf16[8,1,256,1408]{3,2,0,1:T(8,128)(2,1)} %get-tuple-element.99), kind=kOutput, calls=%fused_computation.6 | convolution fusion | flops 11816927232 | bytes 108003328 | tf_op jit(solution)/shard_map/pfd,pcfh->pcdh/dot_general | solution.py:108
  1009.9 102.0 %copy.91 = f32[8,2,1024,1408]{3,0,1,2:T(8,128)} copy(f32[8,2,1024,1408]{2,3,1,0:T(8,128)} %convolution_bitcast_fusion) | data formatting | bytes 184549376 | tf_op jit(solution)/shard_map/pfd,pcfh->pcdh/transpose | solution.py:108
  1113.5 11.4 fusion.56
  1126.6 10.7 add_select_fusion
  1139.8 47.8 %while.3 = (s32[]{:T(128)}, f32[4,258,1024]{2,1,0:T(8,128)}, s32[4,3]{1,0:T(4,128)S(1)}, f32[4,256,1024]{2,1,0:T(8,128)}, s32[]{:T(128)}, /*index=5*/s32[3]{0:T(128)S(1)}, s32[]{:T(128)}) while((s32[]{:T(128)}, f32[4,258,1024]{2,1,0:T(8,128)}, s32[4,3]{1,0:T(4,128)S(1)}, f32[4,256,1024]{2,1,0:T(8,128)}, s32[]{:T(128)}, /*index=5*/s32[3]{0:T(128)S(1)}, ...), condition=%wide.while_cond.1, body=%wide.while_body.1.sunk | while | flops 262163 | bytes 5243059 | solution.py:163
  1143.1 3.6 dynamic-slice_select_fusion.2
  1146.8 5.0 dynamic-update-slice.8
  1155.1 3.6 dynamic-slice_select_fusion.2
  1158.7 5.1 dynamic-update-slice.8
  1167.0 3.6 dynamic-slice_select_fusion.2
  1170.7 5.0 dynamic-update-slice.8
  1179.0 3.6 dynamic-slice_select_fusion.2
  1182.6 5.0 dynamic-update-slice.8
  1192.7 5.3 pad_add_fusion
  1198.0 283.3 %reduce-scatter.29.cloned.1.call-done = f32[8,64,1408]{2,0,1:T(8,128)} async-done(((f32[8,1024,1408]{2,0,1:T(8,128)}), f32[8,64,1408]{2,0,1:T(8,128)}) %reduce-scatter.29.cloned.1.call-update) | async-done | bytes 2883600 | tf_op jit(solution)/shard_map/reduce_scatter | solution.py:172
  1481.3 3.9 copy.96
  1485.3 467.1 %reduce-scatter.23.cloned.1.call-done = f32[8,3,64,512]{3,0,1,2:T(8,128)} async-done(((f32[8,3,1024,512]{3,0,1,2:T(8,128)}), f32[8,3,64,512]{3,0,1,2:T(8,128)}) %reduce-scatter.23.cloned.1.call-update) | async-done | bytes 3145744 | tf_op jit(solution)/shard_map/reduce_scatter | solution.py:169
  1952.3 5.4 copy.94
  1957.7 834.8 %reduce-scatter.27.cloned.1.call-done = f32[8,2,64,1408]{3,0,1,2:T(8,128)} async-done(((f32[8,2,1024,1408]{3,0,1,2:T(8,128)}), f32[8,2,64,1408]{3,0,1,2:T(8,128)}) %reduce-scatter.27.cloned.1.call-update) | async-done | bytes 5767184 | tf_op jit(solution)/shard_map/reduce_scatter | solution.py:171
  2792.5 7.0 copy.95
  2799.6 175.8 %reduce-scatter.25.cloned.1.call-done = f32[8,64,512]{2,1,0:T(8,128)} async-done(((f32[8,1024,512]{2,1,0:T(8,128)}), f32[8,64,512]{2,1,0:T(8,128)}) %reduce-scatter.25.cloned.1.call-update) | async-done | bytes 1048592 | tf_op jit(solution)/shard_map/reduce_scatter | solution.py:170
  (152 shorter events, 69.0 us)
Async XLA Ops:
  7.2 87.8 %all-gather.5.cloned.1.call-start = ((), (), s32[]{:S(2)}) async-start(), calls=%async_computation.10 | async-start | bytes 6291456 | tf_op jit(solution)/shard_map/all_gather | solution.py:62
  8.1 7.8 collective-permute-start
  14.5 271.3 %copy-start.25 = (pred[4,256]{1,0:T(4,128)(4,1)}, pred[4,256]{1,0:T(4,128)(4,1)S(1)}, u32[]{:S(2)}) copy-start(pred[4,256]{1,0:T(4,128)(4,1)S(1)} %subtract_compare_fusion) | copy-start | bytes 3076
  19.4 14.3 copy-start.13
  31.8 254.0 %copy-start.3 = (bf16[4,256,1024]{2,1,0:T(8,128)(2,1)}, bf16[4,256,1024]{2,1,0:T(8,128)(2,1)S(1)}, u32[]{:S(2)}) copy-start(bf16[4,256,1024]{2,1,0:T(8,128)(2,1)S(1)} %get-tuple-element.15) | copy-start | bytes 6291460
  33.1 0.6 copy-start.18
  35.5 250.2 %reduce-scatter.15.cloned.1.call-start = ((), (), s32[]{:S(2)}) async-start(), calls=%async_computation.11 | async-start | bytes 12582912 | tf_op jit(solution)/shard_map/reduce_scatter | solution.py:78
  186.4 104.5 %copy-start.11 = (f32[4,1024]{1,0:T(4,128)S(1)}, f32[4,1024]{1,0:T(4,128)}, u32[]{:S(2)}) copy-start(f32[4,1024]{1,0:T(4,128)} %param.14) | copy-start | bytes 49156
  186.4 163.3 %all-gather.7.cloned.1.call-start = ((), (), s32[]{:S(2)}) async-start(), calls=%async_computation.12 | async-start | bytes 6291456 | tf_op jit(solution)/shard_map/all_gather | solution.py:87
  288.9 2.0 copy-start
  288.9 273.0 %copy-start.16 = (f32[4,256]{1,0:T(4,128)}, f32[4,256]{1,0:T(4,128)S(1)}, u32[]{:S(2)}) copy-start(f32[4,256]{1,0:T(4,128)S(1)} %get-tuple-element.110) | copy-start | bytes 12292
  288.9 273.0 %copy-start.21 = (f32[4,256]{1,0:T(4,128)}, f32[4,256]{1,0:T(4,128)S(1)}, u32[]{:S(2)}) copy-start(f32[4,256]{1,0:T(4,128)S(1)} %get-tuple-element.109) | copy-start | bytes 12292
  292.7 115.2 %all-gather.9.cloned.1.call-start = ((), (), s32[]{:S(2)}) async-start(), calls=%async_computation.14 | async-start | bytes 6291456 | tf_op jit(solution)/shard_map/all_gather | solution.py:102
  293.3 264.0 %reduce-scatter.19.cloned.1.call-start = ((), (), s32[]{:S(2)}) async-start(), calls=%async_computation.15 | async-start | bytes 12582912 | tf_op jit(solution)/shard_map/reduce_scatter | solution.py:113
  457.8 104.7 %copy-start.8 = (bf16[4,256,1024]{2,1,0:T(8,128)(2,1)S(1)}, bf16[4,256,1024]{2,1,0:T(8,128)(2,1)}, u32[]{:S(2)}) copy-start(bf16[4,256,1024]{2,1,0:T(8,128)(2,1)} %param.19) | copy-start | bytes 6291460
  457.9 164.6 %all-gather.11.cloned.1.call-start = ((), (), s32[]{:S(2)}) async-start(), calls=%async_computation.16 | async-start | bytes 6291456 | tf_op jit(solution)/shard_map/all_gather | solution.py:121
  557.3 5.3 copy-start.1
  557.3 5.9 copy-start.7
  561.9 0.6 copy-start.23
  565.5 259.7 %reduce-scatter.21.cloned.1.call-start = ((), (), s32[]{:S(2)}) async-start(), calls=%async_computation.17 | async-start | bytes 12582912 | tf_op jit(solution)/shard_map/reduce_scatter | solution.py:151
  659.6 7.4 copy-start.6
  667.0 4.3 copy-start.2
  725.9 399.8 %reduce-scatter.17.cloned.1.call-start = ((), (), s32[]{:S(2)}) async-start(), calls=%async_computation.13 | async-start | bytes 12582912 | tf_op jit(solution)/shard_map/reduce_scatter | solution.py:95
  742.1 83.1 %copy-start.4 = (bf16[4,256,1024]{2,1,0:T(8,128)(2,1)S(1)}, bf16[4,256,1024]{2,1,0:T(8,128)(2,1)}, u32[]{:S(2)}) copy-start(bf16[4,256,1024]{2,1,0:T(8,128)(2,1)} %copy-done.3) | copy-start | bytes 6291460
  742.1 83.1 %copy-start.14 = (f32[4,1024]{1,0:T(4,128)S(1)}, f32[4,1024]{1,0:T(4,128)}, u32[]{:S(2)}) copy-start(f32[4,1024]{1,0:T(4,128)} %param.13) | copy-start | bytes 49156
  742.1 83.1 %copy-start.19 = (f32[4,256]{1,0:T(4,128)S(1)}, f32[4,256]{1,0:T(4,128)}, u32[]{:S(2)}) copy-start(f32[4,256]{1,0:T(4,128)} %copy-done.18) | copy-start | bytes 12292
  742.1 83.1 %copy-start.26 = (pred[4,256]{1,0:T(4,128)(4,1)S(1)}, pred[4,256]{1,0:T(4,128)(4,1)}, u32[]{:S(2)}) copy-start(pred[4,256]{1,0:T(4,128)(4,1)} %copy-done.25) | copy-start | bytes 3076
  742.2 447.7 %reduce-scatter.33.cloned.1.call-start = ((), (), s32[]{:S(2)}) async-start(), calls=%async_computation.23 | async-start | bytes 557056
  743.3 448.0 %reduce-scatter.31.cloned.1.call-start = ((), (), s32[]{:S(2)}) async-start(), calls=%async_computation.22 | async-start | bytes 557056
  830.0 651.3 %reduce-scatter.29.cloned.1.call-start = ((), (), s32[]{:S(2)}) async-start(), calls=%async_computation.21 | async-start | bytes 49020928 | tf_op jit(solution)/shard_map/reduce_scatter | solution.py:172
  900.4 1.6 copy-start.10
  900.4 1051.9 %reduce-scatter.23.cloned.1.call-start = ((), (), s32[]{:S(2)}) async-start(), calls=%async_computation.18 | async-start | bytes 53477376 | tf_op jit(solution)/shard_map/reduce_scatter | solution.py:169
  972.8 1819.8 %reduce-scatter.27.cloned.1.call-start = ((), (), s32[]{:S(2)}) async-start(), calls=%async_computation.20 | async-start | bytes 98041856 | tf_op jit(solution)/shard_map/reduce_scatter | solution.py:171
  1111.9 1.6 copy-start.9
  1111.9 1863.5 %reduce-scatter.25.cloned.1.call-start = ((), (), s32[]{:S(2)}) async-start(), calls=%async_computation.19 | async-start | bytes 17825792 | tf_op jit(solution)/shard_map/reduce_scatter | solution.py:170
  1124.9 0.7 copy-start.31
  1124.9 0.8 copy-start.28
  1124.9 1.6 copy-start.5
  1124.9 1.6 copy-start.12
  1124.9 1.6 copy-start.15
  1124.9 1.6 copy-start.17
  1124.9 1.6 copy-start.20
  1124.9 1.6 copy-start.22
  1124.9 1.6 copy-start.24
  1125.0 1.6 copy-start.27
  1125.0 1.6 copy-start.29
  1137.2 2.6 copy-start.30
  1188.6 4.2 collective-permute-start.1
Sparse Core Ops, SparseCore 0:
  35.6 59.3 all-gather.4
  186.5 99.2 reduce-scatter.14
  292.8 56.7 all-gather.6
  351.1 56.7 all-gather.8
  458.0 99.2 reduce-scatter.18
  565.6 56.7 all-gather.10
  726.0 99.2 reduce-scatter.20
  827.6 99.2 reduce-scatter.16
  930.5 55.7 reduce-scatter.32
  990.1 54.7 reduce-scatter.30
  1049.2 432.1 reduce-scatter.28
  1485.4 466.8 reduce-scatter.22
  1956.5 835.9 reduce-scatter.26
  2797.6 177.6 reduce-scatter.24
where the time goes:
time: 2990 us; the launch traced here: 2980 us
  waiting for transfers between devices  2250 us (75%)
  local copies, waits for them, and re-layouts  348 us (12%)
  matrix products  287 us (10%)
  other arithmetic  81.7 us (3%)
    reduce_scatter x1, waiting for transfers between devices, local(): lax.psum_scatter(gate_up_local, 'dp', scatter_dimension=2, tiled=True)  835 us
    reduce_scatter x1, waiting for transfers between devices, local(): lax.psum_scatter(qkv_local, 'dp', scatter_dimension=2, tiled=True)  467 us
    reduce_scatter x1, waiting for transfers between devices, local(): lax.psum_scatter(down_local, 'dp', scatter_dimension=1, tiled=True)  283 us
    reduce_scatter x1, waiting for transfers between devices, local(): lax.psum_scatter(out_local, 'dp', scatter_dimension=1, tiled=True)  176 us
    transpose x1, local copies, waits for them, and re-layouts, local(): jnp.einsum('pfd,pcfh->pcdh', normed_f_all, d_gate_up, preferred_element_t...  102 us
    reduce_scatter x1, waiting for transfers between devices, local(): lax.psum_scatter(jnp.einsum('pcfh,pcdh->pfd', grad_rows, weight_rows, pre...  99.3 us
    reduce_scatter x1, waiting for transfers between devices, local(): lax.psum_scatter(jnp.einsum('pfe,pde->pfd', context, weight_rows, preferr...  99.3 us
    reduce_scatter x1, waiting for transfers between devices, local(): lax.psum_scatter(jnp.einsum('pcfe,pcde->pfd', grad_rows, weight_rows, pre...  81.9 us
  transfers between devices with their start and end apart: 16, of which 11 were waited for; matrix products, arithmetic and copies ran while one was open for 15% of the time, Pallas kernels for 0%

commit v1 on v0

v1 whole, which is shorter than its diff:
```python
import functools

import jax
import jax.numpy as jnp
from jax import lax
from jax.experimental import pallas as pl
from jax.experimental.pallas import tpu as pltpu
from jax.sharding import PartitionSpec as P

HD = 64
EPSILON = 1e-05
BF16 = jnp.bfloat16
F32 = jnp.float32


def shift_frames(block, distance):
    devices = range(lax.axis_size("dp"))
    route = [(i - distance, i) for i in devices if i - distance in devices]
    return lax.ppermute(block, "dp", route)


def at(array, index, axis=0):
    return lax.dynamic_index_in_dim(array, index, axis, keepdims=False)


class Group:
    def __init__(self, positions, local_pos):
        self.dp, self.mp = lax.axis_size("dp"), lax.axis_size("mp")
        power = local_pos & (local_pos - 1) == 0
        self.size = local_pos if power and self.dp % local_pos == 0 else 1
        self.outer = self.dp // self.size
        self.member = lax.axis_index("dp") % self.size
        self.m = lax.axis_index("mp")

    def swap(self, block):
        return lax.ppermute(block, "mp", [(0, 1), (1, 0)])

    def gather(self, block):
        if self.mp != 2:
            return lax.all_gather(block, "mp", axis=0)
        other = self.swap(block)
        first = self.m == 0
        return jnp.stack([jnp.where(first, block, other), jnp.where(first, other, block)])

    def scatter(self, blocks):
        if self.mp != 2:
            return lax.psum_scatter(blocks, "mp", scatter_dimension=0, tiled=False)
        other = self.swap(at(blocks, 1 - self.m).astype(BF16))
        return at(blocks, self.m) + other.astype(F32)

    def route(self, step):
        return [(i, i ^ step) for i in range(self.dp)]

    def spread(self, blocks):
        got = [at(blocks, self.member)]
        for step in range(1, self.size):
            got.append(lax.ppermute(at(blocks, self.member ^ step), "dp", self.route(step)))
        return jnp.stack(got)

    def unspread(self, blocks):
        got = [blocks[0]]
        for step in range(1, self.size):
            got.append(lax.ppermute(blocks[step], "dp", self.route(step)))
        return self.in_order(jnp.stack(got))

    def in_order(self, blocks):
        bit = 1
        while bit < self.size:
            flipped = blocks.reshape((self.size // (2 * bit), 2, bit) + blocks.shape[1:])[:, ::-1]
            flipped = flipped.reshape(blocks.shape)
            blocks = jnp.where((self.member & bit) != 0, flipped, blocks)
            bit *= 2
        return blocks

    def by_position(self, blocks):
        got = self.spread(jnp.swapaxes(blocks, 0, 1))
        return jnp.swapaxes(got, 0, 1).reshape(self.mp, -1, blocks.shape[-1])

    def sum_scatter(self, values):
        dp = self.dp
        if dp & (dp - 1):
            return lax.psum_scatter(
                values, "dp", scatter_dimension=values.ndim - 1, tiled=True
            )
        me = lax.axis_index("dp")
        bit = dp // 2
        while bit:
            halves = values.reshape(values.shape[:-1] + (2, values.shape[-1] // 2))
            high = (me & bit) != 0
            keep = jnp.where(high, halves[..., 1, :], halves[..., 0, :])
            give = jnp.where(high, halves[..., 0, :], halves[..., 1, :])
            values = keep + lax.ppermute(give, "dp", self.route(bit))
            bit //= 2
        return values


def grad_kernel(left, right, out):
    out[0, 0, 0] = lax.dot_general(
        left[0], right[0, 0], (((0,), (0,)), ((), ())), preferred_element_type=F32
    ).astype(BF16)


def weight_grad(left, right, outer):
    groups, rows, depth = left.shape
    parts, width = right.shape[1], right.shape[3]
    block = depth // outer
    if block % 128:
        full = jnp.einsum("mrd,mcrn->mcdn", left, right, preferred_element_type=F32).astype(BF16)
        return full.reshape(groups, parts, outer, block, width).transpose(2, 0, 1, 3, 4)
    return pl.pallas_call(
        grad_kernel,
        grid=(groups, parts, outer),
        in_specs=[
            pl.BlockSpec((1, rows, block), lambda m, c, o: (m, 0, o)),
            pl.BlockSpec((1, 1, rows, width), lambda m, c, o: (m, c, 0, 0)),
        ],
        out_specs=pl.BlockSpec((1, 1, 1, block, width), lambda m, c, o: (o, m, c, 0, 0)),
        out_shape=jax.ShapeDtypeStruct((outer, groups, parts, block, width), BF16),
        compiler_params=pltpu.CompilerParams(vmem_limit_bytes=48 * 1024 * 1024),
        cost_estimate=pl.CostEstimate(
            flops=2 * groups * parts * rows * depth * width,
            bytes_accessed=2 * groups * (rows * depth + parts * width * (rows + depth)),
            transcendentals=0,
        ),
        name="weight_grad",
    )(left, right)


def normalize(values, gain):
    scale = lax.rsqrt(jnp.mean(values * values, axis=-1, keepdims=True) + EPSILON)
    return values * scale * gain[:, None, :], scale


def norm_back(values, scale, gain, upstream):
    gained = gain[:, None, :] * upstream
    gain_grad = jnp.sum(upstream * values * scale, axis=1)
    value_grad = scale * gained - values * (scale * scale * scale) * jnp.mean(
        gained * values, axis=-1, keepdims=True
    )
    return value_grad, gain_grad


def local(
    frames_in, delays, item_bounds, attn_gain, ffn_gain, w_qkv, w_out, w_gate_up, w_down, cotangent
):
    local_pos, frames, width = frames_in.shape
    positions, head_width = w_qkv.shape[0], w_qkv.shape[3]
    heads = head_width // HD
    group = Group(positions, local_pos)
    mp, size, outer = group.mp, group.size, group.outer
    if size == local_pos:
        mine = lambda w: at(w.reshape((mp, size) + w.shape[1:]), group.member, 1)
    rest = local_pos // size

    frame_ids = lax.axis_index("dp") * frames + jnp.arange(frames, dtype=jnp.int32)
    earlier = shift_frames(frames_in[:, frames - 2 :, :], 1)
    padded = jnp.concatenate([earlier, frames_in], axis=1)
    one = (delays == 1)[:, None, None]
    shifted = jnp.where(one, padded[:, 1 : frames + 1], padded[:, :frames])
    item_start = jnp.where(
        frame_ids >= item_bounds[1],
        item_bounds[1],
        jnp.where(frame_ids >= item_bounds[0], item_bounds[0], 0),
    )
    usable = frame_ids[None, :] - delays[:, None] >= item_start[None, :]
    resid = jnp.where(usable[:, :, None], shifted.astype(F32), 0.0)

    normed_a, scale_a = normalize(resid, attn_gain)
    normed_all = group.gather(normed_a.astype(BF16)).reshape(positions, frames, width)
    qkv = jnp.einsum("pfd,pcde->pcfe", normed_all, w_qkv, preferred_element_type=F32).astype(BF16)
    split = qkv.reshape(positions, 3, frames, heads, HD)
    queries, key_rows, values = (split[:, 0], split[:, 1], split[:, 2])
    scores = jnp.einsum("ifhe,jfhe->fhij", queries, key_rows, preferred_element_type=F32) * 0.125
    causal = jnp.tril(jnp.ones((positions, positions), dtype=bool))
    scores = jnp.where(causal, scores, -1e30)
    probs = jax.nn.softmax(scores, axis=-1)
    probs_low = probs.astype(BF16)
    context = jnp.einsum("fhij,jfhe->ifhe", probs_low, values, preferred_element_type=F32)
    context = context.astype(BF16).reshape(positions, frames, head_width)
    attn_part = jnp.einsum("pfe,pde->pfd", context, w_out, preferred_element_type=F32)
    middle = resid + group.scatter(attn_part.reshape(mp, local_pos, frames, width))

    normed_f, scale_f = normalize(middle, ffn_gain)
    rows = size * frames
    cot_rows = group.gather(group.spread(cotangent).reshape(rows, width))
    ffn_rows = group.gather(group.spread(normed_f.astype(BF16)).reshape(rows, width))
    up_weights, down_weights = mine(w_gate_up), mine(w_down)
    gate_up = jnp.einsum("mrd,mcdn->mcrn", ffn_rows, up_weights, preferred_element_type=F32)
    gate, up = gate_up[:, 0], gate_up[:, 1]
    sigma = jax.nn.sigmoid(gate)
    hidden = (gate * sigma * up).astype(BF16)
    down_part = weight_grad(cot_rows, hidden[:, None], outer)
    d_hidden = jnp.einsum("mrd,mdn->mrn", cot_rows, down_weights, preferred_element_type=F32)
    d_gate = d_hidden * up * sigma * (1.0 + gate * (1.0 - sigma))
    d_up = d_hidden * gate * sigma
    d_gate_up = jnp.stack([d_gate, d_up], axis=1).astype(BF16)
    gate_up_part = weight_grad(ffn_rows, d_gate_up, outer)
    d_rows = group.scatter(
        jnp.einsum("mcrn,mcdn->mrd", d_gate_up, up_weights, preferred_element_type=F32)
    ).astype(BF16)
    d_normed_f = group.unspread(d_rows.reshape(size, frames, width)).astype(F32)
    out_rows = group.scatter(
        jnp.einsum("mrn,mdn->mrd", hidden, down_weights, preferred_element_type=F32)
    ).astype(BF16)
    mixed = (
        middle + group.unspread(out_rows.reshape(size, frames, width)).astype(F32)
    ).astype(BF16)

    middle_grad, ffn_gain_part = norm_back(middle, scale_f, ffn_gain, d_normed_f)
    d_middle = cotangent.astype(F32) + middle_grad
    d_middle_all = group.gather(d_middle.astype(BF16)).reshape(positions, frames, width)
    d_context = jnp.einsum("pfd,pde->pfe", d_middle_all, w_out, preferred_element_type=F32)
    d_context = d_context.astype(BF16).reshape(positions, frames, heads, HD)
    d_probs = jnp.einsum("ifhe,jfhe->fhij", d_context, values, preferred_element_type=F32)
    d_values = jnp.einsum("fhij,ifhe->jfhe", probs_low, d_context, preferred_element_type=F32)
    d_scores = (probs * (d_probs - jnp.sum(probs * d_probs, axis=-1, keepdims=True))).astype(BF16)
    d_queries = jnp.einsum("fhij,jfhe->ifhe", d_scores, key_rows, preferred_element_type=F32)
    d_keys = jnp.einsum("fhij,ifhe->jfhe", d_scores, queries, preferred_element_type=F32)
    d_qkv = jnp.stack([d_queries * 0.125, d_keys * 0.125, d_values], axis=1)
    d_qkv = d_qkv.reshape(positions, 3, frames, head_width).astype(BF16)
    d_normed_a = group.scatter(
        jnp.einsum("pcfe,pcde->pfd", d_qkv, w_qkv, preferred_element_type=F32).reshape(
            mp, local_pos, frames, width
        )
    )
    by_pos = lambda v: group.by_position(v.reshape((mp, size, frames, v.shape[-1])))
    context_rows, d_middle_rows, normed_rows = by_pos(context), by_pos(d_middle_all), by_pos(normed_all)
    d_qkv_rows = jnp.stack([by_pos(d_qkv[:, c]) for c in range(3)], axis=1)
    out_part = weight_grad(d_middle_rows, context_rows[:, None], outer)
    qkv_part = weight_grad(normed_rows, d_qkv_rows, outer)

    resid_grad, attn_gain_part = norm_back(resid, scale_a, attn_gain, d_normed_a)
    d_resid = d_middle + resid_grad
    spread = jnp.where(usable[:, :, None], d_resid, 0.0)
    blank = jnp.zeros((local_pos, 1, width), F32)
    placed = jnp.where(
        one,
        jnp.concatenate([blank, spread, blank], axis=1),
        jnp.concatenate([spread, blank, blank], axis=1),
    )
    returned = shift_frames(placed[:, :2, :], -1)
    input_grad = placed[:, 2:, :] + jnp.pad(returned, ((0, 0), (frames - 2, 0), (0, 0)))

    lines = [[o * size + k for o in range(outer)] for k in range(size)]

    def finish(part):
        whole = lax.psum_scatter(
            part, "dp", scatter_dimension=0, axis_index_groups=lines, tiled=True
        )[0]
        groups, parts, depth, n = whole.shape
        whole = whole.reshape(groups, parts, size, depth // size, n).transpose(2, 0, 1, 3, 4)
        got = group.in_order(group.spread(whole))
        return got.transpose(1, 0, 2, 3, 4).reshape(positions, parts, depth // size, n).astype(F32)

    down_grad = finish(down_part)[:, 0]
    gate_up_grad = finish(gate_up_part)
    out_grad = finish(out_part)[:, 0]
    qkv_grad = finish(qkv_part)
    attn_gain_grad, ffn_gain_grad = group.sum_scatter(jnp.stack([attn_gain_part, ffn_gain_part]))
    return (
        mixed,
        input_grad,
        attn_gain_grad,
        ffn_gain_grad,
        qkv_grad,
        out_grad,
        gate_up_grad,
        down_grad,
    )


def solution(mesh):
    placed = (
        P("mp", "dp", None),
        P("mp"),
        P(),
        P("mp", None),
        P("mp", None),
        P(None, None, None, "mp"),
        P(None, None, "mp"),
        P(None, None, None, "mp"),
        P(None, None, "mp"),
        P("mp", "dp", None),
    )
    return jax.shard_map(
        local,
        mesh=mesh,
        in_specs=placed,
        out_specs=(
            P("mp", "dp", None),
            P("mp", "dp", None),
            P("mp", "dp"),
            P("mp", "dp"),
            P(None, None, "dp", "mp"),
            P(None, "dp", "mp"),
            P(None, None, "dp", "mp"),
            P(None, "dp", "mp"),
        ),
        check_vma=False,
    )
```

time: 2990 us -> 1230 us (0.41)
  waiting for transfers between devices: 2250 us -> 559 us
  local copies, waits for them, and re-layouts: 348 us -> 208 us
  matrix products: 287 us -> 174 us
  Pallas kernels: 0 us -> 63.1 us
  other arithmetic: 81.7 us -> 143 us
  starting transfers between devices: 5 us -> 52 us
    reduce_scatter x8 -> x4, waiting for transfers between devices: 2040 us -> 97.8 us  [finish(): lax.psum_scatter(part, 'dp', scatter_dimension=0, axis_index_groups=lines...]
    ppermute x2 -> x56, waiting for transfers between devices: 0.01 us -> 461 us  [the longest x8 266 us: swap(): return lax.ppermute(block, 'mp', [(0, 1), (1, 0)])]
    all_gather x4 -> x0, waiting for transfers between devices: 203 us -> none  [the longest x1 58.9 us: local(): lax.all_gather(normed_a.astype(jnp.bfloat16), 'mp', axis=0, tiled=True)]
    transpose x2 -> x4, local copies, waits for them, and re-layouts: 152 us -> 0.88 us  [by_position(): return jnp.swapaxes(got, 0, 1).reshape(self.mp, -1, blocks.shape[-1])]
    dot_general x16 -> x12, matrix products: 274 us -> 161 us  [the longest x1 25.6 us: local(): jnp.einsum('pcfe,pcde->pfd', d_qkv, w_qkv, preferred_element_type=F32)]
    pallas_call x0 -> x4, Pallas kernels: none -> 63.1 us  [weight_grad(): pl.pallas_call(grad_kernel, grid=(groups, parts, outer), in_specs=[pl.Blo...]
    dot_general x1 -> x0, local copies, waits for them, and re-layouts: 49.3 us -> none  [local(): jnp.einsum('pfd,pfh->pdh', cotangent_all, hidden, preferred_element_type=...]
    ppermute x2 -> x56, starting transfers between devices: 3.65 us -> 51.8 us  [the longest x36 24.7 us: spread(): lax.ppermute(at(blocks, self.member ^ step), 'dp', self.route(step))]
  transfers between devices with their start and end apart: 16 -> 60, of which waited for: 11 -> 27; matrix products, arithmetic and copies ran while one was open for 15% -> 27% of each run, Pallas kernels for 0% -> 5%
where the time goes in v1:
time: 1230 us; the launch traced here: 1210 us
  waiting for transfers between devices  559 us (45%)
  local copies, waits for them, and re-layouts  208 us (17%)
  matrix products  174 us (14%)
  other arithmetic  143 us (12%)
  Pallas kernels  63.1 us (5%)
  starting transfers between devices  52 us (4%)
  between operations  15.2 us (1%)
    ppermute x8, waiting for transfers between devices, swap(): return lax.ppermute(block, 'mp', [(0, 1), (1, 0)])  266 us
    ppermute x36, waiting for transfers between devices, spread(): lax.ppermute(at(blocks, self.member ^ step), 'dp', self.route(step))  176 us
    reduce_scatter x4, waiting for transfers between devices, finish(): lax.psum_scatter(part, 'dp', scatter_dimension=0, axis_index_groups=lines...  97.8 us
    pallas_call x4, Pallas kernels, weight_grad(): pl.pallas_call(grad_kernel, grid=(groups, parts, outer), in_specs=[pl.Blo...  63.1 us
    unnamed x136, local copies, waits for them, and re-layouts  41.1 us
    another operation x20, local copies, waits for them, and re-layouts  34.7 us
    dot_general x1, matrix products, local(): jnp.einsum('pcfe,pcde->pfd', d_qkv, w_qkv, preferred_element_type=F32)  25.6 us
    squeeze x2, local copies, waits for them, and re-layouts, at(): return lax.dynamic_index_in_dim(array, index, axis, keepdims=False)  25.1 us
  transfers between devices with their start and end apart: 60, of which 27 were waited for; matrix products, arithmetic and copies ran while one was open for 27% of the time, Pallas kernels for 5%

profile of v1, /device:TPU:0, one launch (start us, length us, event | category | flops | bytes accessed | tf_op | source)
XLA Modules:
  0.0 1214.8 jit_solution(8579399765438583384)
XLA Ops:
  14.5 4.5 multiply_reduce_fusion.4
  23.7 45.6 %collective-permute-done.1 = bf16[4,256,1024]{2,1,0:T(8,128)(2,1)} collective-permute-done((bf16[4,256,1024]{2,1,0:T(8,128)(2,1)}, bf16[4,256,1024]{2,1,0:T(8,128)(2,1)}, u32[]{:S(2)}, u32[]{:S(2)}) %collective-permute-start.1) | collective-permute-done | bytes 2097184 | tf_op jit(solution)/shard_map/ppermute | solution.py:36
  73.8 16.8 %convert_bitcast_fusion = bf16[8,3,256,512]{3,2,1,0:T(8,128)(2,1)} fusion(bf16[8,256,1024,1]{2,1,3,0:T(8,128)(2,1)S(1)} %bitcast.496, bf16[8,3,1024,512]{3,2,1,0:T(8,128)(2,1)} %param.15), kind=kOutput, calls=%fused_computation.54 | convolution fusion | flops 6445596672 | bytes 35651584 | tf_op jit(solution)/shard_map/pfd,pcde->pcfe/dot_general | solution.py:170
  90.6 8.6 copy.83
  99.2 5.8 fusion.103
  105.0 7.5 copy.154
  112.5 7.4 copy.153
  119.9 7.6 copy.155
  127.5 5.8 fusion.43
  133.3 6.6 fusion.107
  140.9 8.7 convert_bitcast_fusion.2
  149.6 5.9 copy.88
  155.5 6.5 fusion.110
  174.3 41.9 %collective-permute-done.2 = bf16[4,256,1024]{2,1,0:T(8,128)(2,1)} collective-permute-done((bf16[4,256,1024]{2,1,0:T(8,128)(2,1)}, bf16[4,256,1024]{2,1,0:T(8,128)(2,1)}, u32[]{:S(2)}, u32[]{:S(2)}) %collective-permute-start.2) | collective-permute-done | bytes 2097184 | tf_op jit(solution)/shard_map/ppermute | solution.py:36
  227.2 8.7 collective-permute-done.5
  235.9 11.6 collective-permute-done.4
  250.9 10.0 dynamic-slice_bitcast_fusion
  260.8 15.2 %copy.146 = bf16[2,2,1024,1408]{2,3,0,1:T(8,128)(2,1)} copy(bf16[2,2,1024,1408]{3,2,1,0:T(8,128)(2,1)} %dynamic-slice_bitcast_fusion) | data formatting | bytes 23068672 | tf_op jit(solution)/shard_map/jit(dynamic_index_in_dim)/squeeze | solution.py:23
  279.8 38.8 %collective-permute-done.6 = bf16[1024,1024]{1,0:T(8,128)(2,1)} collective-permute-done((bf16[1024,1024]{1,0:T(8,128)(2,1)}, bf16[1024,1024]{1,0:T(8,128)(2,1)}, u32[]{:S(2)}, u32[]{:S(2)}) %collective-permute-start.6) | collective-permute-done | bytes 2097184 | tf_op jit(solution)/shard_map/ppermute | solution.py:36
  322.5 21.6 %convolution_bitcast_fusion = f32[2,2,1024,1408]{3,2,0,1:T(8,128)} fusion(bf16[2,2,1024,1408]{2,3,0,1:T(8,128)(2,1)} %copy.146, bf16[1,1024,1024]{2,1,0:T(8,128)(2,1)} %get-tuple-element.37, bf16[1,1024,1024]{2,1,0:T(8,128)(2,1)S(1)} %get-tuple-element.36), kind=kOutput, calls=%fused_computation.1 | convolution fusion | flops 11813257216 | bytes 38797312 | tf_op jit(solution)/shard_map/mrd,mcdn->mcrn/dot_general | solution.py:188
  344.1 14.9 %fusion.21 = f32[2,1024,1024]{2,1,0:T(8,128)} fusion(f32[2,2,1024,1408]{3,2,0,1:T(8,128)} %convolution_bitcast_fusion, bf16[2,4,1024,1408]{3,2,1,0:T(8,128)(2,1)} %bitcast.559, s32[]{:T(128)S(6)} %select_n.424), kind=kOutput, calls=%fused_computation.57 | convolution fusion | flops 5922881536 | bytes 37224452 | tf_op jit(solution)/shard_map/mrn,mdn->mrd/dot_general | solution.py:203
  364.5 18.4 %fusion.25 = (bf16[2,1,1024,1408]{3,2,0,1:T(8,128)(2,1)}, bf16[2,1,1024,1408]{3,2,0,1:T(8,128)(2,1)}) fusion(f32[2,2,1024,1408]{3,2,0,1:T(8,128)} %convolution_bitcast_fusion, bf16[2,4,1024,1408]{3,2,1,0:T(8,128)(2,1)} %bitcast.560, s32[]{:T(128)S(6)} %select_n.424, bf16[1,1024,1024]{2,1,0:T(8,128)(2,1)} %get-tuple-element.35, ...), kind=kOutput, calls=%fused_computation.60 | convolution fusion | flops 5945163776 | bytes 44564484 | tf_op jit(solution)/shard_map/mrd,mdn->mrn/dot_general | solution.py:193
  382.8 17.0 %convolution_bitcast_fusion.1 = f32[2,1024,1024]{2,1,0:T(8,128)S(1)} fusion(bf16[2,2,1024,1408]{2,3,0,1:T(8,128)(2,1)} %copy.146, bf16[2,1,1024,1408]{3,2,0,1:T(8,128)(2,1)} %get-tuple-element.18, bf16[2,1,1024,1408]{3,2,0,1:T(8,128)(2,1)} %get-tuple-element.17), kind=kOutput, calls=%fused_computation.118 | convolution fusion | flops 11816927232 | bytes 31457280 | tf_op jit(solution)/shard_map/mcrn,mcdn->mrd/dot_general | solution.py:199
  400.7 11.1 collective-permute-done.7
  417.1 38.3 %collective-permute-done.15 = bf16[1024,1024]{1,0:T(8,128)(2,1)S(1)} collective-permute-done((bf16[1024,1024]{1,0:T(8,128)(2,1)S(1)}, bf16[1024,1024]{1,0:T(8,128)(2,1)S(1)}, u32[]{:S(2)}, u32[]{:S(2)}) %collective-permute-start.15) | collective-permute-done | bytes 2097184 | tf_op jit(solution)/shard_map/ppermute | solution.py:36
  472.0 10.4 collective-permute-done.17
  491.1 4.9 fusion.34
  507.0 43.1 %collective-permute-done.19 = bf16[4,256,1024]{2,1,0:T(8,128)(2,1)} collective-permute-done((bf16[4,256,1024]{2,1,0:T(8,128)(2,1)S(1)}, bf16[4,256,1024]{2,1,0:T(8,128)(2,1)}, u32[]{:S(2)}, u32[]{:S(2)}) %collective-permute-start.19) | collective-permute-done | bytes 2097184 | tf_op jit(solution)/shard_map/ppermute | solution.py:36
  559.9 54.9 %collective-permute-done.45 = bf16[2,256,512]{2,1,0:T(8,128)(2,1)S(1)} collective-permute-done((bf16[2,256,512]{2,1,0:T(8,128)(2,1)}, bf16[2,256,512]{2,1,0:T(8,128)(2,1)S(1)}, u32[]{:S(2)}, u32[]{:S(2)}) %collective-permute-start.45) | collective-permute-done | bytes 524320 | tf_op jit(solution)/shard_map/ppermute | solution.py:57
  614.8 10.6 collective-permute-done.46
  630.7 7.9 weight_grad.5
  640.7 11.7 fusion.5.right
  652.4 12.3 %weight_grad.7 = bf16[4,2,1,256,1408]{4,3,2,1,0:T(8,128)(2,1)} custom-call(bf16[2,1024,1024]{2,1,0:T(8,128)(2,1)S(1)} %pad_maximum_fusion.5.left, bf16[2,1,1024,1408]{3,2,1,0:T(8,128)(2,1)} %fusion.5.right), custom_call_target="tpu_custom_call" | custom-call | flops 5905580032 | bytes 15728640 | tf_op jit(solution)/shard_map/weight_grad/pallas_call | solution.py:110
  672.1 7.1 convolution_convert_fusion
  682.0 6.7 copy.96
  688.7 10.8 multiply_reduce_fusion
  699.6 5.1 multiply_convert_fusion.2
  706.8 4.2 fusion.35
  711.0 5.0 copy.98
  716.0 7.9 fusion.36
  723.9 6.1 copy.99
  745.1 9.2 convert_bitcast_fusion.1
  754.3 5.9 copy.101
  788.5 9.8 collective-permute-done.34
  800.2 10.8 collective-permute-done.36
  811.0 9.3 collective-permute-done.37
  826.5 19.5 %weight_grad.4 = bf16[4,2,3,256,512]{4,3,2,1,0:T(8,128)(2,1)} custom-call(bf16[2,1024,1024]{2,1,0:T(8,128)(2,1)S(1)} %bitcast.449, bf16[2,3,1024,512]{3,2,1,0:T(8,128)(2,1)} %pad_maximum_fusion.3.right), custom_call_target="tpu_custom_call" | custom-call | flops 6442450944 | bytes 16777216 | tf_op jit(solution)/shard_map/weight_grad/pallas_call | solution.py:110
  846.1 6.2 pad_maximum_fusion
  852.3 5.5 copy.141.right
  858.2 23.3 %weight_grad.6 = bf16[4,2,2,256,1408]{4,3,2,1,0:T(8,128)(2,1)} custom-call(bf16[2,1024,1024]{2,1,0:T(8,128)(2,1)S(1)} %pad_maximum_fusion.4.left, bf16[2,2,1024,1408]{3,2,1,0:T(8,128)(2,1)} %copy.141.right), custom_call_target="tpu_custom_call" | custom-call | flops 11811160064 | bytes 27262976 | tf_op jit(solution)/shard_map/weight_grad/pallas_call | solution.py:110
  883.9 4.1 copy.103
  890.4 25.6 %fusion.13 = f32[8,256,1024,1]{2,1,3,0:T(8,128)} fusion(bf16[8,3,1024,512]{3,2,1,0:T(8,128)(2,1)} %param.15, bf16[8,1,256,512]{3,2,1,0:T(8,128)(2,1)} %copy.104, bf16[8,1,256,512]{3,2,1,0:T(8,128)(2,1)} %copy.103, bf16[8,1,256,512]{3,2,1,0:T(8,128)(2,1)} %copy.102), kind=kOutput, calls=%fused_computation.47 | convolution fusion | flops 6448742400 | bytes 39845888 | tf_op jit(solution)/shard_map/pcfe,pcde->pfd/dot_general | solution.py:222
  921.4 47.2 %collective-permute-done.20 = bf16[4,256,1024]{2,1,0:T(8,128)(2,1)} collective-permute-done((bf16[4,256,1024]{2,1,0:T(8,128)(2,1)}, bf16[4,256,1024]{2,1,0:T(8,128)(2,1)}, u32[]{:S(2)}, u32[]{:S(2)}) %collective-permute-start.20) | collective-permute-done | bytes 2097184 | tf_op jit(solution)/shard_map/ppermute | solution.py:36
  984.1 8.0 add_select_fusion
  992.4 4.7 maximum_select_fusion
  1005.3 5.3 slice_add_fusion
  1017.1 7.7 collective-permute-done.55
  1024.8 7.6 collective-permute-done.54
  1042.1 5.9 collective-permute-done.40
  1048.0 8.8 collective-permute-done.39
  1058.3 97.8 %reduce-scatter.9.cloned.1.call-done = bf16[1,2,2,256,1408]{4,3,2,1,0:T(8,128)(2,1)} async-done(((bf16[4,2,2,256,1408]{4,3,2,1,0:T(8,128)(2,1)}), bf16[1,2,2,256,1408]{4,3,2,1,0:T(8,128)(2,1)}) %reduce-scatter.9.cloned.1.call-update) | async-done | bytes 2883600 | tf_op jit(solution)/shard_map/reduce_scatter | solution.py:247
  1165.5 12.8 %collective-permute-done.52 = bf16[2,2,64,1408]{3,2,1,0:T(8,128)(2,1)} collective-permute-done((bf16[2,2,64,1408]{3,2,1,0:T(8,128)(2,1)}, bf16[2,2,64,1408]{3,2,1,0:T(8,128)(2,1)}, u32[]{:S(2)}, u32[]{:S(2)}) %collective-permute-start.52) | collective-permute-done | bytes 720928 | tf_op jit(solution)/shard_map/ppermute | solution.py:57
  1178.3 15.5 %collective-permute-done.51 = bf16[2,2,64,1408]{3,2,1,0:T(8,128)(2,1)} collective-permute-done((bf16[2,2,64,1408]{3,2,1,0:T(8,128)(2,1)}, bf16[2,2,64,1408]{3,2,1,0:T(8,128)(2,1)}, u32[]{:S(2)}, u32[]{:S(2)}) %collective-permute-start.51) | collective-permute-done | bytes 720928 | tf_op jit(solution)/shard_map/ppermute | solution.py:57
  1203.7 4.2 select_convert_fusion
  (350 shorter events, 251.6 us)
Async XLA Ops:
  7.2 994.2 %reduce-scatter.7.cloned.1.call-start = ((), (), s32[]{:S(2)}) async-start(), calls=%async_computation.5 | async-start | bytes 2621440 | tf_op jit(solution)/shard_map/reduce_scatter | solution.py:247
  8.1 6.4 collective-permute-start
  13.8 202.4 %copy-start.57 = (pred[4,256]{1,0:T(4,128)(4,1)}, pred[4,256]{1,0:T(4,128)(4,1)S(1)}, u32[]{:S(2)}) copy-start(pred[4,256]{1,0:T(4,128)(4,1)S(1)} %subtract_compare_fusion) | copy-start | bytes 3076
  18.9 197.2 %copy-start.3 = (bf16[4,256,1024]{2,1,0:T(8,128)(2,1)}, bf16[4,256,1024]{2,1,0:T(8,128)(2,1)S(1)}, u32[]{:S(2)}) copy-start(bf16[4,256,1024]{2,1,0:T(8,128)(2,1)S(1)} %get-tuple-element.16) | copy-start | bytes 6291460
  21.4 47.9 %collective-permute-start.1 = (bf16[4,256,1024]{2,1,0:T(8,128)(2,1)}, bf16[4,256,1024]{2,1,0:T(8,128)(2,1)}, u32[]{:S(2)}, u32[]{:S(2)}) collective-permute-start(bf16[4,256,1024]{2,1,0:T(8,128)(2,1)} %multiply_convert_fusion.4), channel_id=1, source_target_pairs={{0,1},{1,0},{2,3},{3,2},{4,5},{5,4},{6,7},{7,6},{8,9},{9,8},{10,11... | collective-permute-start | bytes 6291464 | tf_op jit(solution)/shard_map/ppermute | solution.py:36
  167.0 49.2 %collective-permute-start.2 = (bf16[4,256,1024]{2,1,0:T(8,128)(2,1)}, bf16[4,256,1024]{2,1,0:T(8,128)(2,1)}, u32[]{:S(2)}, u32[]{:S(2)}) collective-permute-start(bf16[4,256,1024]{2,1,0:T(8,128)(2,1)} %fusion.63), channel_id=1, source_target_pairs={{0,1},{1,0},{2,3},{3,2},{4,5},{5,4},{6,7},{7,6},{8,9},{9,8},{10,11... | collective-permute-start | bytes 6291464 | tf_op jit(solution)/shard_map/ppermute | solution.py:36
  172.2 51.9 %collective-permute-start.11 = (bf16[256,1024]{1,0:T(8,128)(2,1)}, bf16[256,1024]{1,0:T(8,128)(2,1)S(1)}, u32[]{:S(2)}, u32[]{:S(2)}) collective-permute-start(bf16[256,1024]{1,0:T(8,128)(2,1)} %get-tuple-element.65), channel_id=1, source_target_pairs={{0,2},{2,0},{4,6},{6,4},{8,10},{10,8},{12,14},{14,12},{16,18},{18,... | collective-permute-start | bytes 1572872 | tf_op jit(solution)/shard_map/ppermute | solution.py:57
  172.5 51.6 %collective-permute-start.13 = (bf16[256,1024]{1,0:T(8,128)(2,1)}, bf16[256,1024]{1,0:T(8,128)(2,1)}, u32[]{:S(2)}, u32[]{:S(2)}) collective-permute-start(bf16[256,1024]{1,0:T(8,128)(2,1)} %get-tuple-element.66), channel_id=1, source_target_pairs={{0,6},{2,4},{4,2},{6,0},{8,14},{10,12},{12,10},{14,8},{16,22},{18,... | collective-permute-start | bytes 1572872 | tf_op jit(solution)/shard_map/ppermute | solution.py:57
  174.1 50.0 %collective-permute-start.12 = (bf16[256,1024]{1,0:T(8,128)(2,1)}, bf16[256,1024]{1,0:T(8,128)(2,1)}, u32[]{:S(2)}, u32[]{:S(2)}) collective-permute-start(bf16[256,1024]{1,0:T(8,128)(2,1)} %get-tuple-element.67), channel_id=1, source_target_pairs={{0,4},{2,6},{4,0},{6,2},{8,12},{10,14},{12,8},{14,10},{16,20},{18,... | collective-permute-start | bytes 1572872 | tf_op jit(solution)/shard_map/ppermute | solution.py:57
  220.2 275.8 %copy-start.55 = (f32[4,256]{1,0:T(4,128)}, f32[4,256]{1,0:T(4,128)S(1)}, u32[]{:S(2)}) copy-start(f32[4,256]{1,0:T(4,128)S(1)} %get-tuple-element.99) | copy-start | bytes 12292
  220.2 275.8 %copy-start.59 = (f32[4,256]{1,0:T(4,128)}, f32[4,256]{1,0:T(4,128)S(1)}, u32[]{:S(2)}) copy-start(f32[4,256]{1,0:T(4,128)S(1)} %get-tuple-element.98) | copy-start | bytes 12292
  222.1 13.9 %collective-permute-start.5 = (bf16[256,1024]{1,0:T(8,128)(2,1)S(1)}, bf16[256,1024]{1,0:T(8,128)(2,1)S(1)}, u32[]{:S(2)}, u32[]{:S(2)}) collective-permute-start(bf16[256,1024]{1,0:T(8,128)(2,1)S(1)} %get-tuple-element.73), channel_id=1, source_target_pairs={{0,6},{2,4},{4,2},{6,0},{8,14},{10,12},{12,10},{14,8},{16,22},{18,... | collective-permute-start | bytes 1572872 | tf_op jit(solution)/shard_map/ppermute | solution.py:57
  223.2 24.3 %collective-permute-start.4 = (bf16[256,1024]{1,0:T(8,128)(2,1)S(1)}, bf16[256,1024]{1,0:T(8,128)(2,1)S(1)}, u32[]{:S(2)}, u32[]{:S(2)}) collective-permute-start(bf16[256,1024]{1,0:T(8,128)(2,1)S(1)} %get-tuple-element.74), channel_id=1, source_target_pairs={{0,4},{2,6},{4,0},{6,2},{8,12},{10,14},{12,8},{14,10},{16,20},{18,... | collective-permute-start | bytes 1572872 | tf_op jit(solution)/shard_map/ppermute | solution.py:57
  224.0 23.5 %collective-permute-start.3 = (bf16[256,1024]{1,0:T(8,128)(2,1)S(1)}, bf16[256,1024]{1,0:T(8,128)(2,1)S(1)}, u32[]{:S(2)}, u32[]{:S(2)}) collective-permute-start(bf16[256,1024]{1,0:T(8,128)(2,1)S(1)} %get-tuple-element.75), channel_id=1, source_target_pairs={{0,2},{2,0},{4,6},{6,4},{8,10},{10,8},{12,14},{14,12},{16,18},{18,... | collective-permute-start | bytes 1572872 | tf_op jit(solution)/shard_map/ppermute | solution.py:57
  225.6 50.4 %collective-permute-start.14 = (bf16[1024,1024]{1,0:T(8,128)(2,1)S(1)}, bf16[1024,1024]{1,0:T(8,128)(2,1)}, u32[]{:S(2)}, u32[]{:S(2)}) collective-permute-start(bf16[1024,1024]{1,0:T(8,128)(2,1)S(1)} %bitcast.486), channel_id=1, source_target_pairs={{0,1},{1,0},{2,3},{3,2},{4,5},{5,4},{6,7},{7,6},{8,9},{9,8},{10,11... | collective-permute-start | bytes 6291464 | tf_op jit(solution)/shard_map/ppermute | solution.py:36
  249.1 69.5 %collective-permute-start.6 = (bf16[1024,1024]{1,0:T(8,128)(2,1)}, bf16[1024,1024]{1,0:T(8,128)(2,1)}, u32[]{:S(2)}, u32[]{:S(2)}) collective-permute-start(bf16[1024,1024]{1,0:T(8,128)(2,1)} %bitcast.25), channel_id=1, source_target_pairs={{0,1},{1,0},{2,3},{3,2},{4,5},{5,4},{6,7},{7,6},{8,9},{9,8},{10,11... | collective-permute-start | bytes 6291464 | tf_op jit(solution)/shard_map/ppermute | solution.py:36
  362.9 48.8 %collective-permute-start.7 = (bf16[1024,1024]{1,0:T(8,128)(2,1)}, bf16[1024,1024]{1,0:T(8,128)(2,1)}, u32[]{:S(2)}, u32[]{:S(2)}) collective-permute-start(bf16[1024,1024]{1,0:T(8,128)(2,1)} %fusion.64), channel_id=1, source_target_pairs={{0,1},{1,0},{2,3},{3,2},{4,5},{5,4},{6,7},{7,6},{8,9},{9,8},{10,11... | collective-permute-start | bytes 6291464 | tf_op jit(solution)/shard_map/ppermute | solution.py:36
  400.2 55.2 %collective-permute-start.15 = (bf16[1024,1024]{1,0:T(8,128)(2,1)S(1)}, bf16[1024,1024]{1,0:T(8,128)(2,1)S(1)}, u32[]{:S(2)}, u32[]{:S(2)}) collective-permute-start(bf16[1024,1024]{1,0:T(8,128)(2,1)S(1)} %fusion.65), channel_id=1, source_target_pairs={{0,1},{1,0},{2,3},{3,2},{4,5},{5,4},{6,7},{7,6},{8,9},{9,8},{10,11... | collective-permute-start | bytes 6291464 | tf_op jit(solution)/shard_map/ppermute | solution.py:36
  415.3 43.2 %collective-permute-start.10 = (bf16[256,1024]{1,0:T(8,128)(2,1)S(1)}, bf16[256,1024]{1,0:T(8,128)(2,1)S(1)}, u32[]{:S(2)}, u32[]{:S(2)}) collective-permute-start(bf16[256,1024]{1,0:T(8,128)(2,1)S(1)} %get-tuple-element.69), channel_id=1, source_target_pairs={{0,6},{2,4},{4,2},{6,0},{8,14},{10,12},{12,10},{14,8},{16,22},{18,... | collective-permute-start | bytes 1572872 | tf_op jit(solution)/shard_map/ppermute | solution.py:63
  415.3 44.1 %collective-permute-start.9 = (bf16[256,1024]{1,0:T(8,128)(2,1)}, bf16[256,1024]{1,0:T(8,128)(2,1)S(1)}, u32[]{:S(2)}, u32[]{:S(2)}) collective-permute-start(bf16[256,1024]{1,0:T(8,128)(2,1)} %get-tuple-element.70), channel_id=1, source_target_pairs={{0,4},{2,6},{4,0},{6,2},{8,12},{10,14},{12,8},{14,10},{16,20},{18,... | collective-permute-start | bytes 1572872 | tf_op jit(solution)/shard_map/ppermute | solution.py:63
  416.7 42.7 %collective-permute-start.8 = (bf16[256,1024]{1,0:T(8,128)(2,1)S(1)}, bf16[256,1024]{1,0:T(8,128)(2,1)S(1)}, u32[]{:S(2)}, u32[]{:S(2)}) collective-permute-start(bf16[256,1024]{1,0:T(8,128)(2,1)S(1)} %get-tuple-element.71), channel_id=1, source_target_pairs={{0,2},{2,0},{4,6},{6,4},{8,10},{10,8},{12,14},{14,12},{16,18},{18,... | collective-permute-start | bytes 1572872 | tf_op jit(solution)/shard_map/ppermute | solution.py:63
  457.5 14.5 %collective-permute-start.18 = (bf16[256,1024]{1,0:T(8,128)(2,1)}, bf16[256,1024]{1,0:T(8,128)(2,1)}, u32[]{:S(2)}, u32[]{:S(2)}) collective-permute-start(bf16[256,1024]{1,0:T(8,128)(2,1)} %get-tuple-element.61), channel_id=1, source_target_pairs={{0,6},{2,4},{4,2},{6,0},{8,14},{10,12},{12,10},{14,8},{16,22},{18,... | collective-permute-start | bytes 1572872 | tf_op jit(solution)/shard_map/ppermute | solution.py:63
  457.5 24.8 %collective-permute-start.17 = (bf16[256,1024]{1,0:T(8,128)(2,1)}, bf16[256,1024]{1,0:T(8,128)(2,1)}, u32[]{:S(2)}, u32[]{:S(2)}) collective-permute-start(bf16[256,1024]{1,0:T(8,128)(2,1)} %get-tuple-element.62), channel_id=1, source_target_pairs={{0,4},{2,6},{4,0},{6,2},{8,12},{10,14},{12,8},{14,10},{16,20},{18,... | collective-permute-start | bytes 1572872 | tf_op jit(solution)/shard_map/ppermute | solution.py:63
  458.5 23.9 %collective-permute-start.16 = (bf16[256,1024]{1,0:T(8,128)(2,1)}, bf16[256,1024]{1,0:T(8,128)(2,1)}, u32[]{:S(2)}, u32[]{:S(2)}) collective-permute-start(bf16[256,1024]{1,0:T(8,128)(2,1)} %get-tuple-element.63), channel_id=1, source_target_pairs={{0,2},{2,0},{4,6},{6,4},{8,10},{10,8},{12,14},{14,12},{16,18},{18,... | collective-permute-start | bytes 1572872 | tf_op jit(solution)/shard_map/ppermute | solution.py:63
  502.2 47.9 %collective-permute-start.19 = (bf16[4,256,1024]{2,1,0:T(8,128)(2,1)S(1)}, bf16[4,256,1024]{2,1,0:T(8,128)(2,1)}, u32[]{:S(2)}, u32[]{:S(2)}) collective-permute-start(bf16[4,256,1024]{2,1,0:T(8,128)(2,1)S(1)} %get-tuple-element.32), channel_id=1, source_target_pairs={{0,1},{1,0},{2,3},{3,2},{4,5},{5,4},{6,7},{7,6},{8,9},{9,8},{10,11... | collective-permute-start | bytes 6291464 | tf_op jit(solution)/shard_map/ppermute | solution.py:36
  507.0 52.1 %collective-permute-start.44 = (bf16[2,256,512]{2,1,0:T(8,128)(2,1)}, bf16[2,256,512]{2,1,0:T(8,128)(2,1)}, u32[]{:S(2)}, u32[]{:S(2)}) collective-permute-start(bf16[2,256,512]{2,1,0:T(8,128)(2,1)} %bitcast.538), channel_id=1, source_target_pairs={{0,2},{2,0},{4,6},{6,4},{8,10},{10,8},{12,14},{14,12},{16,18},{18,... | collective-permute-start | bytes 1572872 | tf_op jit(solution)/shard_map/ppermute | solution.py:57
  554.9 72.1 %collective-permute-start.41 = (bf16[2,256,1024]{2,1,0:T(8,128)(2,1)}, bf16[2,256,1024]{2,1,0:T(8,128)(2,1)}, u32[]{:S(2)}, u32[]{:S(2)}) collective-permute-start(bf16[2,256,1024]{2,1,0:T(8,128)(2,1)} %get-tuple-element.23), channel_id=1, source_target_pairs={{0,2},{2,0},{4,6},{6,4},{8,10},{10,8},{12,14},{14,12},{16,18},{18,... | collective-permute-start | bytes 3145736 | tf_op jit(solution)/shard_map/ppermute | solution.py:57
  554.9 72.1 %collective-permute-start.42 = (bf16[2,256,1024]{2,1,0:T(8,128)(2,1)}, bf16[2,256,1024]{2,1,0:T(8,128)(2,1)}, u32[]{:S(2)}, u32[]{:S(2)}) collective-permute-start(bf16[2,256,1024]{2,1,0:T(8,128)(2,1)} %get-tuple-element.24), channel_id=1, source_target_pairs={{0,4},{2,6},{4,0},{6,2},{8,12},{10,14},{12,8},{14,10},{16,20},{18,... | collective-permute-start | bytes 3145736 | tf_op jit(solution)/shard_map/ppermute | solution.py:57
  556.0 71.0 %collective-permute-start.43 = (bf16[2,256,1024]{2,1,0:T(8,128)(2,1)}, bf16[2,256,1024]{2,1,0:T(8,128)(2,1)}, u32[]{:S(2)}, u32[]{:S(2)}) collective-permute-start(bf16[2,256,1024]{2,1,0:T(8,128)(2,1)} %get-tuple-element.25), channel_id=1, source_target_pairs={{0,6},{2,4},{4,2},{6,0},{8,14},{10,12},{12,10},{14,8},{16,22},{18,... | collective-permute-start | bytes 3145736 | tf_op jit(solution)/shard_map/ppermute | solution.py:57
  558.0 56.8 %collective-permute-start.45 = (bf16[2,256,512]{2,1,0:T(8,128)(2,1)}, bf16[2,256,512]{2,1,0:T(8,128)(2,1)S(1)}, u32[]{:S(2)}, u32[]{:S(2)}) collective-permute-start(bf16[2,256,512]{2,1,0:T(8,128)(2,1)} %bitcast.168), channel_id=1, source_target_pairs={{0,4},{2,6},{4,0},{6,2},{8,12},{10,14},{12,8},{14,10},{16,20},{18,... | collective-permute-start | bytes 1572872 | tf_op jit(solution)/shard_map/ppermute | solution.py:57
  559.1 66.2 %collective-permute-start.46 = (bf16[2,256,512]{2,1,0:T(8,128)(2,1)S(1)}, bf16[2,256,512]{2,1,0:T(8,128)(2,1)}, u32[]{:S(2)}, u32[]{:S(2)}) collective-permute-start(bf16[2,256,512]{2,1,0:T(8,128)(2,1)S(1)} %bitcast.539), channel_id=1, source_target_pairs={{0,6},{2,4},{4,2},{6,0},{8,14},{10,12},{12,10},{14,8},{16,22},{18,... | collective-permute-start | bytes 1572872 | tf_op jit(solution)/shard_map/ppermute | solution.py:57
  638.6 372.6 %reduce-scatter.11.cloned.1.call-start = ((), (), s32[]{:S(2)}) async-start(), calls=%async_computation.7 | async-start | bytes 7208960 | tf_op jit(solution)/shard_map/reduce_scatter | solution.py:247
  664.8 370.7 %reduce-scatter.5.cloned.1.call-start = ((), (), s32[]{:S(2)}) async-start(), calls=%async_computation.4 | async-start | bytes 7864320 | tf_op jit(solution)/shard_map/reduce_scatter | solution.py:247
  669.8 74.1 %collective-permute-start.26 = (bf16[2,256,1024]{2,1,0:T(8,128)(2,1)}, bf16[2,256,1024]{2,1,0:T(8,128)(2,1)}, u32[]{:S(2)}, u32[]{:S(2)}) collective-permute-start(bf16[2,256,1024]{2,1,0:T(8,128)(2,1)} %get-tuple-element.27), channel_id=1, source_target_pairs={{0,2},{2,0},{4,6},{6,4},{8,10},{10,8},{12,14},{14,12},{16,18},{18,... | collective-permute-start | bytes 3145736 | tf_op jit(solution)/shard_map/ppermute | solution.py:57
  670.0 74.3 %collective-permute-start.27 = (bf16[2,256,1024]{2,1,0:T(8,128)(2,1)}, bf16[2,256,1024]{2,1,0:T(8,128)(2,1)}, u32[]{:S(2)}, u32[]{:S(2)}) collective-permute-start(bf16[2,256,1024]{2,1,0:T(8,128)(2,1)} %get-tuple-element.28), channel_id=1, source_target_pairs={{0,4},{2,6},{4,0},{6,2},{8,12},{10,14},{12,8},{14,10},{16,20},{18,... | collective-permute-start | bytes 3145736 | tf_op jit(solution)/shard_map/ppermute | solution.py:57
  671.0 102.4 %collective-permute-start.28 = (bf16[2,256,1024]{2,1,0:T(8,128)(2,1)}, bf16[2,256,1024]{2,1,0:T(8,128)(2,1)}, u32[]{:S(2)}, u32[]{:S(2)}) collective-permute-start(bf16[2,256,1024]{2,1,0:T(8,128)(2,1)} %get-tuple-element.29), channel_id=1, source_target_pairs={{0,6},{2,4},{4,2},{6,0},{8,14},{10,12},{12,10},{14,8},{16,22},{18,... | collective-permute-start | bytes 3145736 | tf_op jit(solution)/shard_map/ppermute | solution.py:57
  737.5 36.9 %collective-permute-start.29 = (bf16[2,256,512]{2,1,0:T(8,128)(2,1)}, bf16[2,256,512]{2,1,0:T(8,128)(2,1)}, u32[]{:S(2)}, u32[]{:S(2)}) collective-permute-start(bf16[2,256,512]{2,1,0:T(8,128)(2,1)} %bitcast.537), channel_id=1, source_target_pairs={{0,2},{2,0},{4,6},{6,4},{8,10},{10,8},{12,14},{14,12},{16,18},{18,... | collective-permute-start | bytes 1572872 | tf_op jit(solution)/shard_map/ppermute | solution.py:57
  738.0 36.7 %collective-permute-start.30 = (bf16[2,256,512]{2,1,0:T(8,128)(2,1)}, bf16[2,256,512]{2,1,0:T(8,128)(2,1)}, u32[]{:S(2)}, u32[]{:S(2)}) collective-permute-start(bf16[2,256,512]{2,1,0:T(8,128)(2,1)} %bitcast.535), channel_id=1, source_target_pairs={{0,4},{2,6},{4,0},{6,2},{8,12},{10,14},{12,8},{14,10},{16,20},{18,... | collective-permute-start | bytes 1572872 | tf_op jit(solution)/shard_map/ppermute | solution.py:57
  743.9 31.6 %collective-permute-start.31 = (bf16[2,256,512]{2,1,0:T(8,128)(2,1)}, bf16[2,256,512]{2,1,0:T(8,128)(2,1)}, u32[]{:S(2)}, u32[]{:S(2)}) collective-permute-start(bf16[2,256,512]{2,1,0:T(8,128)(2,1)} %bitcast.531), channel_id=1, source_target_pairs={{0,6},{2,4},{4,2},{6,0},{8,14},{10,12},{12,10},{14,8},{16,22},{18,... | collective-permute-start | bytes 1572872 | tf_op jit(solution)/shard_map/ppermute | solution.py:57
  744.3 32.3 %collective-permute-start.32 = (bf16[2,256,512]{2,1,0:T(8,128)(2,1)}, bf16[2,256,512]{2,1,0:T(8,128)(2,1)}, u32[]{:S(2)}, u32[]{:S(2)}) collective-permute-start(bf16[2,256,512]{2,1,0:T(8,128)(2,1)} %bitcast.536), channel_id=1, source_target_pairs={{0,2},{2,0},{4,6},{6,4},{8,10},{10,8},{12,14},{14,12},{16,18},{18,... | collective-permute-start | bytes 1572872 | tf_op jit(solution)/shard_map/ppermute | solution.py:57
  773.4 15.1 %collective-permute-start.33 = (bf16[2,256,512]{2,1,0:T(8,128)(2,1)}, bf16[2,256,512]{2,1,0:T(8,128)(2,1)}, u32[]{:S(2)}, u32[]{:S(2)}) collective-permute-start(bf16[2,256,512]{2,1,0:T(8,128)(2,1)} %bitcast.534), channel_id=1, source_target_pairs={{0,4},{2,6},{4,0},{6,2},{8,12},{10,14},{12,8},{14,10},{16,20},{18,... | collective-permute-start | bytes 1572872 | tf_op jit(solution)/shard_map/ppermute | solution.py:57
  774.4 23.9 %collective-permute-start.34 = (bf16[2,256,512]{2,1,0:T(8,128)(2,1)}, bf16[2,256,512]{2,1,0:T(8,128)(2,1)}, u32[]{:S(2)}, u32[]{:S(2)}) collective-permute-start(bf16[2,256,512]{2,1,0:T(8,128)(2,1)} %bitcast.532), channel_id=1, source_target_pairs={{0,6},{2,4},{4,2},{6,0},{8,14},{10,12},{12,10},{14,8},{16,22},{18,... | collective-permute-start | bytes 1572872 | tf_op jit(solution)/shard_map/ppermute | solution.py:57
  774.7 25.4 %collective-permute-start.35 = (bf16[2,256,512]{2,1,0:T(8,128)(2,1)}, bf16[2,256,512]{2,1,0:T(8,128)(2,1)}, u32[]{:S(2)}, u32[]{:S(2)}) collective-permute-start(bf16[2,256,512]{2,1,0:T(8,128)(2,1)} %bitcast.533), channel_id=1, source_target_pairs={{0,2},{2,0},{4,6},{6,4},{8,10},{10,8},{12,14},{14,12},{16,18},{18,... | collective-permute-start | bytes 1572872 | tf_op jit(solution)/shard_map/ppermute | solution.py:57
  775.5 35.4 %collective-permute-start.36 = (bf16[2,256,512]{2,1,0:T(8,128)(2,1)}, bf16[2,256,512]{2,1,0:T(8,128)(2,1)}, u32[]{:S(2)}, u32[]{:S(2)}) collective-permute-start(bf16[2,256,512]{2,1,0:T(8,128)(2,1)} %bitcast.530), channel_id=1, source_target_pairs={{0,4},{2,6},{4,0},{6,2},{8,12},{10,14},{12,8},{14,10},{16,20},{18,... | collective-permute-start | bytes 1572872 | tf_op jit(solution)/shard_map/ppermute | solution.py:57
  776.6 43.7 %collective-permute-start.37 = (bf16[2,256,512]{2,1,0:T(8,128)(2,1)}, bf16[2,256,512]{2,1,0:T(8,128)(2,1)}, u32[]{:S(2)}, u32[]{:S(2)}) collective-permute-start(bf16[2,256,512]{2,1,0:T(8,128)(2,1)} %bitcast.529), channel_id=1, source_target_pairs={{0,6},{2,4},{4,2},{6,0},{8,14},{10,12},{12,10},{14,8},{16,22},{18,... | collective-permute-start | bytes 1572872 | tf_op jit(solution)/shard_map/ppermute | solution.py:57
  846.0 310.1 %reduce-scatter.9.cloned.1.call-start = ((), (), s32[]{:S(2)}) async-start(), calls=%async_computation.6 | async-start | bytes 14417920 | tf_op jit(solution)/shard_map/reduce_scatter | solution.py:247
  920.0 48.7 %collective-permute-start.20 = (bf16[4,256,1024]{2,1,0:T(8,128)(2,1)}, bf16[4,256,1024]{2,1,0:T(8,128)(2,1)}, u32[]{:S(2)}, u32[]{:S(2)}) collective-permute-start(bf16[4,256,1024]{2,1,0:T(8,128)(2,1)} %fusion.66), channel_id=1, source_target_pairs={{0,1},{1,0},{2,3},{3,2},{4,5},{5,4},{6,7},{7,6},{8,9},{9,8},{10,11... | collective-permute-start | bytes 6291464 | tf_op jit(solution)/shard_map/ppermute | solution.py:36
  972.4 5.2 collective-permute-start.22
  977.7 4.8 collective-permute-start.23
  982.6 9.6 collective-permute-start.24
  992.3 8.4 collective-permute-start.25
  999.2 6.2 collective-permute-start.21
  1002.5 8.2 collective-permute-start.49
  1003.8 7.3 collective-permute-start.48
  1005.3 5.9 collective-permute-start.47
  1013.6 11.2 collective-permute-start.55
  1015.6 16.8 %collective-permute-start.54 = (bf16[2,1,64,1408]{3,2,0,1:T(8,128)(2,1)}, bf16[2,1,64,1408]{3,2,0,1:T(8,128)(2,1)S(1)}, u32[]{:S(2)}, u32[]{:S(2)}) collective-permute-start(bf16[2,1,64,1408]{3,2,0,1:T(8,128)(2,1)} %get-tuple-element.82), channel_id=1, source_target_pairs={{0,4},{2,6},{4,0},{6,2},{8,12},{10,14},{12,8},{14,10},{16,20},{18,... | collective-permute-start | bytes 1081352 | tf_op jit(solution)/shard_map/ppermute | solution.py:57
  1015.6 16.8 %collective-permute-start.53 = (bf16[2,1,64,1408]{3,2,0,1:T(8,128)(2,1)}, bf16[2,1,64,1408]{3,2,0,1:T(8,128)(2,1)S(1)}, u32[]{:S(2)}, u32[]{:S(2)}) collective-permute-start(bf16[2,1,64,1408]{3,2,0,1:T(8,128)(2,1)} %get-tuple-element.83), channel_id=1, source_target_pairs={{0,2},{2,0},{4,6},{6,4},{8,10},{10,8},{12,14},{14,12},{16,18},{18,... | collective-permute-start | bytes 1081352 | tf_op jit(solution)/shard_map/ppermute | solution.py:57
  1036.9 11.1 collective-permute-start.40
  1037.4 19.4 %collective-permute-start.39 = (bf16[2,3,64,512]{3,2,1,0:T(8,128)(2,1)S(1)}, bf16[2,3,64,512]{3,2,1,0:T(8,128)(2,1)S(1)}, u32[]{:S(2)}, u32[]{:S(2)}) collective-permute-start(bf16[2,3,64,512]{3,2,1,0:T(8,128)(2,1)S(1)} %get-tuple-element.78), channel_id=1, source_target_pairs={{0,4},{2,6},{4,0},{6,2},{8,12},{10,14},{12,8},{14,10},{16,20},{18,... | collective-permute-start | bytes 1179656 | tf_op jit(solution)/shard_map/ppermute | solution.py:57
  1038.9 17.9 %collective-permute-start.38 = (bf16[2,3,64,512]{3,2,1,0:T(8,128)(2,1)S(1)}, bf16[2,3,64,512]{3,2,1,0:T(8,128)(2,1)S(1)}, u32[]{:S(2)}, u32[]{:S(2)}) collective-permute-start(bf16[2,3,64,512]{3,2,1,0:T(8,128)(2,1)S(1)} %get-tuple-element.79), channel_id=1, source_target_pairs={{0,2},{2,0},{4,6},{6,4},{8,10},{10,8},{12,14},{14,12},{16,18},{18,... | collective-permute-start | bytes 1179656 | tf_op jit(solution)/shard_map/ppermute | solution.py:57
  1159.5 18.8 %collective-permute-start.52 = (bf16[2,2,64,1408]{3,2,1,0:T(8,128)(2,1)}, bf16[2,2,64,1408]{3,2,1,0:T(8,128)(2,1)}, u32[]{:S(2)}, u32[]{:S(2)}) collective-permute-start(bf16[2,2,64,1408]{3,2,1,0:T(8,128)(2,1)} %get-tuple-element.41), channel_id=1, source_target_pairs={{0,6},{2,4},{4,2},{6,0},{8,14},{10,12},{12,10},{14,8},{16,22},{18,... | collective-permute-start | bytes 2162696 | tf_op jit(solution)/shard_map/ppermute | solution.py:57
  1160.2 33.6 %collective-permute-start.51 = (bf16[2,2,64,1408]{3,2,1,0:T(8,128)(2,1)}, bf16[2,2,64,1408]{3,2,1,0:T(8,128)(2,1)}, u32[]{:S(2)}, u32[]{:S(2)}) collective-permute-start(bf16[2,2,64,1408]{3,2,1,0:T(8,128)(2,1)} %get-tuple-element.42), channel_id=1, source_target_pairs={{0,4},{2,6},{4,0},{6,2},{8,12},{10,14},{12,8},{14,10},{16,20},{18,... | collective-permute-start | bytes 2162696 | tf_op jit(solution)/shard_map/ppermute | solution.py:57
  1161.1 32.7 %collective-permute-start.50 = (bf16[2,2,64,1408]{3,2,1,0:T(8,128)(2,1)}, bf16[2,2,64,1408]{3,2,1,0:T(8,128)(2,1)}, u32[]{:S(2)}, u32[]{:S(2)}) collective-permute-start(bf16[2,2,64,1408]{3,2,1,0:T(8,128)(2,1)} %get-tuple-element.43), channel_id=1, source_target_pairs={{0,2},{2,0},{4,6},{6,4},{8,10},{10,8},{12,14},{14,12},{16,18},{18,... | collective-permute-start | bytes 2162696 | tf_op jit(solution)/shard_map/ppermute | solution.py:57
  (62 other events, 1295.8 us)
Sparse Core Ops, SparseCore 0:
  638.8 44.0 reduce-scatter.6
  685.3 101.5 reduce-scatter.10
  846.1 111.2 reduce-scatter.4
  959.8 196.3 reduce-scatter.8

commit v2 on v1

v2 whole, which is shorter than its diff:
```python
import functools

import jax
import jax.numpy as jnp
from jax import lax
from jax.experimental import pallas as pl
from jax.experimental.pallas import tpu as pltpu
from jax.sharding import PartitionSpec as P

HD = 64
LANES = 128
EPSILON = 1e-05
BF16 = jnp.bfloat16
F32 = jnp.float32
MIB = 1024 * 1024
WEIGHT = 100


def dot(left, right, contract):
    return lax.dot_general(left, right, ((contract[:1], contract[1:]), ((), ())), preferred_element_type=F32)


def shift_frames(block, distance):
    devices = range(lax.axis_size("dp"))
    route = [(i - distance, i) for i in devices if i - distance in devices]
    return lax.ppermute(block, "dp", route)


def at(array, index, axis=0):
    return lax.dynamic_index_in_dim(array, index, axis, keepdims=False)


def tied(first, *then):
    return lax.optimization_barrier((first, *then))[1:]


def region(ready, body, *operands):
    blank = lambda *_: jax.tree.map(lambda o: jnp.zeros(o.shape, o.dtype), jax.eval_shape(body, *operands))
    return lax.cond(ready, body, blank, *operands)


class Group:
    def __init__(self, local_pos):
        self.dp, self.mp = lax.axis_size("dp"), lax.axis_size("mp")
        power = local_pos & (local_pos - 1) == 0
        self.size = local_pos if power and self.dp % local_pos == 0 else 1
        self.outer = self.dp // self.size
        self.member = lax.axis_index("dp") % self.size
        self.m = lax.axis_index("mp")
        self.given = self.sent = None
        self.pair = self.mp == 2

    def index(self, r):
        return lax.rem(self.m + r, 2) if self.pair else r

    def swap(self, block):
        return lax.ppermute(block, "mp", [(0, 1), (1, 0)])

    def gather(self, block):
        if self.pair:
            return [block, self.swap(block)]
        every = lax.all_gather(block, "mp", axis=0)
        return [every[r] for r in range(self.mp)]

    def scatter(self, parts, after=None):
        if self.pair:
            got = self.swap(parts[1].astype(BF16))
            if after is not None:
                got = tied(after, got)[0]
            return parts[0].astype(F32) + got.astype(F32)
        return lax.psum_scatter(jnp.stack(parts).astype(F32), "mp", scatter_dimension=0, tiled=False)

    def by_index(self, parts):
        if self.pair:
            first = self.m == 0
            return [jnp.where(first, parts[0], parts[1]), jnp.where(first, parts[1], parts[0])]
        return parts

    def route(self, step):
        return [(i, i ^ step) for i in range(self.dp)]

    def spread(self, blocks, after=None):
        held, bit = blocks[:, None], 1
        while bit < self.size:
            halves = held.reshape((held.shape[0] // 2, 2) + held.shape[1:])
            side = jnp.where((self.member & bit) != 0, 1, 0)
            self.given = at(halves, 1 - side, 1)
            got = lax.ppermute(self.given, "dp", self.route(bit))
            bit *= 2
            if after is not None and bit == self.size:
                got = tied(after, got)[0]
            held = jnp.concatenate([at(halves, side, 1), got], axis=1)
        return held[0]

    def unspread(self, blocks, after=None):
        held, bit = [blocks[s][None] for s in range(self.size)], self.size // 2
        self.sent = jnp.stack(held[bit:])
        while bit:
            got = lax.ppermute(jnp.stack(held[bit:]), "dp", self.route(bit))
            if after is not None:
                got, after = tied(after, got)[0], None
            held = [jnp.concatenate([held[s], got[s]]) for s in range(bit)]
            bit //= 2
        bits = self.size.bit_length() - 1
        turn = [int(format(s, "b").zfill(bits)[::-1] or "0", 2) for s in range(self.size)]
        return self.in_order([held[0][turn[s]] for s in range(self.size)])

    def in_order(self, blocks):
        bit = 1
        while bit < self.size:
            odd = (self.member & bit) != 0
            blocks = [jnp.where(odd, blocks[s ^ bit], blocks[s]) for s in range(self.size)]
            bit *= 2
        return jnp.stack(blocks)

    def sum_scatter(self, values):
        if self.dp & (self.dp - 1):
            return lax.psum_scatter(values, "dp", scatter_dimension=values.ndim - 1, tiled=True)
        me, bit = lax.axis_index("dp"), self.dp // 2
        while bit:
            halves = values.reshape(values.shape[:-1] + (2, values.shape[-1] // 2))
            high = (me & bit) != 0
            keep = jnp.where(high, halves[..., 1, :], halves[..., 0, :])
            give = jnp.where(high, halves[..., 0, :], halves[..., 1, :])
            values = keep + lax.ppermute(give, "dp", self.route(bit))
            bit //= 2
        return values


def params(mib, **more):
    return pltpu.CompilerParams(vmem_limit_bytes=mib * MIB, **more)


def cost(flops, moved, weight):
    return pl.CostEstimate(flops=int(flops * weight), bytes_accessed=int(moved * weight), transcendentals=0)


def call(kernel, grid, args, in_specs, outs, out_specs, scratch, name, flops, prefetch=0, aliases={}, mib=48, weight=WEIGHT):
    moved = sum(a.size * a.dtype.itemsize for a in args) + sum(o.size * o.dtype.itemsize for o in outs)
    return pl.pallas_call(
        kernel,
        grid_spec=pltpu.PrefetchScalarGridSpec(
            num_scalar_prefetch=prefetch,
            grid=grid,
            in_specs=in_specs,
            out_specs=out_specs,
            scratch_shapes=scratch,
        ),
        out_shape=outs,
        input_output_aliases=aliases,
        compiler_params=params(mib),
        cost_estimate=cost(flops, moved, weight),
        name=name,
    )(*args)


def turned(rows, heads):
    return rows.T.reshape(heads, HD, rows.shape[0])


def per_head(scores):
    return scores[:, None, :]


def attention_fwd_kernel(
    heads, held, info, own, other, gain, w_qkv, w_out,
    normed_ref, qkv_ref, probs_ref, context_ref, own_ref, other_ref, keys, values, total
):
    p = pl.program_id(0)
    is_own = (p >= info[0]) & (p < info[0] + held)
    rows = jnp.where(is_own, own[0].astype(F32), other[0].astype(F32))
    scale = lax.rsqrt(jnp.mean(rows * rows, axis=-1, keepdims=True) + EPSILON)
    normed = (rows * scale * gain[0]).astype(BF16)
    normed_ref[0] = normed
    parts = []
    for c in range(3):
        wide = turned(dot(normed, w_qkv[0, c], (1, 0)), heads)
        low = wide.astype(BF16)
        qkv_ref[0, c] = low
        parts.append(low.astype(F32))
    query = parts[0] * 0.125
    keys[p], values[p] = parts[1], parts[2]
    probs_ref[...] = jnp.full(probs_ref.shape, -1e30, F32)

    def score(j, carry):
        probs_ref[0, j] = jnp.sum(query * keys[j], axis=1)
        return carry

    lax.fori_loop(0, p + 1, score, 0)
    scores = probs_ref[0]
    weights = jnp.exp(scores - jnp.max(scores, axis=0, keepdims=True))
    probs_ref[0] = weights / jnp.sum(weights, axis=0, keepdims=True)
    total[...] = jnp.zeros_like(total)

    def mix(j, carry):
        low = probs_ref[0, j].astype(BF16).astype(F32)
        total[...] += per_head(low) * values[j]
        return carry

    lax.fori_loop(0, p + 1, mix, 0)
    context = total[...].reshape(heads * HD, -1).T.astype(BF16)
    context_ref[0] = context
    part = dot(context, w_out[0], (1, 1))

    @pl.when(is_own)
    def _():
        own_ref[0] = part

    @pl.when(jnp.logical_not(is_own))
    def _():
        other_ref[0] = part.astype(BF16)


def attention_fwd(info, own, other, gain, w_qkv, w_out):
    positions, _, width, head_width = w_qkv.shape
    heads = head_width // HD
    held, frames = own.shape[:2]
    rest = other.shape[0]
    block = lambda p, info: jnp.clip(p - info[0], 0, held - 1)
    away = lambda p, info: jnp.clip(p - info[1], 0, rest - 1)
    in_specs = [
        pl.BlockSpec((1, frames, width), lambda p, info: (block(p, info), 0, 0)),
        pl.BlockSpec((1, frames, width), lambda p, info: (away(p, info), 0, 0)),
        pl.BlockSpec((1, 1, width), lambda p, info: (p, 0, 0)),
        pl.BlockSpec((1, 3, width, head_width), lambda p, info: (p, 0, 0, 0)),
        pl.BlockSpec((1, width, head_width), lambda p, info: (p, 0, 0)),
    ]
    outs = [
        jax.ShapeDtypeStruct((positions, frames, width), BF16),
        jax.ShapeDtypeStruct((positions, 3, heads, HD, frames), BF16),
        jax.ShapeDtypeStruct((positions, positions, heads, frames), F32),
        jax.ShapeDtypeStruct((positions, frames, head_width), BF16),
        jax.ShapeDtypeStruct((held, frames, width), F32),
        jax.ShapeDtypeStruct((rest, frames, width), BF16),
    ]
    out_specs = [
        pl.BlockSpec((1, frames, width), lambda p, info: (p, 0, 0)),
        pl.BlockSpec((1, 3, heads, HD, frames), lambda p, info: (p, 0, 0, 0, 0)),
        pl.BlockSpec((1, positions, heads, frames), lambda p, info: (p, 0, 0, 0)),
        pl.BlockSpec((1, frames, head_width), lambda p, info: (p, 0, 0)),
        pl.BlockSpec((1, frames, width), lambda p, info: (block(p, info), 0, 0)),
        pl.BlockSpec((1, frames, width), lambda p, info: (away(p, info), 0, 0)),
    ]
    return call(
        functools.partial(attention_fwd_kernel, heads, held),
        (positions,),
        (info, own, other, gain, w_qkv, w_out),
        in_specs,
        outs,
        out_specs,
        [
            pltpu.VMEM((positions, heads, HD, frames), F32),
            pltpu.VMEM((positions, heads, HD, frames), F32),
            pltpu.VMEM((heads, HD, frames), F32),
        ],
        "attention_fwd",
        8 * positions * frames * width * head_width,
        prefetch=1,
    )


def attention_bwd_kernel(
    positions, heads, held, info, own, other, qkv, probs, w_qkv, w_out,
    d_qkv_ref, own_ref, other_ref, d_keys, d_values, d_query, d_scores
):
    step = pl.program_id(0)
    p = positions - 1 - step

    @pl.when(step == 0)
    def _():
        d_keys[...] = jnp.zeros_like(d_keys)
        d_values[...] = jnp.zeros_like(d_values)

    is_own = (p >= info[0]) & (p < info[0] + held)
    rows = jnp.where(is_own, own[0].astype(F32), other[0].astype(F32)).astype(BF16)
    d_context = dot(rows, w_out[0], (1, 0)).astype(BF16).astype(F32)
    d_context = turned(d_context, heads)
    d_scores[...] = jnp.zeros_like(d_scores)

    def weigh(j, carry):
        d_scores[j] = jnp.sum(d_context * qkv[j, 2].astype(F32), axis=1)
        d_values[j] += per_head(probs[0, j].astype(BF16).astype(F32)) * d_context
        return carry

    lax.fori_loop(0, p + 1, weigh, 0)
    prob, d_probs = probs[0], d_scores[...]
    d_scores[...] = (
        (prob * (d_probs - jnp.sum(prob * d_probs, axis=0, keepdims=True))).astype(BF16).astype(F32)
    ) * 0.125
    d_query[...] = jnp.zeros_like(d_query)
    query = qkv[p, 0].astype(F32)

    def back(j, carry):
        share = per_head(d_scores[j])
        d_query[...] += share * qkv[j, 1].astype(F32)
        d_keys[j] += share * query
        return carry

    lax.fori_loop(0, p + 1, back, 0)
    part = 0.0
    for c, grad in enumerate((d_query[...], d_keys[p], d_values[p])):
        low = grad.reshape(heads * HD, -1).T.astype(BF16)
        d_qkv_ref[0, c] = low
        part = part + dot(low, w_qkv[0, c], (1, 1))

    @pl.when(is_own)
    def _():
        own_ref[0] = part

    @pl.when(jnp.logical_not(is_own))
    def _():
        other_ref[0] = part.astype(BF16)


def attention_bwd(info, own, other, qkv, probs, w_qkv, w_out):
    positions, _, width, head_width = w_qkv.shape
    heads = head_width // HD
    held, frames = own.shape[:2]
    rest = other.shape[0]
    back = lambda s: positions - 1 - s
    block = lambda s, info: jnp.clip(back(s) - info[0], 0, held - 1)
    away = lambda s, info: jnp.clip(back(s) - info[1], 0, rest - 1)
    return call(
        functools.partial(attention_bwd_kernel, positions, heads, held),
        (positions,),
        (info, own, other, qkv, probs, w_qkv, w_out),
        [
            pl.BlockSpec((1, frames, width), lambda s, info: (block(s, info), 0, 0)),
            pl.BlockSpec((1, frames, width), lambda s, info: (away(s, info), 0, 0)),
            pl.BlockSpec((positions, 3, heads, HD, frames), lambda s, info: (0, 0, 0, 0, 0)),
            pl.BlockSpec((1, positions, heads, frames), lambda s, info: (back(s), 0, 0, 0)),
            pl.BlockSpec((1, 3, width, head_width), lambda s, info: (back(s), 0, 0, 0)),
            pl.BlockSpec((1, width, head_width), lambda s, info: (back(s), 0, 0)),
        ],
        [
            jax.ShapeDtypeStruct((positions, 3, frames, head_width), BF16),
            jax.ShapeDtypeStruct((held, frames, width), F32),
            jax.ShapeDtypeStruct((rest, frames, width), BF16),
        ],
        [
            pl.BlockSpec((1, 3, frames, head_width), lambda s, info: (back(s), 0, 0, 0)),
            pl.BlockSpec((1, frames, width), lambda s, info: (block(s, info), 0, 0)),
            pl.BlockSpec((1, frames, width), lambda s, info: (away(s, info), 0, 0)),
        ],
        [
            pltpu.VMEM((positions, heads, HD, frames), F32),
            pltpu.VMEM((positions, heads, HD, frames), F32),
            pltpu.VMEM((heads, HD, frames), F32),
            pltpu.VMEM((positions, heads, frames), F32),
        ],
        "attention_bwd",
        8 * positions * frames * width * head_width,
        prefetch=1,
        mib=56,
    )


def ffn_kernel(info, rows, cot, w_up, w_down, hidden_ref, d_gate_up_ref, d_rows_ref, out_ref):
    gate = dot(rows[...], w_up[0, 0], (1, 0))
    up = dot(rows[...], w_up[0, 1], (1, 0))
    sigma = jax.nn.sigmoid(gate)
    silu = gate * sigma
    hidden = (silu * up).astype(BF16)
    hidden_ref[...] = hidden
    d_hidden = dot(cot[...], w_down[0], (1, 0))
    d_gate = (d_hidden * up * sigma * (1.0 + gate * (1.0 - sigma))).astype(BF16)
    d_up = (d_hidden * silu).astype(BF16)
    d_gate_up_ref[0], d_gate_up_ref[1] = d_gate, d_up
    d_rows = dot(d_gate, w_up[0, 0], (1, 1)) + dot(d_up, w_up[0, 1], (1, 1))
    d_rows_ref[...] = d_rows.astype(d_rows_ref.dtype)
    out_ref[...] = dot(hidden, w_down[0], (1, 1)).astype(out_ref.dtype)


def ffn(position, rows, cot, w_gate_up, w_down, kind):
    count, width = rows.shape
    units = w_down.shape[2]
    block = min(count, 256)
    row = lambda i, info: (i, 0)
    return call(
        ffn_kernel,
        (count // block,),
        (position.reshape(1), rows, cot, w_gate_up, w_down),
        [
            pl.BlockSpec((block, width), row),
            pl.BlockSpec((block, width), row),
            pl.BlockSpec((1, 2, width, units), lambda i, info: (info[0], 0, 0, 0)),
            pl.BlockSpec((1, width, units), lambda i, info: (info[0], 0, 0)),
        ],
        [
            jax.ShapeDtypeStruct((count, units), BF16),
            jax.ShapeDtypeStruct((2, count, units), BF16),
            jax.ShapeDtypeStruct((count, width), kind),
            jax.ShapeDtypeStruct((count, width), kind),
        ],
        [
            pl.BlockSpec((block, units), row),
            pl.BlockSpec((2, block, units), lambda i, info: (0, i, 0)),
            pl.BlockSpec((block, width), row),
            pl.BlockSpec((block, width), row),
        ],
        [],
        "feed_forward",
        12 * count * width * units,
        prefetch=1,
        mib=56,
    )


def weight_grad_kernel(count, *refs):
    lefts, rights, out = refs[:count], refs[count:-1], refs[-1]
    sums = 0.0
    for left, right in zip(lefts, rights, strict=True):
        sums = sums + dot(left[0], right[0, 0], (0, 0))
    out[0, 0, 0] = sums.astype(BF16)


def weight_grad(lefts, rights, outer):
    groups, rows, depth = lefts[0].shape
    parts, width = rights[0].shape[1], rights[0].shape[3]
    block = depth // outer
    if block % LANES:
        full = sum(
            jnp.einsum("grd,gcrn->gcdn", left, right, preferred_element_type=F32)
            for left, right in zip(lefts, rights, strict=True)
        )
        return full.astype(BF16).reshape(groups, parts, outer, block, width).transpose(2, 0, 1, 3, 4)
    count = len(lefts)
    return call(
        functools.partial(weight_grad_kernel, count),
        (groups, parts, outer),
        (*lefts, *rights),
        [pl.BlockSpec((1, rows, block), lambda g, c, o: (g, 0, o))] * count
        + [pl.BlockSpec((1, 1, rows, width), lambda g, c, o: (g, c, 0, 0))] * count,
        [jax.ShapeDtypeStruct((outer, groups, parts, block, width), BF16)],
        [pl.BlockSpec((1, 1, 1, block, width), lambda g, c, o: (o, g, c, 0, 0))],
        [],
        "weight_grad",
        2 * count * groups * parts * rows * depth * width,
    )[0]


def ffn_grad_kernel(count, *refs):
    cots, rows, hidden, d_gate_up = (refs[i * count : (i + 1) * count] for i in range(4))
    out = refs[-1]

    @pl.when(pl.program_id(0) == 0)
    def _():
        out[0, 0] = sum(dot(x[...], y[...], (0, 0)) for x, y in zip(cots, hidden, strict=True)).astype(BF16)

    @pl.when(pl.program_id(0) > 0)
    def _():
        out[0, 0] = sum(dot(x[...], y[0], (0, 0)) for x, y in zip(rows, d_gate_up, strict=True)).astype(BF16)


def ffn_grad(cots, rows, hidden, d_gate_up, outer):
    length, depth = cots[0].shape
    width = hidden[0].shape[1]
    block = depth // outer
    if block % LANES:
        first = sum(dot(x, y, (0, 0)) for x, y in zip(cots, hidden, strict=True))[None]
        others = sum(
            jnp.einsum("rd,crn->cdn", x, y, preferred_element_type=F32)
            for x, y in zip(rows, d_gate_up, strict=True)
        )
        full = jnp.concatenate([first, others]).astype(BF16)
        return full.reshape(3, outer, block, width).transpose(1, 0, 2, 3)
    count = len(cots)
    return call(
        functools.partial(ffn_grad_kernel, count),
        (3, outer),
        (*cots, *rows, *hidden, *d_gate_up),
        [pl.BlockSpec((length, block), lambda c, o: (0, jnp.where(c == 0, o, outer - 1)))] * count
        + [pl.BlockSpec((length, block), lambda c, o: (0, jnp.where(c == 0, 0, o)))] * count
        + [pl.BlockSpec((length, width), lambda c, o: (0, 0))] * count
        + [pl.BlockSpec((1, length, width), lambda c, o: (jnp.maximum(c - 1, 0), 0, 0))] * count,
        [jax.ShapeDtypeStruct((outer, 3, block, width), BF16)],
        [pl.BlockSpec((1, 1, block, width), lambda c, o: (o, c, 0, 0))],
        [],
        "ffn_grad",
        6 * count * length * depth * width,
    )[0]


def norm_back(values, gain, upstream):
    scale = lax.rsqrt(jnp.mean(values * values, axis=-1, keepdims=True) + EPSILON)
    gained = gain[:, None, :] * upstream
    gain_grad = jnp.sum(upstream * values * scale, axis=1)
    value_grad = scale * gained - values * (scale * scale * scale) * jnp.mean(
        gained * values, axis=-1, keepdims=True
    )
    return value_grad, gain_grad


def local(
    frames_in, delays, item_bounds, attn_gain, ffn_gain, w_qkv, w_out, w_gate_up, w_down, cotangent
):
    local_pos, frames, width = frames_in.shape
    positions, head_width = w_qkv.shape[0], w_qkv.shape[3]
    group = Group(local_pos)
    mp, size, outer, pair = group.mp, group.size, group.outer, group.pair
    chunks = 2 if pair and frames % 32 == 0 else 1
    part = frames // chunks

    frame_ids = lax.axis_index("dp") * frames + jnp.arange(frames, dtype=jnp.int32)
    item_start = jnp.where(
        frame_ids >= item_bounds[1],
        item_bounds[1],
        jnp.where(frame_ids >= item_bounds[0], item_bounds[0], 0),
    )

    def delayed(lags, before, block, c):
        padded = jnp.concatenate([before, block], axis=1)
        shifted = jnp.where((lags == 1)[:, None, None], padded[:, 1:-1], padded[:, :-2])
        usable = frame_ids[None, :] - lags[:, None] >= item_start[None, :]
        usable = usable[:, c * part : (c + 1) * part]
        return jnp.where(usable[:, :, None], shifted, jnp.zeros_like(shifted))

    def delayed_chunk(lags, earlier, blocks, c):
        return delayed(lags, blocks[c - 1][:, part - 2 :] if c else earlier, blocks[c], c)

    own_blocks = [frames_in[:, c * part : (c + 1) * part] for c in range(chunks)]
    earlier = shift_frames(frames_in[:, frames - 2 :, :], 1)
    resid = [delayed_chunk(delays, earlier, own_blocks, c) for c in range(chunks)]
    if pair:
        small = jnp.concatenate(
            [attn_gain, jnp.broadcast_to(delays.astype(F32)[:, None], (local_pos, LANES))], axis=1
        )
        small = group.swap(small)
        other_blocks = []
        for block in own_blocks:
            if other_blocks:
                block = tied(other_blocks[-1], block)[0]
            other_blocks.append(group.swap(block))
        other_gain, other_lags = small[:, :width], small[:, width].astype(jnp.int32)
        other_earlier = group.swap(earlier)
        gains = jnp.concatenate(group.by_index([attn_gain, other_gain]))
        first, second = group.m * local_pos, (1 - group.m) * local_pos
        info = jnp.stack([first, second]).astype(jnp.int32)
    else:
        gains = lax.all_gather(attn_gain, "mp", axis=0, tiled=True)
        every = lax.all_gather(resid[0], "mp", axis=0, tiled=True)
        info = jnp.array([0, positions], jnp.int32)
        dummy = jnp.zeros((1, frames, width), BF16)
    gains = gains[:, None, :]

    rows = size * part
    cot_chunks = [cotangent[:, c * part : (c + 1) * part] for c in range(chunks)]
    def by_position(v, after=None):
        blocks = v.reshape((mp, size) + v.shape[1:])
        got = group.spread(jnp.moveaxis(blocks, 1, 0), after)
        got = jnp.moveaxis(got, 0, -3)
        return got.reshape(got.shape[:-3] + (rows, v.shape[-1]))

    normed_all, qkv, probs, context, attn_parts = [], [], [], [], []
    cot_own = [group.spread(chunk).reshape(rows, width) for chunk in cot_chunks]
    step = None
    for c in range(chunks):
        if not pair:
            own, other = every, dummy
        else:
            if c:
                other_blocks[c] = tied(step, other_blocks[c])[0]
            other = delayed_chunk(other_lags, other_earlier, other_blocks, c)
            own, other, cot_own[c] = lax.optimization_barrier((resid[c], other, cot_own[c]))
        *kept, own_part, other_part = attention_fwd(info, own, other, gains, w_qkv, w_out)
        step = own_part
        for held, array in zip((normed_all, qkv, probs, context), kept, strict=True):
            held.append(array)
        attn_parts.append((own_part, other_part))

    lines = [[o * size + k for o in range(outer)] for k in range(size)]

    def sum_lines(part):
        return lax.psum_scatter(
            part, "dp", scatter_dimension=0, axis_index_groups=lines, tiled=True
        )[0]

    middle, ffn_own, given = [], [], None
    for c in range(chunks):
        if pair:
            got = group.swap(attn_parts[c][1])
            if c:
                got = tied(given, got)[0]
            else:
                got, step = lax.optimization_barrier((got, step))
            whole = attn_parts[c][0] + got.astype(F32)
        else:
            whole = lax.psum_scatter(attn_parts[c][0], "mp", scatter_dimension=0, tiled=True)
        middle.append(resid[c].astype(F32) + whole)
        scale = lax.rsqrt(jnp.mean(middle[c] * middle[c], axis=-1, keepdims=True) + EPSILON)
        normed_f = (middle[c] * scale * ffn_gain[:, None, :]).astype(BF16)
        if pair and c == chunks - 1:
            last_normed_f = normed_f
            break
        ffn_own.append(group.spread(normed_f).reshape(rows, width))
        given = group.given
    def feed(r, step, x_rows, g_rows):
        position = jnp.asarray(group.index(r) * size + group.member, jnp.int32)
        kind = F32 if r == 0 or not pair else BF16
        results = []
        for c in range(chunks):
            xs, gs = tied(step, x_rows[c], g_rows[c])
            results.append(ffn(position, xs, gs, w_gate_up, w_down, kind))
            step = results[-1][0]
        return [list(v) for v in zip(*results, strict=True)]

    blocks_of = lambda d_rows: d_rows.astype(BF16).reshape(size, part, width)

    def back_to_positions(d_rows, c, after=None):
        d_normed_f = group.unspread(d_rows, after).astype(F32)
        middle_grad, gain_part = norm_back(middle[c], ffn_gain, d_normed_f)
        return cot_chunks[c].astype(F32) + middle_grad, gain_part

    ffn_sums = []
    if pair:

        def own_positions(x_rows, last, g_rows):
            last = group.spread(last).reshape(rows, width)
            swapped = [group.swap(g_rows[0]), group.swap(x_rows)]
            hidden, d_gate_up, d_own, out_own = feed(0, x_rows, [x_rows, last], g_rows)
            hidden[1], *swapped = lax.optimization_barrier((hidden[1], *swapped))
            grad = ffn_grad(g_rows, [x_rows, last], hidden, d_gate_up, outer)
            return grad, last, swapped, d_own, out_own

        grad_own, last, (cot_other, ffn_other), d_own, out_own = region(
            item_bounds[0] >= 0, own_positions, ffn_own[0], last_normed_f, cot_own
        )
        ffn_sums.append(sum_lines(grad_own))

        def other_positions(x_first, g_first, x_last, g_last, d_own, normed):
            x_rows, g_rows = [x_first, group.swap(x_last)], [g_first, group.swap(g_last)]
            hidden, d_gate_up, d_other, out_other = feed(1, x_first, x_rows, g_rows)
            normed = [by_position(v) for v in normed]
            got = group.swap(d_other[0])
            got, *normed = lax.optimization_barrier((got, *normed))
            d_first = blocks_of(d_own[0] + got.astype(F32))
            hidden[0] = tied(d_first, hidden[0])[0]
            grad = ffn_grad(g_rows, x_rows, hidden, d_gate_up, outer)
            d_middle, gain_part = back_to_positions(d_first, 0, grad)
            got = tied(grad, group.swap(d_other[1]))[0]
            d_late, gain_late = back_to_positions(blocks_of(d_own[1] + got.astype(F32)), 1)
            low = d_middle.astype(BF16)
            d_middle = [d_middle, d_late]
            lows = [low, d_late.astype(BF16)]
            return grad, d_middle, lows, group.swap(low), gain_part + gain_late, out_other, normed

        grad, d_middle, d_middle_low, d_first, ffn_gain_part, out_other, normed_rows = region(
            item_bounds[0] >= 0,
            other_positions,
            ffn_other,
            cot_other,
            last,
            cot_own[1],
            d_own,
            normed_all,
        )
        out_parts = [out_own, out_other]
        ffn_sums[0], d_middle_low[1] = lax.optimization_barrier((ffn_sums[0], d_middle_low[1]))
        ffn_sums.append(sum_lines(tied(ffn_sums[0], grad)[0]))
    else:
        normed_rows = [by_position(normed_all[0])]
        context_rows = [by_position(context[0])[:, None]]
        cot_rows = [[block] for block in group.gather(cot_own[0])]
        ffn_rows = [[block] for block in group.gather(ffn_own[0])]
        d_parts, out_parts = [], []
        for r in range(mp):
            hidden, d_gate_up, d_part, out_part = feed(r, step, ffn_rows[r], cot_rows[r])
            d_parts.append(d_part[0])
            out_parts.append(out_part)
            step = ffn_grad(cot_rows[r], ffn_rows[r], hidden, d_gate_up, outer)
            ffn_sums.append(sum_lines(step))
        d_mid, ffn_gain_part = back_to_positions(blocks_of(group.scatter(d_parts)), 0)
        d_middle, d_middle_low = [d_mid], [d_mid.astype(BF16)]
        d_middle_all = [lax.all_gather(d_middle_low[0], "mp", axis=0, tiled=True)]
        d_middle_two = [[d_middle_all[0], dummy]]

    def finish(whole):
        depth, n = whole.shape[-2:]
        blocks = whole.reshape(whole.shape[:-2] + (size, depth // size, n))
        return group.in_order(group.spread(jnp.moveaxis(blocks, -3, 0)))

    def ends(d_normed_a, out_rows, middle, d_middle, ffn_gain_part):
        mixed = []
        for c in range(chunks):
            got = group.unspread(blocks_of(out_rows[c]))
            mixed.append((middle[c] + got.astype(F32)).astype(BF16))
        mixed = jnp.concatenate(mixed, axis=1)

        d_resid, attn_gain_part = [], 0.0
        for c in range(chunks):
            resid_grad, gain_part = norm_back(resid[c].astype(F32), attn_gain, d_normed_a[c])
            attn_gain_part = attn_gain_part + gain_part
            d_resid.append(d_middle[c] + resid_grad)
        d_resid = jnp.concatenate(d_resid, axis=1)
        usable = frame_ids[None, :] - delays[:, None] >= item_start[None, :]
        spread = jnp.where(usable[:, :, None], d_resid, 0.0)
        one = (delays == 1)[:, None, None]
        blank = jnp.zeros((local_pos, 1, width), F32)
        head = spread[:, :2]
        placed = jnp.where(one, jnp.concatenate([blank, head[:, :1]], axis=1), head)
        returned = shift_frames(placed, -1)
        tail = jnp.concatenate([spread, blank, blank], axis=1)
        input_grad = jnp.where(one, tail[:, 1 : frames + 1], tail[:, 2:])
        input_grad = input_grad + jnp.pad(returned, ((0, 0), (frames - 2, 0), (0, 0)))
        gains = group.sum_scatter(jnp.stack([attn_gain_part, ffn_gain_part]))
        return mixed, input_grad, gains[0], gains[1]

    if pair:

        def attention_back(d_middle_low, d_first, qkv, probs, normed_rows, out_other, sums):
            d_last = group.swap(d_middle_low[1])
            two = [[d_middle_low[0], d_first], [d_middle_low[1], d_last]]
            d_qkv, own_first, other_first = attention_bwd(info, *two[0], qkv[0], probs[0], w_qkv, w_out)
            two[1] = tied(d_qkv, *two[1])
            sums = finish(sums)
            *two[1], sums = lax.optimization_barrier((*two[1], sums))
            d_later, own_last, other_last = attention_bwd(info, *two[1], qkv[1], probs[1], w_qkv, w_out)
            d_qkv, d_later = by_position(d_qkv), by_position(d_later)
            sent = [group.swap(block) for block in out_other]
            d_later, *sent = lax.optimization_barrier((d_later, *sent))
            qkv_part = weight_grad(normed_rows, [d_qkv, d_later], outer)
            return qkv_part, d_last, [own_first, own_last], [other_first, other_last], sent, sums

        qkv_part, d_last, own_parts, other_parts, sent, ffn_first = region(
            item_bounds[0] >= 0,
            attention_back,
            d_middle_low,
            d_first,
            qkv,
            probs,
            normed_rows,
            out_parts[1],
            ffn_sums[0],
        )
        ffn_sums[1], own_parts[0] = lax.optimization_barrier((ffn_sums[1], own_parts[0]))
        qkv_sums = sum_lines(tied(ffn_sums[1], qkv_part)[0])

        def others(d_two, context, own_parts, other_parts, out_own, sent, middle, d_middle, sums, gain_part):
            d_normed_a = [group.scatter([own_parts[c], other_parts[c]]) for c in range(chunks)]
            out_rows = [out_own[c] + sent[c].astype(F32) for c in range(chunks)]
            held = [by_position(v)[:, None] for v in context]
            out_part = weight_grad(
                [by_position(jnp.concatenate(group.by_index(two))) for two in d_two], held, outer
            )
            return out_part, finish(sums), *ends(d_normed_a, out_rows, middle, d_middle, gain_part)

        out_part, ffn_last, mixed, input_grad, attn_gain_grad, ffn_gain_grad = region(
            item_bounds[0] >= 0,
            others,
            [[d_middle_low[0], d_first], [d_middle_low[1], d_last]],
            context,
            own_parts,
            other_parts,
            out_parts[0],
            sent,
            middle,
            d_middle,
            ffn_sums[1],
            ffn_gain_part,
        )
        qkv_sums, out_part = lax.optimization_barrier((qkv_sums, out_part))
        out_sums = sum_lines(out_part)
        ffn_done = [ffn_first, ffn_last]
    else:
        d_qkv, own_part, _ = attention_bwd(info, *d_middle_two[0], qkv[0], probs[0], w_qkv, w_out)
        d_normed_a = [lax.psum_scatter(own_part, "mp", scatter_dimension=0, tiled=True)]
        out_part = weight_grad([by_position(d_middle_all[0])], context_rows, outer)
        qkv_part = weight_grad(normed_rows, [by_position(d_qkv)], outer)
        out_rows = [group.scatter([out_parts[r][0] for r in range(mp)])]
        qkv_sums, out_sums = sum_lines(qkv_part), sum_lines(out_part)
        ffn_done = [finish(sums) for sums in ffn_sums]
        mixed, input_grad, attn_gain_grad, ffn_gain_grad = ends(
            d_normed_a, out_rows, middle, d_middle, ffn_gain_part
        )

    qkv_done = finish(qkv_sums)
    out_done = finish(tied(qkv_done, out_sums)[0])
    ffn_done = jnp.stack(group.by_index(ffn_done)).astype(F32)
    ffn_done = ffn_done.reshape((positions,) + ffn_done.shape[2:])
    down_grad, gate_up_grad = ffn_done[:, 0], ffn_done[:, 1:]

    def both(got):
        got = jnp.swapaxes(got, 0, 1)
        return got.reshape((positions,) + got.shape[2:]).astype(F32)

    out_grad, qkv_grad = both(out_done)[:, 0], both(qkv_done)
    return (
        mixed,
        input_grad,
        attn_gain_grad,
        ffn_gain_grad,
        qkv_grad,
        out_grad,
        gate_up_grad,
        down_grad,
    )


def solution(mesh):
    placed = (
        P("mp", "dp", None),
        P("mp"),
        P(),
        P("mp", None),
        P("mp", None),
        P(None, None, None, "mp"),
        P(None, None, "mp"),
        P(None, None, None, "mp"),
        P(None, None, "mp"),
        P("mp", "dp", None),
    )
    return jax.shard_map(
        local,
        mesh=mesh,
        in_specs=placed,
        out_specs=(
            P("mp", "dp", None),
            P("mp", "dp", None),
            P("mp", "dp"),
            P("mp", "dp"),
            P(None, None, "dp", "mp"),
            P(None, "dp", "mp"),
            P(None, None, "dp", "mp"),
            P(None, "dp", "mp"),
        ),
        check_vma=False,
    )
```

time: 1230 us -> 776 us (0.63)
  waiting for transfers between devices: 559 us -> 281 us
  matrix products: 174 us -> 0 us
  Pallas kernels: 63.1 us -> 217 us
  local copies, waits for them, and re-layouts: 208 us -> 74.9 us
  other arithmetic: 143 us -> 118 us
    ppermute x8 -> x18, waiting for transfers between devices: 266 us -> 80.5 us  [swap(): return lax.ppermute(block, 'mp', [(0, 1), (1, 0)])]
    dot_general x14 -> x0, matrix products: 174 us -> none  [the longest x1 25.6 us: local(): jnp.einsum('pcfe,pcde->pfd', d_qkv, w_qkv, preferred_element_type=F32)]
    pallas_call x4 -> x12, Pallas kernels: 63.1 us -> 217 us  [call(): pl.pallas_call(kernel, grid_spec=pltpu.PrefetchScalarGridSpec(num_scalar_...]
    reduce_scatter x4, waiting for transfers between devices: 97.8 us -> 33.5 us  [sum_lines(): lax.psum_scatter(part, 'dp', scatter_dimension=0, axis_index_groups=lines...]
    another operation x25 -> x0, local copies, waits for them, and re-layouts: 49.7 us -> none
    ppermute x42 -> x40, waiting for transfers between devices: 189 us -> 141 us  [the longest x32 121 us: spread(): got = lax.ppermute(self.given, 'dp', self.route(bit))]
    concatenate x0 -> x33, other arithmetic: none -> 45.9 us  [the longest x28 43.2 us: spread(): held = jnp.concatenate([at(halves, side, 1), got], axis=1)]
    unnamed x136 -> x59, local copies, waits for them, and re-layouts: 41.1 us -> 9.15 us
  transfers between devices with their start and end apart: 60 -> 68, of which waited for: 27 -> 23; matrix products, arithmetic and copies ran while one was open for 27% -> 22% of each run, Pallas kernels for 5% -> 26%
where the time goes in v2:
time: 776 us; the launch traced here: 765 us
  waiting for transfers between devices  281 us (36%)
  Pallas kernels  217 us (28%)
  other arithmetic  118 us (15%)
  local copies, waits for them, and re-layouts  74.9 us (10%)
  starting transfers between devices  57.4 us (7%)
  between operations  15.4 us (2%)
    pallas_call x12, Pallas kernels, call(): pl.pallas_call(kernel, grid_spec=pltpu.PrefetchScalarGridSpec(num_scalar_...  217 us
    ppermute x32, waiting for transfers between devices, spread(): got = lax.ppermute(self.given, 'dp', self.route(bit))  121 us
    ppermute x18, waiting for transfers between devices, swap(): return lax.ppermute(block, 'mp', [(0, 1), (1, 0)])  80.5 us
    concatenate x28, other arithmetic, spread(): held = jnp.concatenate([at(halves, side, 1), got], axis=1)  43.2 us
    reduce_scatter x4, waiting for transfers between devices, sum_lines(): lax.psum_scatter(part, 'dp', scatter_dimension=0, axis_index_groups=lines...  33.5 us
    ppermute x4, waiting for transfers between devices, sum_scatter(): values = keep + lax.ppermute(give, 'dp', self.route(bit))  25.7 us
    cond x115, local copies, waits for them, and re-layouts  23.3 us
    ppermute x32, starting transfers between devices, spread(): got = lax.ppermute(self.given, 'dp', self.route(bit))  22.5 us
  transfers between devices with their start and end apart: 68, of which 23 were waited for; matrix products, arithmetic and copies ran while one was open for 22% of the time, Pallas kernels for 26%

profile of v2, /device:TPU:0, one launch (start us, length us, event | category | flops | bytes accessed | tf_op | source)
XLA Modules:
  0.0 765.2 jit_solution(7551485890790051916)
XLA Ops:
  8.1 2.4 collective-permute-start.49
  11.9 2.3 collective-permute-start.47
  22.3 4.4 fusion.100
  32.9 11.9 %collective-permute-done.52 = bf16[1,2,128,1024]{3,2,1,0:T(8,128)(2,1)S(1)} collective-permute-done((bf16[1,2,128,1024]{3,2,1,0:T(8,128)(2,1)S(1)}, bf16[1,2,128,1024]{3,2,1,0:T(8,128)(2,1)S(1)}, u32[]{:S(2)}, u32[]{:S(2)}) %collective-permute-start.52) | collective-permute-done | bytes 524320 | tf_op jit(solution)/shard_map/ppermute | solution.py:88
  45.9 9.0 %collective-permute-done.55 = bf16[1,2,128,1024]{3,2,1,0:T(8,128)(2,1)S(1)} collective-permute-done((bf16[1,2,128,1024]{3,2,1,0:T(8,128)(2,1)S(1)}, bf16[1,2,128,1024]{3,2,1,0:T(8,128)(2,1)S(1)}, u32[]{:S(2)}, u32[]{:S(2)}) %collective-permute-start.55) | collective-permute-done | bytes 524320 | tf_op jit(solution)/shard_map/ppermute | solution.py:88
  57.5 19.8 %attention_fwd.2 = (bf16[8,128,1024]{2,1,0:T(8,128)(2,1)}, bf16[8,3,8,64,128]{4,3,2,1,0:T(8,128)(2,1)}, f32[8,8,8,128]{3,2,1,0:T(8,128)}, bf16[8,128,512]{2,1,0:...) custom-call(s32[2]{0:T(128)S(1)} %pad_add_fusion.1.info, ...), custom_call_target="tpu_custom_call" | custom-call | flops 429496729600 | bytes 4538369024 | tf_op jit(solution)/shard_map/attention_fwd/pallas_call | solution.py:140
  79.9 3.4 collective-permute-done.53
  83.4 2.4 fusion.74.other
  85.8 19.6 %attention_fwd.3 = (bf16[8,128,1024]{2,1,0:T(8,128)(2,1)}, bf16[8,3,8,64,128]{4,3,2,1,0:T(8,128)(2,1)}, f32[8,8,8,128]{3,2,1,0:T(8,128)}, bf16[8,128,512]{2,1,0:...) custom-call(s32[2]{0:T(128)S(1)} %pad_add_fusion.1.info, ...), custom_call_target="tpu_custom_call" | custom-call | flops 429496729600 | bytes 4538369024 | tf_op jit(solution)/shard_map/attention_fwd/pallas_call | solution.py:140
  114.0 15.0 %collective-permute-done.59 = bf16[4,128,1024]{2,1,0:T(8,128)(2,1)} collective-permute-done((bf16[4,128,1024]{2,1,0:T(8,128)(2,1)S(1)}, bf16[4,128,1024]{2,1,0:T(8,128)(2,1)}, u32[]{:S(2)}, u32[]{:S(2)}) %collective-permute-start.59) | collective-permute-done | bytes 1048608 | tf_op jit(solution)/shard_map/ppermute | solution.py:57
  132.4 66.9 %conditional.4 = (bf16[4,3,256,1408]{3,2,1,0:T(8,128)(2,1)}, bf16[512,1024]{1,0:T(8,128)(2,1)}, bf16[512,1024]{1,0:T(8,128)(2,1)}, bf16[512,1024]{1,0:T(8,128)(2...) conditional(s32[]{:T(128)} %convert_element_type.132, () %tuple.72, ...), branch_computations={%region_2.3_spmd, %region_3.4_spmd} | conditional | flops 2657512062976 | bytes 18158192640 | solution.py:39
  137.5 16.6 %feed_forward.4 = (bf16[512,1408]{1,0:T(8,128)(2,1)}, bf16[2,512,1408]{2,1,0:T(8,128)(2,1)}, f32[512,1024]{1,0:T(8,128)}, f32[512,1024]{1,0:T(8,128)}) custom-call(s32[1]{0:T(128)} %bitcast.5.info, bf16[512,1024]{1,0:T(8,128)(2,1)} %bitcast.rows.refs_2_, bf16[512,1024]{1,0:T(8,128)(2,1)} %get-tuple-element.160.cot.refs_0_, ...), custom_call_target="tpu_custom_call" | custom-call | flops 885837004800 | bytes 7982285312 | tf_op jit(solution)/shard_map/cond/branch_1_fun/feed_forward/pallas_call | solution.py:140
  156.3 16.7 %feed_forward.5 = (bf16[512,1408]{1,0:T(8,128)(2,1)}, bf16[2,512,1408]{2,1,0:T(8,128)(2,1)}, f32[512,1024]{1,0:T(8,128)}, f32[512,1024]{1,0:T(8,128)}) custom-call(s32[1]{0:T(128)} %bitcast.5.info, bf16[512,1024]{1,0:T(8,128)(2,1)} %bitcast.4.rows.refs_3_, bf16[512,1024]{1,0:T(8,128)(2,1)} %get-tuple-element.165.cot.refs_1_, ...), custom_call_target="tpu_custom_call" | custom-call | flops 885837004800 | bytes 7982285312 | tf_op jit(solution)/shard_map/cond/branch_1_fun/feed_forward/pallas_call | solution.py:140
  173.0 8.1 %collective-permute-done.2 = bf16[512,1024]{1,0:T(8,128)(2,1)} collective-permute-done((bf16[512,1024]{1,0:T(8,128)(2,1)}, bf16[512,1024]{1,0:T(8,128)(2,1)}, u32[]{:S(2)}, u32[]{:S(2)}) %collective-permute-start.2) | collective-permute-done | bytes 1048608 | tf_op jit(solution)/shard_map/cond/branch_1_fun/ppermute | solution.py:57
  182.5 16.8 %ffn_grad.2 = bf16[4,3,256,1408]{3,2,1,0:T(8,128)(2,1)} custom-call(bf16[512,1024]{1,0:T(8,128)(2,1)} %get-tuple-element.160.cot.refs_0_, bf16[512,1024]{1,0:T(8,128)(2,1)} %get-tuple-element.165.cot.refs_1_, bf16[512,1024]{1,0:T(8,128)(2,1)} %bitcast.rows.refs_2_, bf16[512,1024]{1,0:T(8,128)(2,1)} %bitcast.4.rows.refs_3_, bf16[512,1408]{1,0:T(8,128)(2,1)S(1)} %copy-done.2, ...), custom_call_target="tpu_custom_call" | custom-call | flops 885837004800 | bytes 2149580800 | tf_op jit(solution)/shard_map/cond/branch_1_fun/ffn_grad/pallas_call | solution.py:140
  200.8 153.5 %conditional.5 = (bf16[4,3,256,1408]{3,2,1,0:T(8,128)(2,1)}, f32[4,128,1024]{2,1,0:T(8,128)}, f32[4,128,1024]{2,1,0:T(8,128)}, bf16[4,128,1024]{2,1,0:T(8,128)(2...) conditional(s32[]{:T(128)} %convert_element_type.132, () %tuple.67, ...), branch_computations={%region_5.6_spmd, %region_6.13_spmd} | conditional | flops 2657546665984 | bytes 17895268352 | solution.py:39
  208.9 16.9 %feed_forward.6 = (bf16[512,1408]{1,0:T(8,128)(2,1)}, bf16[2,512,1408]{2,1,0:T(8,128)(2,1)}, bf16[512,1024]{1,0:T(8,128)(2,1)}, bf16[512,1024]{1,0:T(8,128)(2,1)}) custom-call(s32[1]{0:T(128)} %bitcast.6.info, bf16[512,1024]{1,0:T(8,128)(2,1)} %get-tuple-element.182.rows.refs_2_, bf16[512,1024]{1,0:T(8,128)(2,1)} %get-tuple-element.183.cot.refs_0_, ...), custom_call_target="tpu_custom_call" | custom-call | flops 885837004800 | bytes 7772570112 | tf_op jit(solution)/shard_map/cond/branch_1_fun/feed_forward/pallas_call | solution.py:140
  229.5 2.6 multiply_reduce_fusion
  232.7 2.7 fusion.19
  236.9 2.7 fusion.17
  240.1 9.9 %collective-permute-done.14.rows.refs_3_ = bf16[512,1024]{1,0:T(8,128)(2,1)} collective-permute-done((bf16[512,1024]{1,0:T(8,128)(2,1)}, bf16[512,1024]{1,0:T(8,128)(2,1)}, u32[]{:S(2)}, u32[]{:S(2)}) %collective-permute-start.14) | collective-permute-done | bytes 1048608 | tf_op jit(solution)/shard_map/cond/branch_1_fun/ppermute | solution.py:57
  250.0 16.4 %feed_forward.7 = (bf16[512,1408]{1,0:T(8,128)(2,1)}, bf16[2,512,1408]{2,1,0:T(8,128)(2,1)}, bf16[512,1024]{1,0:T(8,128)(2,1)}, bf16[512,1024]{1,0:T(8,128)(2,1)}) custom-call(s32[1]{0:T(128)} %bitcast.6.info, bf16[512,1024]{1,0:T(8,128)(2,1)} %collective-permute-done.14.rows.refs_3_, bf16[512,1024]{1,0:T(8,128)(2,1)} %collective-permute-done.13.cot.refs_1_, ...), custom_call_target="tpu_custom_call" | custom-call | flops 885837004800 | bytes 7772570112 | tf_op jit(solution)/shard_map/cond/branch_1_fun/feed_forward/pallas_call | solution.py:140
  269.1 17.9 %ffn_grad.3 = bf16[4,3,256,1408]{3,2,1,0:T(8,128)(2,1)} custom-call(bf16[512,1024]{1,0:T(8,128)(2,1)} %get-tuple-element.183.cot.refs_0_, bf16[512,1024]{1,0:T(8,128)(2,1)} %collective-permute-done.13.cot.refs_1_, bf16[512,1024]{1,0:T(8,128)(2,1)} %get-tuple-element.182.rows.refs_2_, bf16[512,1024]{1,0:T(8,128)(2,1)} %collective-permute-done.14.rows.refs_3_, ...), custom_call_target="tpu_custom_call" | custom-call | flops 885837004800 | bytes 2149580800 | tf_op jit(solution)/shard_map/cond/branch_1_fun/ffn_grad/pallas_call | solution.py:140
  287.1 2.8 pad_maximum_fusion.1
  289.9 2.7 pad_maximum_fusion.2
  300.4 10.4 %collective-permute-done.23 = bf16[2,1,128,1024]{3,2,1,0:T(8,128)(2,1)S(1)} collective-permute-done((bf16[2,1,128,1024]{3,2,1,0:T(8,128)(2,1)S(1)}, bf16[2,1,128,1024]{3,2,1,0:T(8,128)(2,1)S(1)}, u32[]{:S(2)}, u32[]{:S(2)}) %collective-permute-start.23) | collective-permute-done | bytes 524320 | tf_op jit(solution)/shard_map/cond/branch_1_fun/ppermute | solution.py:99
  311.1 8.7 %collective-permute-done.20 = bf16[2,1,128,1024]{3,2,1,0:T(8,128)(2,1)S(1)} collective-permute-done((bf16[2,1,128,1024]{3,2,1,0:T(8,128)(2,1)S(1)}, bf16[2,1,128,1024]{3,2,1,0:T(8,128)(2,1)S(1)}, u32[]{:S(2)}, u32[]{:S(2)}) %collective-permute-start.20) | collective-permute-done | bytes 524320 | tf_op jit(solution)/shard_map/cond/branch_1_fun/ppermute | solution.py:99
  322.0 3.9 fusion.93
  326.0 2.4 fusion.95
  330.3 23.8 %collective-permute-done.25 = bf16[4,128,1024]{2,1,0:T(8,128)(2,1)} collective-permute-done((bf16[4,128,1024]{2,1,0:T(8,128)(2,1)}, bf16[4,128,1024]{2,1,0:T(8,128)(2,1)}, u32[]{:S(2)}, u32[]{:S(2)}) %collective-permute-start.25) | collective-permute-done | bytes 1048608 | tf_op jit(solution)/shard_map/cond/branch_1_fun/ppermute | solution.py:57
  355.4 164.5 %conditional.6 = (bf16[4,2,3,256,512]{4,3,2,1,0:T(8,128)(2,1)}, bf16[4,128,1024]{2,1,0:T(8,128)(2,1)}, f32[4,128,1024]{2,1,0:T(8,128)}, f32[4,128,1024]{2,1,0:T(...) conditional(s32[]{:T(128)} %convert_element_type.132, () %tuple.78, ...), branch_computations={%region_13.14_spmd, %region_14.15_spmd} | conditional | flops 1503251267584 | bytes 10903095296 | solution.py:39
  364.4 23.3 %attention_bwd.2 = (bf16[8,3,128,512]{3,2,1,0:T(8,128)(2,1)}, f32[4,128,1024]{2,1,0:T(8,128)}, bf16[4,128,1024]{2,1,0:T(8,128)(2,1)}) custom-call(s32[2]{0:T(128)S(1)} %get-tuple-element.212.info, bf16[4,128,1024]{2,1,0:T(8,128)(2,1)} %get-tuple-element.213.own, bf16[4,128,1024]{2,1,0:T(8,128)(2,1)} %get-tuple-element.214.other, ...), custom_call_target="tpu_custom_call" | custom-call | flops 429496729600 | bytes 4535092224 | tf_op jit(solution)/shard_map/cond/branch_1_fun/attention_bwd/pallas_call | solution.py:140
  387.7 3.3 constant_dynamic-slice_fusion.6
  396.9 23.5 %attention_bwd.3 = (bf16[8,3,128,512]{3,2,1,0:T(8,128)(2,1)}, f32[4,128,1024]{2,1,0:T(8,128)}, bf16[4,128,1024]{2,1,0:T(8,128)(2,1)}) custom-call(s32[2]{0:T(128)S(1)} %get-tuple-element.212.info, bf16[4,128,1024]{2,1,0:T(8,128)(2,1)} %get-tuple-element.225.own, bf16[4,128,1024]{2,1,0:T(8,128)(2,1)} %collective-permute-done.6.other, ...), custom_call_target="tpu_custom_call" | custom-call | flops 429496729600 | bytes 4535092224 | tf_op jit(solution)/shard_map/cond/branch_1_fun/attention_bwd/pallas_call | solution.py:140
  430.3 32.7 %collective-permute-done.5 = bf16[1,2,2,3,128,512]{5,4,1,3,2,0:T(8,128)(2,1)S(1)} collective-permute-done((bf16[1,2,2,3,128,512]{5,4,1,3,2,0:T(8,128)(2,1)S(1)}, bf16[1,2,2,3,128,512]{5,4,1,3,2,0:T(8,128)(2,1)S(1)}, u32[]{:S(2)}, u32[]{:S(2)}) %collective-permute-start.5) | collective-permute-done | bytes 1572896 | tf_op jit(solution)/shard_map/cond/branch_1_fun/ppermute | solution.py:88
  463.3 32.8 %collective-permute-done.10 = bf16[1,2,2,3,128,512]{5,4,1,3,2,0:T(8,128)(2,1)S(1)} collective-permute-done((bf16[1,2,2,3,128,512]{5,4,1,3,2,0:T(8,128)(2,1)S(1)}, bf16[1,2,2,3,128,512]{5,4,1,3,2,0:T(8,128)(2,1)S(1)}, u32[]{:S(2)}, u32[]{:S(2)}) %collective-permute-start.10) | collective-permute-done | bytes 1572896 | tf_op jit(solution)/shard_map/cond/branch_1_fun/ppermute | solution.py:88
  498.1 21.8 %weight_grad.2 = bf16[4,2,3,256,512]{4,3,2,1,0:T(8,128)(2,1)} custom-call(bf16[2,512,1024]{2,1,0:T(8,128)(2,1)} %get-tuple-element.210.refs_0_, bf16[2,512,1024]{2,1,0:T(8,128)(2,1)} %get-tuple-element.211.refs_1_, bf16[2,3,512,512]{3,2,1,0:T(8,128)(2,1)S(1)} %bitcast.487, bf16[2,3,512,512]{3,2,1,0:T(8,128)(2,1)} %bitcast.508), custom_call_target="tpu_custom_call" | custom-call | flops 644245094400 | bytes 1677721600 | tf_op jit(solution)/shard_map/cond/branch_1_fun/weight_grad/pallas_call | solution.py:140
  521.7 171.7 %conditional.7 = (bf16[4,2,1,256,512]{4,3,2,1,0:T(8,128)(2,1)}, bf16[4,3,64,1408]{3,2,1,0:T(8,128)(2,1)}, bf16[4,256,1024]{2,1,0:T(8,128)(2,1)}, f32[4,256,1024]...) conditional(s32[]{:T(128)} %convert_element_type.132, () %tuple.66, (s32[]{:T(128)}, ...), branch_computations={%region_16.17_spmd, %region_17.24_spmd} | conditional | flops 214808363008 | bytes 1174617984 | solution.py:39
  522.0 2.2 add_convert_fusion.5
  527.1 2.3 add_convert_fusion.3
  537.5 2.5 broadcast_select_fusion.13
  548.8 2.4 copy.244
  564.5 19.3 %collective-permute-done.41 = bf16[4,128,1024]{2,1,0:T(8,128)(2,1)} collective-permute-done((bf16[4,128,1024]{2,1,0:T(8,128)(2,1)}, bf16[4,128,1024]{2,1,0:T(8,128)(2,1)}, u32[]{:S(2)}, u32[]{:S(2)}) %collective-permute-start.41) | collective-permute-done | bytes 1048608 | tf_op jit(solution)/shard_map/cond/branch_1_fun/ppermute | solution.py:57
  583.9 4.5 fusion.40
  588.4 4.7 fusion.37
  601.7 2.7 collective-permute-start.43
  605.6 5.6 collective-permute-done.43
  613.5 2.9 fusion.53
  616.4 3.5 collective-permute-done.44
  621.5 2.5 collective-permute-start.45
  625.3 16.6 %collective-permute-done.45 = f32[2,4,128]{2,1,0:T(4,128)S(1)} collective-permute-done((f32[2,4,128]{2,1,0:T(4,128)S(1)}, f32[2,4,128]{2,1,0:T(4,128)S(1)}, u32[]{:S(2)}, u32[]{:S(2)}) %collective-permute-start.45) | collective-permute-done | bytes 4128 | tf_op jit(solution)/shard_map/cond/branch_1_fun/ppermute | solution.py:125
  644.7 3.0 fusion.48
  649.1 3.1 pad_add_fusion
  652.1 2.8 pad_maximum_fusion.14
  654.9 13.4 %collective-permute-done.27 = bf16[1,2,2,128,1024]{4,3,1,2,0:T(8,128)(2,1)} collective-permute-done((bf16[1,2,2,128,1024]{4,3,1,2,0:T(8,128)(2,1)}, bf16[1,2,2,128,1024]{4,3,1,2,0:T(8,128)(2,1)}, u32[]{:S(2)}, u32[]{:S(2)}) %collective-permute-start.27) | collective-permute-done | bytes 1048608 | tf_op jit(solution)/shard_map/cond/branch_1_fun/ppermute | solution.py:88
  669.7 7.5 weight_grad.3
  677.2 12.7 %collective-permute-done.35 = bf16[1,2,3,64,1408]{4,3,2,1,0:T(8,128)(2,1)} collective-permute-done((bf16[1,2,3,64,1408]{4,3,2,1,0:T(8,128)(2,1)}, bf16[1,2,3,64,1408]{4,3,2,1,0:T(8,128)(2,1)}, u32[]{:S(2)}, u32[]{:S(2)}) %collective-permute-start.35) | collective-permute-done | bytes 1081376 | tf_op jit(solution)/shard_map/cond/branch_1_fun/ppermute | solution.py:88
  695.2 2.6 select_bitcast_fusion.11
  698.4 4.2 copy.181
  703.9 33.5 %reduce-scatter.11.cloned.1.call-done = bf16[1,2,1,256,512]{4,3,2,1,0:T(8,128)(2,1)} async-done(((bf16[4,2,1,256,512]{4,3,2,1,0:T(8,128)(2,1)}), bf16[1,2,1,256,512]{4,3,2,1,0:T(8,128)(2,1)}) %reduce-scatter.11.cloned.1.call-update) | async-done | bytes 524304 | tf_op jit(solution)/shard_map/reduce_scatter | solution.py:574
  738.6 3.6 slice_bitcast_fusion.22
  742.2 3.0 slice.461
  745.2 2.9 copy.182
  751.9 5.1 collective-permute-done.63
  (418 shorter events, 168.5 us)
Async XLA Ops:
  7.2 347.2 %reduce-scatter.5.cloned.1.call-start = ((), (), s32[]{:S(2)}) async-start(), calls=%async_computation.4 | async-start | bytes 10813440 | tf_op jit(solution)/shard_map/reduce_scatter | solution.py:574
  8.1 13.5 %collective-permute-start.49 = (bf16[4,2,1024]{2,1,0:T(2,128)(2,1)S(1)}, bf16[4,2,1024]{2,1,0:T(2,128)(2,1)S(1)}, u32[]{:S(2)}, u32[]{:S(2)}) collective-permute-start(bf16[4,2,1024]{2,1,0:T(2,128)(2,1)S(1)} %slice.368), channel_id=1, source_target_pairs={{0,2},{2,4},{4,6},{6,8},{8,10},{10,12},{12,14},{14,16},{16,18},{18... | collective-permute-start | bytes 49160 | tf_op jit(solution)/shard_map/ppermute | solution.py:26
  11.9 10.2 %collective-permute-start.47 = (f32[4,1152]{1,0:T(4,128)S(1)}, f32[4,1152]{1,0:T(4,128)S(1)}, u32[]{:S(2)}, u32[]{:S(2)}) collective-permute-start(f32[4,1152]{1,0:T(4,128)S(1)} %pad_maximum_fusion.29), channel_id=1, source_target_pairs={{0,1},{1,0},{2,3},{3,2},{4,5},{5,4},{6,7},{7,6},{8,9},{9,8},{10,11... | collective-permute-start | bytes 55304 | tf_op jit(solution)/shard_map/ppermute | solution.py:57
  17.2 11.5 %collective-permute-start.51 = (bf16[2,1,128,1024]{3,2,1,0:T(8,128)(2,1)}, bf16[2,1,128,1024]{3,2,1,0:T(8,128)(2,1)}, u32[]{:S(2)}, u32[]{:S(2)}) collective-permute-start(bf16[2,1,128,1024]{3,2,1,0:T(8,128)(2,1)} %get-tuple-element.594), channel_id=1, source_target_pairs={{0,2},{2,0},{4,6},{6,4},{8,10},{10,8},{12,14},{14,12},{16,18},{18,... | collective-permute-start | bytes 1572872 | tf_op jit(solution)/shard_map/ppermute | solution.py:88
  19.6 11.9 %collective-permute-start.54 = (bf16[2,1,128,1024]{3,2,1,0:T(8,128)(2,1)}, bf16[2,1,128,1024]{3,2,1,0:T(8,128)(2,1)S(1)}, u32[]{:S(2)}, u32[]{:S(2)}) collective-permute-start(bf16[2,1,128,1024]{3,2,1,0:T(8,128)(2,1)} %get-tuple-element.590), channel_id=1, source_target_pairs={{0,2},{2,0},{4,6},{6,4},{8,10},{10,8},{12,14},{14,12},{16,18},{18,... | collective-permute-start | bytes 1572872 | tf_op jit(solution)/shard_map/ppermute | solution.py:88
  21.6 34.4 %collective-permute-start.50 = (bf16[4,2,1024]{2,1,0:T(2,128)(2,1)S(1)}, bf16[4,2,1024]{2,1,0:T(2,128)(2,1)S(1)}, u32[]{:S(2)}, u32[]{:S(2)}) collective-permute-start(bf16[4,2,1024]{2,1,0:T(2,128)(2,1)S(1)} %collective-permute-done.49), channel_id=1, source_target_pairs={{0,1},{1,0},{2,3},{3,2},{4,5},{5,4},{6,7},{7,6},{8,9},{9,8},{10,11... | collective-permute-start | bytes 49160 | tf_op jit(solution)/shard_map/ppermute | solution.py:57
  26.7 29.3 %collective-permute-start.48 = (bf16[4,128,1024]{2,1,0:T(8,128)(2,1)S(1)}, bf16[4,128,1024]{2,1,0:T(8,128)(2,1)S(1)}, u32[]{:S(2)}, u32[]{:S(2)}) collective-permute-start(bf16[4,128,1024]{2,1,0:T(8,128)(2,1)S(1)} %get-tuple-element.575), channel_id=1, source_target_pairs={{0,1},{1,0},{2,3},{3,2},{4,5},{5,4},{6,7},{7,6},{8,9},{9,8},{10,11... | collective-permute-start | bytes 3145736 | tf_op jit(solution)/shard_map/ppermute | solution.py:57
  29.9 14.9 %collective-permute-start.52 = (bf16[1,2,128,1024]{3,2,1,0:T(8,128)(2,1)S(1)}, bf16[1,2,128,1024]{3,2,1,0:T(8,128)(2,1)S(1)}, u32[]{:S(2)}, u32[]{:S(2)}) collective-permute-start(bf16[1,2,128,1024]{3,2,1,0:T(8,128)(2,1)S(1)} %get-tuple-element.593), channel_id=1, source_target_pairs={{0,4},{2,6},{4,0},{6,2},{8,12},{10,14},{12,8},{14,10},{16,20},{18,... | collective-permute-start | bytes 1572872 | tf_op jit(solution)/shard_map/ppermute | solution.py:88
  31.6 23.3 %collective-permute-start.55 = (bf16[1,2,128,1024]{3,2,1,0:T(8,128)(2,1)S(1)}, bf16[1,2,128,1024]{3,2,1,0:T(8,128)(2,1)S(1)}, u32[]{:S(2)}, u32[]{:S(2)}) collective-permute-start(bf16[1,2,128,1024]{3,2,1,0:T(8,128)(2,1)S(1)} %get-tuple-element.589), channel_id=1, source_target_pairs={{0,4},{2,6},{4,0},{6,2},{8,12},{10,14},{12,8},{14,10},{16,20},{18,... | collective-permute-start | bytes 1572872 | tf_op jit(solution)/shard_map/ppermute | solution.py:88
  57.0 26.4 %collective-permute-start.53 = (bf16[4,128,1024]{2,1,0:T(8,128)(2,1)}, bf16[4,128,1024]{2,1,0:T(8,128)(2,1)}, u32[]{:S(2)}, u32[]{:S(2)}) collective-permute-start(bf16[4,128,1024]{2,1,0:T(8,128)(2,1)} %get-tuple-element.345), channel_id=1, source_target_pairs={{0,1},{1,0},{2,3},{3,2},{4,5},{5,4},{6,7},{7,6},{8,9},{9,8},{10,11... | collective-permute-start | bytes 3145736 | tf_op jit(solution)/shard_map/ppermute | solution.py:57
  77.3 28.2 %collective-permute-start.56 = (bf16[4,128,1024]{2,1,0:T(8,128)(2,1)}, bf16[4,128,1024]{2,1,0:T(8,128)(2,1)}, u32[]{:S(2)}, u32[]{:S(2)}) collective-permute-start(bf16[4,128,1024]{2,1,0:T(8,128)(2,1)} %get-tuple-element.348), channel_id=1, source_target_pairs={{0,1},{1,0},{2,3},{3,2},{4,5},{5,4},{6,7},{7,6},{8,9},{9,8},{10,11... | collective-permute-start | bytes 3145736 | tf_op jit(solution)/shard_map/ppermute | solution.py:57
  107.2 21.8 %collective-permute-start.59 = (bf16[4,128,1024]{2,1,0:T(8,128)(2,1)S(1)}, bf16[4,128,1024]{2,1,0:T(8,128)(2,1)}, u32[]{:S(2)}, u32[]{:S(2)}) collective-permute-start(bf16[4,128,1024]{2,1,0:T(8,128)(2,1)S(1)} %get-tuple-element.353), channel_id=1, source_target_pairs={{0,1},{1,0},{2,3},{3,2},{4,5},{5,4},{6,7},{7,6},{8,9},{9,8},{10,11... | collective-permute-start | bytes 3145736 | tf_op jit(solution)/shard_map/ppermute | solution.py:57
  112.4 18.6 %collective-permute-start.58 = (bf16[1,2,128,1024]{3,2,1,0:T(8,128)(2,1)S(1)}, bf16[1,2,128,1024]{3,2,1,0:T(8,128)(2,1)S(1)}, u32[]{:S(2)}, u32[]{:S(2)}) collective-permute-start(bf16[1,2,128,1024]{3,2,1,0:T(8,128)(2,1)S(1)} %get-tuple-element.585), channel_id=1, source_target_pairs={{0,4},{2,6},{4,0},{6,2},{8,12},{10,14},{12,8},{14,10},{16,20},{18,... | collective-permute-start | bytes 1572872 | tf_op jit(solution)/shard_map/ppermute | solution.py:88
  132.8 40.2 %collective-permute-start.3 = (bf16[512,1024]{1,0:T(8,128)(2,1)}, bf16[512,1024]{1,0:T(8,128)(2,1)}, u32[]{:S(2)}, u32[]{:S(2)}) collective-permute-start(bf16[512,1024]{1,0:T(8,128)(2,1)} %bitcast.rows.refs_2_), channel_id=1, source_target_pairs={{0,1},{1,0},{2,3},{3,2},{4,5},{5,4},{6,7},{7,6},{8,9},{9,8},{10,11... | collective-permute-start | bytes 3145736 | tf_op jit(solution)/shard_map/cond/branch_1_fun/ppermute | solution.py:57
  134.2 46.9 %collective-permute-start.2 = (bf16[512,1024]{1,0:T(8,128)(2,1)}, bf16[512,1024]{1,0:T(8,128)(2,1)}, u32[]{:S(2)}, u32[]{:S(2)}) collective-permute-start(bf16[512,1024]{1,0:T(8,128)(2,1)} %get-tuple-element.160.cot.refs_0_), channel_id=1, source_target_pairs={{0,1},{1,0},{2,3},{3,2},{4,5},{5,4},{6,7},{7,6},{8,9},{9,8},{10,11... | collective-permute-start | bytes 3145736 | tf_op jit(solution)/shard_map/cond/branch_1_fun/ppermute | solution.py:57
  136.0 18.2 %collective-permute-start.1 = (bf16[1,2,128,1024]{3,2,1,0:T(8,128)(2,1)}, bf16[1,2,128,1024]{3,2,1,0:T(8,128)(2,1)}, u32[]{:S(2)}, u32[]{:S(2)}) collective-permute-start(bf16[1,2,128,1024]{3,2,1,0:T(8,128)(2,1)} %get-tuple-element.456), channel_id=1, source_target_pairs={{0,4},{2,6},{4,0},{6,2},{8,12},{10,14},{12,8},{14,10},{16,20},{18,... | collective-permute-start | bytes 1572872 | tf_op jit(solution)/shard_map/cond/branch_1_fun/ppermute | solution.py:88
  199.3 320.6 %reduce-scatter.7.cloned.1.call-start = ((), (), s32[]{:S(2)}) async-start(), calls=%async_computation.5 | async-start | bytes 10813440 | tf_op jit(solution)/shard_map/reduce_scatter | solution.py:574
  201.1 39.1 %collective-permute-start.13 = (bf16[512,1024]{1,0:T(8,128)(2,1)}, bf16[512,1024]{1,0:T(8,128)(2,1)}, u32[]{:S(2)}, u32[]{:S(2)}) collective-permute-start(bf16[512,1024]{1,0:T(8,128)(2,1)} %get-tuple-element.177), channel_id=1, source_target_pairs={{0,1},{1,0},{2,3},{3,2},{4,5},{5,4},{6,7},{7,6},{8,9},{9,8},{10,11... | collective-permute-start | bytes 3145736 | tf_op jit(solution)/shard_map/cond/branch_1_fun/ppermute | solution.py:57
  202.5 47.5 %collective-permute-start.14 = (bf16[512,1024]{1,0:T(8,128)(2,1)}, bf16[512,1024]{1,0:T(8,128)(2,1)}, u32[]{:S(2)}, u32[]{:S(2)}) collective-permute-start(bf16[512,1024]{1,0:T(8,128)(2,1)} %get-tuple-element.179), channel_id=1, source_target_pairs={{0,1},{1,0},{2,3},{3,2},{4,5},{5,4},{6,7},{7,6},{8,9},{9,8},{10,11... | collective-permute-start | bytes 3145736 | tf_op jit(solution)/shard_map/cond/branch_1_fun/ppermute | solution.py:57
  205.4 27.3 %collective-permute-start.16 = (bf16[2,1,2,128,1024]{4,3,1,2,0:T(8,128)(2,1)}, bf16[2,1,2,128,1024]{4,3,1,2,0:T(8,128)(2,1)}, u32[]{:S(2)}, u32[]{:S(2)}) collective-permute-start(bf16[2,1,2,128,1024]{4,3,1,2,0:T(8,128)(2,1)} %bitcast.472), channel_id=1, source_target_pairs={{0,2},{2,0},{4,6},{6,4},{8,10},{10,8},{12,14},{14,12},{16,18},{18,... | collective-permute-start | bytes 3145736 | tf_op jit(solution)/shard_map/cond/branch_1_fun/ppermute | solution.py:88
  208.9 28.1 %collective-permute-start.18 = (bf16[2,1,2,128,1024]{4,3,1,2,0:T(8,128)(2,1)}, bf16[2,1,2,128,1024]{4,3,1,2,0:T(8,128)(2,1)}, u32[]{:S(2)}, u32[]{:S(2)}) collective-permute-start(bf16[2,1,2,128,1024]{4,3,1,2,0:T(8,128)(2,1)} %bitcast.470), channel_id=1, source_target_pairs={{0,2},{2,0},{4,6},{6,4},{8,10},{10,8},{12,14},{14,12},{16,18},{18,... | collective-permute-start | bytes 3145736 | tf_op jit(solution)/shard_map/cond/branch_1_fun/ppermute | solution.py:88
  225.8 66.9 %collective-permute-start.15 = (bf16[512,1024]{1,0:T(8,128)(2,1)}, bf16[512,1024]{1,0:T(8,128)(2,1)}, u32[]{:S(2)}, u32[]{:S(2)}) collective-permute-start(bf16[512,1024]{1,0:T(8,128)(2,1)} %get-tuple-element.196), channel_id=1, source_target_pairs={{0,1},{1,0},{2,3},{3,2},{4,5},{5,4},{6,7},{7,6},{8,9},{9,8},{10,11... | collective-permute-start | bytes 3145736 | tf_op jit(solution)/shard_map/cond/branch_1_fun/ppermute | solution.py:57
  235.4 51.7 %collective-permute-start.17 = (bf16[1,2,2,128,1024]{4,3,1,2,0:T(8,128)(2,1)}, bf16[1,2,2,128,1024]{4,3,1,2,0:T(8,128)(2,1)}, u32[]{:S(2)}, u32[]{:S(2)}) collective-permute-start(bf16[1,2,2,128,1024]{4,3,1,2,0:T(8,128)(2,1)} %get-tuple-element.552), channel_id=1, source_target_pairs={{0,4},{2,6},{4,0},{6,2},{8,12},{10,14},{12,8},{14,10},{16,20},{18,... | collective-permute-start | bytes 3145736 | tf_op jit(solution)/shard_map/cond/branch_1_fun/ppermute | solution.py:88
  239.6 50.3 %collective-permute-start.19 = (bf16[1,2,2,128,1024]{4,3,1,2,0:T(8,128)(2,1)}, bf16[1,2,2,128,1024]{4,3,1,2,0:T(8,128)(2,1)}, u32[]{:S(2)}, u32[]{:S(2)}) collective-permute-start(bf16[1,2,2,128,1024]{4,3,1,2,0:T(8,128)(2,1)} %get-tuple-element.548), channel_id=1, source_target_pairs={{0,4},{2,6},{4,0},{6,2},{8,12},{10,14},{12,8},{14,10},{16,20},{18,... | collective-permute-start | bytes 3145736 | tf_op jit(solution)/shard_map/cond/branch_1_fun/ppermute | solution.py:88
  266.4 27.2 %collective-permute-start.22 = (bf16[512,1024]{1,0:T(8,128)(2,1)}, bf16[512,1024]{1,0:T(8,128)(2,1)}, u32[]{:S(2)}, u32[]{:S(2)}) collective-permute-start(bf16[512,1024]{1,0:T(8,128)(2,1)} %get-tuple-element.204), channel_id=1, source_target_pairs={{0,1},{1,0},{2,3},{3,2},{4,5},{5,4},{6,7},{7,6},{8,9},{9,8},{10,11... | collective-permute-start | bytes 3145736 | tf_op jit(solution)/shard_map/cond/branch_1_fun/ppermute | solution.py:57
  295.9 14.9 %collective-permute-start.23 = (bf16[2,1,128,1024]{3,2,1,0:T(8,128)(2,1)S(1)}, bf16[2,1,128,1024]{3,2,1,0:T(8,128)(2,1)S(1)}, u32[]{:S(2)}, u32[]{:S(2)}) collective-permute-start(bf16[2,1,128,1024]{3,2,1,0:T(8,128)(2,1)S(1)} %pad_maximum_fusion.6), channel_id=1, source_target_pairs={{0,4},{2,6},{4,0},{6,2},{8,12},{10,14},{12,8},{14,10},{16,20},{18,... | collective-permute-start | bytes 1572872 | tf_op jit(solution)/shard_map/cond/branch_1_fun/ppermute | solution.py:99
  299.9 19.9 %collective-permute-start.20 = (bf16[2,1,128,1024]{3,2,1,0:T(8,128)(2,1)S(1)}, bf16[2,1,128,1024]{3,2,1,0:T(8,128)(2,1)S(1)}, u32[]{:S(2)}, u32[]{:S(2)}) collective-permute-start(bf16[2,1,128,1024]{3,2,1,0:T(8,128)(2,1)S(1)} %pad_maximum_fusion.5), channel_id=1, source_target_pairs={{0,4},{2,6},{4,0},{6,2},{8,12},{10,14},{12,8},{14,10},{16,20},{18,... | collective-permute-start | bytes 1572872 | tf_op jit(solution)/shard_map/cond/branch_1_fun/ppermute | solution.py:99
  311.0 9.0 %collective-permute-start.24 = (bf16[1,2,128,1024]{3,2,1,0:T(8,128)(2,1)S(1)}, bf16[1,2,128,1024]{3,2,1,0:T(8,128)(2,1)S(1)}, u32[]{:S(2)}, u32[]{:S(2)}) collective-permute-start(bf16[1,2,128,1024]{3,2,1,0:T(8,128)(2,1)S(1)} %maximum_bitcast_fusion.1), channel_id=1, source_target_pairs={{0,2},{2,0},{4,6},{6,4},{8,10},{10,8},{12,14},{14,12},{16,18},{18,... | collective-permute-start | bytes 1572872 | tf_op jit(solution)/shard_map/cond/branch_1_fun/ppermute | solution.py:99
  328.3 25.8 %collective-permute-start.25 = (bf16[4,128,1024]{2,1,0:T(8,128)(2,1)}, bf16[4,128,1024]{2,1,0:T(8,128)(2,1)}, u32[]{:S(2)}, u32[]{:S(2)}) collective-permute-start(bf16[4,128,1024]{2,1,0:T(8,128)(2,1)} %get-tuple-element.644), channel_id=1, source_target_pairs={{0,1},{1,0},{2,3},{3,2},{4,5},{5,4},{6,7},{7,6},{8,9},{9,8},{10,11... | collective-permute-start | bytes 3145736 | tf_op jit(solution)/shard_map/cond/branch_1_fun/ppermute | solution.py:57
  354.4 339.0 %reduce-scatter.9.cloned.1.call-start = ((), (), s32[]{:S(2)}) async-start(), calls=%async_computation.6 | async-start | bytes 7864320 | tf_op jit(solution)/shard_map/reduce_scatter | solution.py:574
  358.3 2.9 collective-permute-start.7
  358.3 34.0 %collective-permute-start.6 = (bf16[4,128,1024]{2,1,0:T(8,128)(2,1)}, bf16[4,128,1024]{2,1,0:T(8,128)(2,1)}, u32[]{:S(2)}, u32[]{:S(2)}) collective-permute-start(bf16[4,128,1024]{2,1,0:T(8,128)(2,1)} %get-tuple-element.225.own), channel_id=1, source_target_pairs={{0,1},{1,0},{2,3},{3,2},{4,5},{5,4},{6,7},{7,6},{8,9},{9,8},{10,11... | collective-permute-start | bytes 3145736 | tf_op jit(solution)/shard_map/cond/branch_1_fun/ppermute | solution.py:57
  362.8 29.5 %collective-permute-start.8 = (bf16[1,2,3,64,1408]{4,3,2,1,0:T(8,128)(2,1)}, bf16[1,2,3,64,1408]{4,3,2,1,0:T(8,128)(2,1)}, u32[]{:S(2)}, u32[]{:S(2)}) collective-permute-start(bf16[1,2,3,64,1408]{4,3,2,1,0:T(8,128)(2,1)} %get-tuple-element.472), channel_id=1, source_target_pairs={{0,4},{2,6},{4,0},{6,2},{8,12},{10,14},{12,8},{14,10},{16,20},{18,... | collective-permute-start | bytes 3244040 | tf_op jit(solution)/shard_map/cond/branch_1_fun/ppermute | solution.py:88
  392.3 31.8 %collective-permute-start.4 = (bf16[2,1,2,3,128,512]{5,4,1,3,2,0:T(8,128)(2,1)}, bf16[2,1,2,3,128,512]{5,4,1,3,2,0:T(8,128)(2,1)}, u32[]{:S(2)}, u32[]{:S(2)}) collective-permute-start(bf16[2,1,2,3,128,512]{5,4,1,3,2,0:T(8,128)(2,1)} %bitcast.468), channel_id=1, source_target_pairs={{0,2},{2,0},{4,6},{6,4},{8,10},{10,8},{12,14},{14,12},{16,18},{18,... | collective-permute-start | bytes 4718600 | tf_op jit(solution)/shard_map/cond/branch_1_fun/ppermute | solution.py:88
  422.6 4.6 collective-permute-start.9
  425.8 37.3 %collective-permute-start.5 = (bf16[1,2,2,3,128,512]{5,4,1,3,2,0:T(8,128)(2,1)S(1)}, bf16[1,2,2,3,128,512]{5,4,1,3,2,0:T(8,128)(2,1)S(1)}, u32[]{:S(2)}, u32[]{:S(2)}) collective-permute-start(bf16[1,2,2,3,128,512]{5,4,1,3,2,0:T(8,128)(2,1)S(1)} %get-tuple-element.464), channel_id=1, source_target_pairs={{0,4},{2,6},{4,0},{6,2},{8,12},{10,14},{12,8},{14,10},{16,20},{18,... | collective-permute-start | bytes 4718600 | tf_op jit(solution)/shard_map/cond/branch_1_fun/ppermute | solution.py:88
  427.5 68.6 %collective-permute-start.10 = (bf16[1,2,2,3,128,512]{5,4,1,3,2,0:T(8,128)(2,1)S(1)}, bf16[1,2,2,3,128,512]{5,4,1,3,2,0:T(8,128)(2,1)S(1)}, u32[]{:S(2)}, u32[]{:S(2)}) collective-permute-start(bf16[1,2,2,3,128,512]{5,4,1,3,2,0:T(8,128)(2,1)S(1)} %get-tuple-element.460), channel_id=1, source_target_pairs={{0,4},{2,6},{4,0},{6,2},{8,12},{10,14},{12,8},{14,10},{16,20},{18,... | collective-permute-start | bytes 4718600 | tf_op jit(solution)/shard_map/cond/branch_1_fun/ppermute | solution.py:88
  428.3 69.7 %collective-permute-start.11 = (bf16[512,1024]{1,0:T(8,128)(2,1)}, bf16[512,1024]{1,0:T(8,128)(2,1)}, u32[]{:S(2)}, u32[]{:S(2)}) collective-permute-start(bf16[512,1024]{1,0:T(8,128)(2,1)} %get-tuple-element.230), channel_id=1, source_target_pairs={{0,1},{1,0},{2,3},{3,2},{4,5},{5,4},{6,7},{7,6},{8,9},{9,8},{10,11... | collective-permute-start | bytes 3145736 | tf_op jit(solution)/shard_map/cond/branch_1_fun/ppermute | solution.py:57
  429.6 68.5 %collective-permute-start.12 = (bf16[512,1024]{1,0:T(8,128)(2,1)}, bf16[512,1024]{1,0:T(8,128)(2,1)}, u32[]{:S(2)}, u32[]{:S(2)}) collective-permute-start(bf16[512,1024]{1,0:T(8,128)(2,1)} %get-tuple-element.231), channel_id=1, source_target_pairs={{0,1},{1,0},{2,3},{3,2},{4,5},{5,4},{6,7},{7,6},{8,9},{9,8},{10,11... | collective-permute-start | bytes 3145736 | tf_op jit(solution)/shard_map/cond/branch_1_fun/ppermute | solution.py:57
  519.9 217.4 %reduce-scatter.11.cloned.1.call-start = ((), (), s32[]{:S(2)}) async-start(), calls=%async_computation.7 | async-start | bytes 2621440 | tf_op jit(solution)/shard_map/reduce_scatter | solution.py:574
  525.9 31.1 %collective-permute-start.36 = (bf16[2,1,128,1024]{3,2,1,0:T(8,128)(2,1)}, bf16[2,1,128,1024]{3,2,1,0:T(8,128)(2,1)}, u32[]{:S(2)}, u32[]{:S(2)}) collective-permute-start(bf16[2,1,128,1024]{3,2,1,0:T(8,128)(2,1)} %pad_maximum_fusion.18), channel_id=1, source_target_pairs={{0,4},{2,6},{4,0},{6,2},{8,12},{10,14},{12,8},{14,10},{16,20},{18,... | collective-permute-start | bytes 1572872 | tf_op jit(solution)/shard_map/cond/branch_1_fun/ppermute | solution.py:99
  531.2 27.8 %collective-permute-start.38 = (bf16[2,1,128,1024]{3,2,1,0:T(8,128)(2,1)}, bf16[2,1,128,1024]{3,2,1,0:T(8,128)(2,1)}, u32[]{:S(2)}, u32[]{:S(2)}) collective-permute-start(bf16[2,1,128,1024]{3,2,1,0:T(8,128)(2,1)} %pad_maximum_fusion.19), channel_id=1, source_target_pairs={{0,4},{2,6},{4,0},{6,2},{8,12},{10,14},{12,8},{14,10},{16,20},{18,... | collective-permute-start | bytes 1572872 | tf_op jit(solution)/shard_map/cond/branch_1_fun/ppermute | solution.py:99
  535.5 25.1 %collective-permute-start.30 = (bf16[2,1,2,128,512]{4,3,1,2,0:T(8,128)(2,1)}, bf16[2,1,2,128,512]{4,3,1,2,0:T(8,128)(2,1)}, u32[]{:S(2)}, u32[]{:S(2)}) collective-permute-start(bf16[2,1,2,128,512]{4,3,1,2,0:T(8,128)(2,1)} %bitcast.480), channel_id=1, source_target_pairs={{0,2},{2,0},{4,6},{6,4},{8,10},{10,8},{12,14},{14,12},{16,18},{18,... | collective-permute-start | bytes 1572872 | tf_op jit(solution)/shard_map/cond/branch_1_fun/ppermute | solution.py:88
  535.5 28.9 %collective-permute-start.40 = (bf16[4,128,1024]{2,1,0:T(8,128)(2,1)}, bf16[4,128,1024]{2,1,0:T(8,128)(2,1)}, u32[]{:S(2)}, u32[]{:S(2)}) collective-permute-start(bf16[4,128,1024]{2,1,0:T(8,128)(2,1)} %get-tuple-element.263), channel_id=1, source_target_pairs={{0,1},{1,0},{2,3},{3,2},{4,5},{5,4},{6,7},{7,6},{8,9},{9,8},{10,11... | collective-permute-start | bytes 3145736 | tf_op jit(solution)/shard_map/cond/branch_1_fun/ppermute | solution.py:57
  536.8 47.1 %collective-permute-start.41 = (bf16[4,128,1024]{2,1,0:T(8,128)(2,1)}, bf16[4,128,1024]{2,1,0:T(8,128)(2,1)}, u32[]{:S(2)}, u32[]{:S(2)}) collective-permute-start(bf16[4,128,1024]{2,1,0:T(8,128)(2,1)} %get-tuple-element.267), channel_id=1, source_target_pairs={{0,1},{1,0},{2,3},{3,2},{4,5},{5,4},{6,7},{7,6},{8,9},{9,8},{10,11... | collective-permute-start | bytes 3145736 | tf_op jit(solution)/shard_map/cond/branch_1_fun/ppermute | solution.py:57
  557.0 6.0 collective-permute-start.32
  559.0 42.7 %collective-permute-start.28 = (bf16[2,1,2,128,1024]{4,3,1,2,0:T(8,128)(2,1)}, bf16[2,1,2,128,1024]{4,3,1,2,0:T(8,128)(2,1)S(1)}, u32[]{:S(2)}, u32[]{:S(2)}) collective-permute-start(bf16[2,1,2,128,1024]{4,3,1,2,0:T(8,128)(2,1)} %bitcast.525), channel_id=1, source_target_pairs={{0,2},{2,0},{4,6},{6,4},{8,10},{10,8},{12,14},{14,12},{16,18},{18,... | collective-permute-start | bytes 3145736 | tf_op jit(solution)/shard_map/cond/branch_1_fun/ppermute | solution.py:88
  560.6 52.8 %collective-permute-start.26 = (bf16[2,1,2,128,1024]{4,3,1,2,0:T(8,128)(2,1)}, bf16[2,1,2,128,1024]{4,3,1,2,0:T(8,128)(2,1)}, u32[]{:S(2)}, u32[]{:S(2)}) collective-permute-start(bf16[2,1,2,128,1024]{4,3,1,2,0:T(8,128)(2,1)} %bitcast.476), channel_id=1, source_target_pairs={{0,2},{2,0},{4,6},{6,4},{8,10},{10,8},{12,14},{14,12},{16,18},{18,... | collective-permute-start | bytes 3145736 | tf_op jit(solution)/shard_map/cond/branch_1_fun/ppermute | solution.py:88
  563.0 81.8 %collective-permute-start.34 = (bf16[2,1,3,64,1408]{4,3,2,1,0:T(8,128)(2,1)}, bf16[2,1,3,64,1408]{4,3,2,1,0:T(8,128)(2,1)}, u32[]{:S(2)}, u32[]{:S(2)}) collective-permute-start(bf16[2,1,3,64,1408]{4,3,2,1,0:T(8,128)(2,1)} %get-tuple-element.481), channel_id=1, source_target_pairs={{0,2},{2,0},{4,6},{6,4},{8,10},{10,8},{12,14},{14,12},{16,18},{18,... | collective-permute-start | bytes 3244040 | tf_op jit(solution)/shard_map/cond/branch_1_fun/ppermute | solution.py:88
  564.5 28.6 %collective-permute-start.37 = (bf16[1,2,128,1024]{3,2,1,0:T(8,128)(2,1)S(1)}, bf16[1,2,128,1024]{3,2,1,0:T(8,128)(2,1)S(1)}, u32[]{:S(2)}, u32[]{:S(2)}) collective-permute-start(bf16[1,2,128,1024]{3,2,1,0:T(8,128)(2,1)S(1)} %maximum_bitcast_fusion.2), channel_id=1, source_target_pairs={{0,2},{2,0},{4,6},{6,4},{8,10},{10,8},{12,14},{14,12},{16,18},{18,... | collective-permute-start | bytes 1572872 | tf_op jit(solution)/shard_map/cond/branch_1_fun/ppermute | solution.py:99
  583.9 11.5 %collective-permute-start.39 = (bf16[1,2,128,1024]{3,2,1,0:T(8,128)(2,1)S(1)}, bf16[1,2,128,1024]{3,2,1,0:T(8,128)(2,1)S(1)}, u32[]{:S(2)}, u32[]{:S(2)}) collective-permute-start(bf16[1,2,128,1024]{3,2,1,0:T(8,128)(2,1)S(1)} %maximum_bitcast_fusion.3), channel_id=1, source_target_pairs={{0,2},{2,0},{4,6},{6,4},{8,10},{10,8},{12,14},{14,12},{16,18},{18,... | collective-permute-start | bytes 1572872 | tf_op jit(solution)/shard_map/cond/branch_1_fun/ppermute | solution.py:99
  593.1 28.4 %collective-permute-start.31 = (bf16[1,2,2,128,512]{4,3,1,2,0:T(8,128)(2,1)}, bf16[1,2,2,128,512]{4,3,1,2,0:T(8,128)(2,1)}, u32[]{:S(2)}, u32[]{:S(2)}) collective-permute-start(bf16[1,2,2,128,512]{4,3,1,2,0:T(8,128)(2,1)} %get-tuple-element.514), channel_id=1, source_target_pairs={{0,4},{2,6},{4,0},{6,2},{8,12},{10,14},{12,8},{14,10},{16,20},{18,... | collective-permute-start | bytes 1572872 | tf_op jit(solution)/shard_map/cond/branch_1_fun/ppermute | solution.py:88
  595.4 47.3 %collective-permute-start.33 = (bf16[1,2,2,128,512]{4,3,1,2,0:T(8,128)(2,1)}, bf16[1,2,2,128,512]{4,3,1,2,0:T(8,128)(2,1)}, u32[]{:S(2)}, u32[]{:S(2)}) collective-permute-start(bf16[1,2,2,128,512]{4,3,1,2,0:T(8,128)(2,1)} %get-tuple-element.510), channel_id=1, source_target_pairs={{0,4},{2,6},{4,0},{6,2},{8,12},{10,14},{12,8},{14,10},{16,20},{18,... | collective-permute-start | bytes 1572872 | tf_op jit(solution)/shard_map/cond/branch_1_fun/ppermute | solution.py:88
  601.7 9.5 %collective-permute-start.43 = (f32[2,4,512]{2,1,0:T(4,128)S(1)}, f32[2,4,512]{2,1,0:T(4,128)S(1)}, u32[]{:S(2)}, u32[]{:S(2)}) collective-permute-start(f32[2,4,512]{2,1,0:T(4,128)S(1)} %select_bitcast_fusion.8), channel_id=1, source_target_pairs={{0,16},{2,18},{4,20},{6,22},{8,24},{10,26},{12,28},{14,30},{16,0},... | collective-permute-start | bytes 49160 | tf_op jit(solution)/shard_map/cond/branch_1_fun/ppermute | solution.py:125
  611.2 40.9 %collective-permute-start.29 = (bf16[1,2,2,128,1024]{4,3,1,2,0:T(8,128)(2,1)}, bf16[1,2,2,128,1024]{4,3,1,2,0:T(8,128)(2,1)}, u32[]{:S(2)}, u32[]{:S(2)}) collective-permute-start(bf16[1,2,2,128,1024]{4,3,1,2,0:T(8,128)(2,1)} %get-tuple-element.492), channel_id=1, source_target_pairs={{0,4},{2,6},{4,0},{6,2},{8,12},{10,14},{12,8},{14,10},{16,20},{18,... | collective-permute-start | bytes 3145736 | tf_op jit(solution)/shard_map/cond/branch_1_fun/ppermute | solution.py:88
  613.4 6.5 collective-permute-start.44
  619.9 29.2 %collective-permute-start.42 = (f32[4,2,1024]{2,1,0:T(2,128)S(1)}, f32[4,2,1024]{2,1,0:T(2,128)S(1)}, u32[]{:S(2)}, u32[]{:S(2)}) collective-permute-start(f32[4,2,1024]{2,1,0:T(2,128)S(1)} %slice_select_fusion), channel_id=1, source_target_pairs={{2,0},{4,2},{6,4},{8,6},{10,8},{12,10},{14,12},{16,14},{18,16},{20... | collective-permute-start | bytes 98312 | tf_op jit(solution)/shard_map/cond/branch_1_fun/ppermute | solution.py:26
  621.5 20.4 %collective-permute-start.45 = (f32[2,4,128]{2,1,0:T(4,128)S(1)}, f32[2,4,128]{2,1,0:T(4,128)S(1)}, u32[]{:S(2)}, u32[]{:S(2)}) collective-permute-start(f32[2,4,128]{2,1,0:T(4,128)S(1)} %select_bitcast_fusion.9), channel_id=1, source_target_pairs={{0,4},{2,6},{4,0},{6,2},{8,12},{10,14},{12,8},{14,10},{16,20},{18,... | collective-permute-start | bytes 12296 | tf_op jit(solution)/shard_map/cond/branch_1_fun/ppermute | solution.py:125
  641.9 26.4 %collective-permute-start.27 = (bf16[1,2,2,128,1024]{4,3,1,2,0:T(8,128)(2,1)}, bf16[1,2,2,128,1024]{4,3,1,2,0:T(8,128)(2,1)}, u32[]{:S(2)}, u32[]{:S(2)}) collective-permute-start(bf16[1,2,2,128,1024]{4,3,1,2,0:T(8,128)(2,1)} %get-tuple-element.498), channel_id=1, source_target_pairs={{0,4},{2,6},{4,0},{6,2},{8,12},{10,14},{12,8},{14,10},{16,20},{18,... | collective-permute-start | bytes 3145736 | tf_op jit(solution)/shard_map/cond/branch_1_fun/ppermute | solution.py:88
  647.7 42.2 %collective-permute-start.35 = (bf16[1,2,3,64,1408]{4,3,2,1,0:T(8,128)(2,1)}, bf16[1,2,3,64,1408]{4,3,2,1,0:T(8,128)(2,1)}, u32[]{:S(2)}, u32[]{:S(2)}) collective-permute-start(bf16[1,2,3,64,1408]{4,3,2,1,0:T(8,128)(2,1)} %get-tuple-element.480), channel_id=1, source_target_pairs={{0,4},{2,6},{4,0},{6,2},{8,12},{10,14},{12,8},{14,10},{16,20},{18,... | collective-permute-start | bytes 3244040 | tf_op jit(solution)/shard_map/cond/branch_1_fun/ppermute | solution.py:88
  695.1 7.6 collective-permute-start.60
  702.9 47.0 %collective-permute-start.61 = (bf16[1,2,2,3,64,512]{5,4,3,2,1,0:T(8,128)(2,1)S(1)}, bf16[1,2,2,3,64,512]{5,4,3,2,1,0:T(8,128)(2,1)S(1)}, u32[]{:S(2)}, u32[]{:S(2)}) collective-permute-start(bf16[1,2,2,3,64,512]{5,4,3,2,1,0:T(8,128)(2,1)S(1)} %get-tuple-element.581), channel_id=1, source_target_pairs={{0,4},{2,6},{4,0},{6,2},{8,12},{10,14},{12,8},{14,10},{16,20},{18,... | collective-permute-start | bytes 2359304 | tf_op jit(solution)/shard_map/ppermute | solution.py:88
  738.5 9.7 %collective-permute-start.62 = (bf16[2,1,2,1,64,512]{5,4,2,3,1,0:T(8,128)(2,1)S(1)}, bf16[2,1,2,1,64,512]{5,4,2,3,1,0:T(8,128)(2,1)S(1)}, u32[]{:S(2)}, u32[]{:S(2)}) collective-permute-start(bf16[2,1,2,1,64,512]{5,4,2,3,1,0:T(8,128)(2,1)S(1)} %bitcast.531), channel_id=1, source_target_pairs={{0,2},{2,0},{4,6},{6,4},{8,10},{10,8},{12,14},{14,12},{16,18},{18,... | collective-permute-start | bytes 786440 | tf_op jit(solution)/shard_map/ppermute | solution.py:88
  748.3 8.8 %collective-permute-start.63 = (bf16[1,2,2,1,64,512]{5,4,2,3,1,0:T(8,128)(2,1)S(1)}, bf16[1,2,2,1,64,512]{5,4,2,3,1,0:T(8,128)(2,1)S(1)}, u32[]{:S(2)}, u32[]{:S(2)}) collective-permute-start(bf16[1,2,2,1,64,512]{5,4,2,3,1,0:T(8,128)(2,1)S(1)} %get-tuple-element.601), channel_id=1, source_target_pairs={{0,4},{2,6},{4,0},{6,2},{8,12},{10,14},{12,8},{14,10},{16,20},{18,... | collective-permute-start | bytes 786440 | tf_op jit(solution)/shard_map/ppermute | solution.py:88
  (80 other events, 610.0 us)
Sparse Core Ops, SparseCore 0:
  199.4 148.8 reduce-scatter.4
  354.6 148.8 reduce-scatter.6
  520.1 111.5 reduce-scatter.8
  693.6 43.7 reduce-scatter.10

commit v3 on v2

--- a/solution.py
+++ b/solution.py
@@ -47,7 +47,6 @@
         self.outer = self.dp // self.size
         self.member = lax.axis_index("dp") % self.size
         self.m = lax.axis_index("mp")
-        self.given = self.sent = None
         self.pair = self.mp == 2
 
     def index(self, r):
@@ -79,31 +78,47 @@
     def route(self, step):
         return [(i, i ^ step) for i in range(self.dp)]
 
-    def spread(self, blocks, after=None):
+    def begin(self, blocks):
         held, bit = blocks[:, None], 1
         while bit < self.size:
             halves = held.reshape((held.shape[0] // 2, 2) + held.shape[1:])
             side = jnp.where((self.member & bit) != 0, 1, 0)
-            self.given = at(halves, 1 - side, 1)
-            got = lax.ppermute(self.given, "dp", self.route(bit))
+            keep, give = at(halves, side, 1), at(halves, 1 - side, 1)
+            if 2 * bit == self.size:
+                return keep, give
+            held = jnp.concatenate([keep, lax.ppermute(give, "dp", self.route(bit))], axis=1)
             bit *= 2
-            if after is not None and bit == self.size:
-                got = tied(after, got)[0]
-            held = jnp.concatenate([at(halves, side, 1), got], axis=1)
-        return held[0]
-
-    def unspread(self, blocks, after=None):
-        held, bit = [blocks[s][None] for s in range(self.size)], self.size // 2
-        self.sent = jnp.stack(held[bit:])
+        return held, None
+
+    def end(self, keep, give):
+        if give is None:
+            return keep[0]
+        return jnp.concatenate([keep, lax.ppermute(give, "dp", self.route(self.size // 2))], axis=1)[0]
+
+    def spread(self, blocks):
+        return self.end(*self.begin(blocks))
+
+    def begin_back(self, blocks):
+        held, half = [blocks[s][None] for s in range(self.size)], self.size // 2
+        return held, jnp.stack(held[half:]) if half else None
+
+    def first_back(self, give):
+        return give if give is None else lax.ppermute(give, "dp", self.route(self.size // 2))
+
+    def end_back(self, held, got):
+        bit = self.size // 2
         while bit:
-            got = lax.ppermute(jnp.stack(held[bit:]), "dp", self.route(bit))
-            if after is not None:
-                got, after = tied(after, got)[0], None
-            held = [jnp.concatenate([held[s], got[s]]) for s in range(bit)]
+            if got is None:
+                got = lax.ppermute(jnp.stack(held[bit:]), "dp", self.route(bit))
+            held, got = [jnp.concatenate([held[s], got[s]]) for s in range(bit)], None
             bit //= 2
         bits = self.size.bit_length() - 1
         turn = [int(format(s, "b").zfill(bits)[::-1] or "0", 2) for s in range(self.size)]
         return self.in_order([held[0][turn[s]] for s in range(self.size)])
+
+    def unspread(self, blocks):
+        held, give = self.begin_back(blocks)
+        return self.end_back(held, self.first_back(give))
 
     def in_order(self, blocks):
         bit = 1
@@ -174,8 +189,7 @@
     normed_ref[0] = normed
     parts = []
     for c in range(3):
-        wide = turned(dot(normed, w_qkv[0, c], (1, 0)), heads)
-        low = wide.astype(BF16)
+        low = turned(dot(normed, w_qkv[0, c], (1, 0)).astype(BF16), heads)
         qkv_ref[0, c] = low
         parts.append(low.astype(F32))
     query = parts[0] * 0.125
@@ -198,7 +212,7 @@
         return carry
 
     lax.fori_loop(0, p + 1, mix, 0)
-    context = total[...].reshape(heads * HD, -1).T.astype(BF16)
+    context = total[...].astype(BF16).reshape(heads * HD, -1).T
     context_ref[0] = context
     part = dot(context, w_out[0], (1, 1))
 
@@ -273,8 +287,7 @@
 
     is_own = (p >= info[0]) & (p < info[0] + held)
     rows = jnp.where(is_own, own[0].astype(F32), other[0].astype(F32)).astype(BF16)
-    d_context = dot(rows, w_out[0], (1, 0)).astype(BF16).astype(F32)
-    d_context = turned(d_context, heads)
+    d_context = turned(dot(rows, w_out[0], (1, 0)).astype(BF16), heads).astype(F32)
     d_scores[...] = jnp.zeros_like(d_scores)
 
     def weigh(j, carry):
@@ -299,7 +312,7 @@
     lax.fori_loop(0, p + 1, back, 0)
     part = 0.0
     for c, grad in enumerate((d_query[...], d_keys[p], d_values[p])):
-        low = grad.reshape(heads * HD, -1).T.astype(BF16)
+        low = grad.astype(BF16).reshape(heads * HD, -1).T
         d_qkv_ref[0, c] = low
         part = part + dot(low, w_qkv[0, c], (1, 1))
 
@@ -519,6 +532,9 @@
         return delayed(lags, blocks[c - 1][:, part - 2 :] if c else earlier, blocks[c], c)
 
     own_blocks = [frames_in[:, c * part : (c + 1) * part] for c in range(chunks)]
+    rows = size * part
+    *own_blocks, late_cotangent = lax.optimization_barrier((*own_blocks, cotangent))
+    cot_chunks = [late_cotangent[:, c * part : (c + 1) * part] for c in range(chunks)]
     earlier = shift_frames(frames_in[:, frames - 2 :, :], 1)
     resid = [delayed_chunk(delays, earlier, own_blocks, c) for c in range(chunks)]
     if pair:
@@ -543,13 +559,15 @@
         dummy = jnp.zeros((1, frames, width), BF16)
     gains = gains[:, None, :]
 
-    rows = size * part
-    cot_chunks = [cotangent[:, c * part : (c + 1) * part] for c in range(chunks)]
-    def by_position(v, after=None):
-        blocks = v.reshape((mp, size) + v.shape[1:])
-        got = group.spread(jnp.moveaxis(blocks, 1, 0), after)
-        got = jnp.moveaxis(got, 0, -3)
-        return got.reshape(got.shape[:-3] + (rows, v.shape[-1]))
+    def begin_position(v):
+        return group.begin(jnp.moveaxis(v.reshape((mp, size) + v.shape[1:]), 1, 0))
+
+    def end_position(keep, give):
+        got = jnp.moveaxis(group.end(keep, give), 0, -3)
+        return got.reshape(got.shape[:-3] + (rows, got.shape[-1]))
+
+    def by_position(v):
+        return end_position(*begin_position(v))
 
     normed_all, qkv, probs, context, attn_parts = [], [], [], [], []
     cot_own = [group.spread(chunk).reshape(rows, width) for chunk in cot_chunks]
@@ -592,23 +610,30 @@
         if pair and c == chunks - 1:
             last_normed_f = normed_f
             break
-        ffn_own.append(group.spread(normed_f).reshape(rows, width))
-        given = group.given
-    def feed(r, step, x_rows, g_rows):
+        keep, given = group.begin(normed_f)
+        ffn_own.append(group.end(keep, given).reshape(rows, width))
+    def feed(r, step, x_rows, g_rows, beside=()):
         position = jnp.asarray(group.index(r) * size + group.member, jnp.int32)
         kind = F32 if r == 0 or not pair else BF16
-        results = []
+        results, moved = [], []
         for c in range(chunks):
             xs, gs = tied(step, x_rows[c], g_rows[c])
-            results.append(ffn(position, xs, gs, w_gate_up, w_down, kind))
-            step = results[-1][0]
-        return [list(v) for v in zip(*results, strict=True)]
+            if beside:
+                keep, give = begin_position(beside[c])
+                xs, give = lax.optimization_barrier((xs, give))
+                moved.append(end_position(keep, give))
+            result = ffn(position, xs, gs, w_gate_up, w_down, kind)
+            step = result[0]
+            if beside:
+                step, moved[c] = lax.optimization_barrier((step, moved[c]))
+                result = (step, *result[1:])
+            results.append(result)
+        return [list(v) for v in zip(*results, strict=True)], moved
 
     blocks_of = lambda d_rows: d_rows.astype(BF16).reshape(size, part, width)
 
-    def back_to_positions(d_rows, c, after=None):
-        d_normed_f = group.unspread(d_rows, after).astype(F32)
-        middle_grad, gain_part = norm_back(middle[c], ffn_gain, d_normed_f)
+    def back_to_positions(d_normed_f, c):
+        middle_grad, gain_part = norm_back(middle[c], ffn_gain, d_normed_f.astype(F32))
         return cot_chunks[c].astype(F32) + middle_grad, gain_part
 
     ffn_sums = []
@@ -617,7 +642,7 @@
         def own_positions(x_rows, last, g_rows):
             last = group.spread(last).reshape(rows, width)
             swapped = [group.swap(g_rows[0]), group.swap(x_rows)]
-            hidden, d_gate_up, d_own, out_own = feed(0, x_rows, [x_rows, last], g_rows)
+            (hidden, d_gate_up, d_own, out_own), _ = feed(0, x_rows, [x_rows, last], g_rows)
             hidden[1], *swapped = lax.optimization_barrier((hidden[1], *swapped))
             grad = ffn_grad(g_rows, [x_rows, last], hidden, d_gate_up, outer)
             return grad, last, swapped, d_own, out_own
@@ -627,24 +652,26 @@
         )
         ffn_sums.append(sum_lines(grad_own))
 
-        def other_positions(x_first, g_first, x_last, g_last, d_own, normed):
+        def other_positions(x_first, g_first, x_last, g_last, d_own, normed, held):
             x_rows, g_rows = [x_first, group.swap(x_last)], [g_first, group.swap(g_last)]
-            hidden, d_gate_up, d_other, out_other = feed(1, x_first, x_rows, g_rows)
-            normed = [by_position(v) for v in normed]
-            got = group.swap(d_other[0])
-            got, *normed = lax.optimization_barrier((got, *normed))
-            d_first = blocks_of(d_own[0] + got.astype(F32))
-            hidden[0] = tied(d_first, hidden[0])[0]
+            (hidden, d_gate_up, d_other, out_other), normed = feed(1, x_first, x_rows, g_rows, normed)
+            got = [group.swap(block) for block in d_other]
+            hidden[1], got[0] = lax.optimization_barrier((hidden[1], got[0]))
+            keep, give = group.begin_back(blocks_of(d_own[0] + got[0].astype(F32)))
+            hidden[0], give = lax.optimization_barrier((hidden[0], give))
             grad = ffn_grad(g_rows, x_rows, hidden, d_gate_up, outer)
-            d_middle, gain_part = back_to_positions(d_first, 0, grad)
-            got = tied(grad, group.swap(d_other[1]))[0]
-            d_late, gain_late = back_to_positions(blocks_of(d_own[1] + got.astype(F32)), 1)
+            moved = group.first_back(give)
+            grad, moved, got[1] = lax.optimization_barrier((grad, moved, got[1]))
+            d_middle, gain_part = back_to_positions(group.end_back(keep, moved), 0)
+            d_last = group.unspread(blocks_of(d_own[1] + got[1].astype(F32)))
+            d_late, gain_late = back_to_positions(d_last, 1)
+            held = [by_position(v)[:, None] for v in held]
             low = d_middle.astype(BF16)
             d_middle = [d_middle, d_late]
             lows = [low, d_late.astype(BF16)]
-            return grad, d_middle, lows, group.swap(low), gain_part + gain_late, out_other, normed
-
-        grad, d_middle, d_middle_low, d_first, ffn_gain_part, out_other, normed_rows = region(
+            return grad, d_middle, lows, group.swap(low), gain_part + gain_late, out_other, normed, held
+
+        grad, d_middle, d_middle_low, d_first, ffn_gain_part, out_other, normed_rows, context_rows = region(
             item_bounds[0] >= 0,
             other_positions,
             ffn_other,
@@ -653,6 +680,7 @@
             cot_own[1],
             d_own,
             normed_all,
+            context,
         )
         out_parts = [out_own, out_other]
         ffn_sums[0], d_middle_low[1] = lax.optimization_barrier((ffn_sums[0], d_middle_low[1]))
@@ -664,12 +692,12 @@
         ffn_rows = [[block] for block in group.gather(ffn_own[0])]
         d_parts, out_parts = [], []
         for r in range(mp):
-            hidden, d_gate_up, d_part, out_part = feed(r, step, ffn_rows[r], cot_rows[r])
+            (hidden, d_gate_up, d_part, out_part), _ = feed(r, step, ffn_rows[r], cot_rows[r])
             d_parts.append(d_part[0])
             out_parts.append(out_part)
             step = ffn_grad(cot_rows[r], ffn_rows[r], hidden, d_gate_up, outer)
             ffn_sums.append(sum_lines(step))
-        d_mid, ffn_gain_part = back_to_positions(blocks_of(group.scatter(d_parts)), 0)
+        d_mid, ffn_gain_part = back_to_positions(group.unspread(blocks_of(group.scatter(d_parts))), 0)
         d_middle, d_middle_low = [d_mid], [d_mid.astype(BF16)]
         d_middle_all = [lax.all_gather(d_middle_low[0], "mp", axis=0, tiled=True)]
         d_middle_two = [[d_middle_all[0], dummy]]
@@ -678,6 +706,11 @@
         depth, n = whole.shape[-2:]
         blocks = whole.reshape(whole.shape[:-2] + (size, depth // size, n))
         return group.in_order(group.spread(jnp.moveaxis(blocks, -3, 0)))
+
+    def ffn_grads(sums):
+        done = jnp.stack(group.by_index([finish(v) for v in sums])).astype(F32)
+        done = done.reshape((positions,) + done.shape[2:])
+        return done[:, 0], done[:, 1:]
 
     def ends(d_normed_a, out_rows, middle, d_middle, ffn_gain_part):
         mixed = []
@@ -707,21 +740,30 @@
 
     if pair:
 
-        def attention_back(d_middle_low, d_first, qkv, probs, normed_rows, out_other, sums):
+        def attention_back(d_middle_low, d_first, qkv, probs, normed_rows, context_rows, out_other):
             d_last = group.swap(d_middle_low[1])
             two = [[d_middle_low[0], d_first], [d_middle_low[1], d_last]]
+            keep, give = begin_position(jnp.concatenate(group.by_index(two[0])))
+            *two[0], give = lax.optimization_barrier((*two[0], give))
+            mid_first = end_position(keep, give)
             d_qkv, own_first, other_first = attention_bwd(info, *two[0], qkv[0], probs[0], w_qkv, w_out)
-            two[1] = tied(d_qkv, *two[1])
-            sums = finish(sums)
-            *two[1], sums = lax.optimization_barrier((*two[1], sums))
+            d_qkv, mid_first, two[1][1] = lax.optimization_barrier((d_qkv, mid_first, two[1][1]))
+            keep, give = begin_position(d_qkv)
+            *two[1], give = lax.optimization_barrier((*two[1], give))
             d_later, own_last, other_last = attention_bwd(info, *two[1], qkv[1], probs[1], w_qkv, w_out)
-            d_qkv, d_later = by_position(d_qkv), by_position(d_later)
+            d_qkv = end_position(keep, give)
             sent = [group.swap(block) for block in out_other]
-            d_later, *sent = lax.optimization_barrier((d_later, *sent))
+            d_later, d_qkv, sent[0] = lax.optimization_barrier((d_later, d_qkv, sent[0]))
+            d_later = by_position(d_later)
+            keep, give = begin_position(jnp.concatenate(group.by_index(two[1])))
+            d_later, give = lax.optimization_barrier((d_later, give))
+            mid_last = end_position(keep, give)
             qkv_part = weight_grad(normed_rows, [d_qkv, d_later], outer)
-            return qkv_part, d_last, [own_first, own_last], [other_first, other_last], sent, sums
-
-        qkv_part, d_last, own_parts, other_parts, sent, ffn_first = region(
+            qkv_part, mid_last, sent[1] = lax.optimization_barrier((qkv_part, mid_last, sent[1]))
+            out_part = weight_grad([mid_first, mid_last], context_rows, outer)
+            return qkv_part, out_part, [own_first, own_last], [other_first, other_last], sent
+
+        qkv_part, out_part, own_parts, other_parts, sent = region(
             item_bounds[0] >= 0,
             attention_back,
             d_middle_low,
@@ -729,38 +771,31 @@
             qkv,
             probs,
             normed_rows,
+            context_rows,
             out_parts[1],
-            ffn_sums[0],
         )
         ffn_sums[1], own_parts[0] = lax.optimization_barrier((ffn_sums[1], own_parts[0]))
-        qkv_sums = sum_lines(tied(ffn_sums[1], qkv_part)[0])
-
-        def others(d_two, context, own_parts, other_parts, out_own, sent, middle, d_middle, sums, gain_part):
+        qkv_part, out_part = tied(ffn_sums[1], qkv_part, out_part)
+        qkv_sums, out_sums = sum_lines(qkv_part), sum_lines(out_part)
+
+        def others(own_parts, other_parts, out_own, sent, middle, d_middle, sums, gain_part):
             d_normed_a = [group.scatter([own_parts[c], other_parts[c]]) for c in range(chunks)]
             out_rows = [out_own[c] + sent[c].astype(F32) for c in range(chunks)]
-            held = [by_position(v)[:, None] for v in context]
-            out_part = weight_grad(
-                [by_position(jnp.concatenate(group.by_index(two))) for two in d_two], held, outer
-            )
-            return out_part, finish(sums), *ends(d_normed_a, out_rows, middle, d_middle, gain_part)
-
-        out_part, ffn_last, mixed, input_grad, attn_gain_grad, ffn_gain_grad = region(
+            return ffn_grads(sums), *ends(d_normed_a, out_rows, middle, d_middle, gain_part)
+
+        (down_grad, gate_up_grad), mixed, input_grad, attn_gain_grad, ffn_gain_grad = region(
             item_bounds[0] >= 0,
             others,
-            [[d_middle_low[0], d_first], [d_middle_low[1], d_last]],
-            context,
             own_parts,
             other_parts,
             out_parts[0],
             sent,
             middle,
             d_middle,
-            ffn_sums[1],
+            ffn_sums,
             ffn_gain_part,
         )
-        qkv_sums, out_part = lax.optimization_barrier((qkv_sums, out_part))
-        out_sums = sum_lines(out_part)
-        ffn_done = [ffn_first, ffn_last]
+        qkv_sums, out_sums, attn_gain_grad = lax.optimization_barrier((qkv_sums, out_sums, attn_gain_grad))
     else:
         d_qkv, own_part, _ = attention_bwd(info, *d_middle_two[0], qkv[0], probs[0], w_qkv, w_out)
         d_normed_a = [lax.psum_scatter(own_part, "mp", scatter_dimension=0, tiled=True)]
@@ -768,17 +803,13 @@
         qkv_part = weight_grad(normed_rows, [by_position(d_qkv)], outer)
         out_rows = [group.scatter([out_parts[r][0] for r in range(mp)])]
         qkv_sums, out_sums = sum_lines(qkv_part), sum_lines(out_part)
-        ffn_done = [finish(sums) for sums in ffn_sums]
+        down_grad, gate_up_grad = ffn_grads(ffn_sums)
         mixed, input_grad, attn_gain_grad, ffn_gain_grad = ends(
             d_normed_a, out_rows, middle, d_middle, ffn_gain_part
         )
 
     qkv_done = finish(qkv_sums)
     out_done = finish(tied(qkv_done, out_sums)[0])
-    ffn_done = jnp.stack(group.by_index(ffn_done)).astype(F32)
-    ffn_done = ffn_done.reshape((positions,) + ffn_done.shape[2:])
-    down_grad, gate_up_grad = ffn_done[:, 0], ffn_done[:, 1:]
-
     def both(got):
         got = jnp.swapaxes(got, 0, 1)
         return got.reshape((positions,) + got.shape[2:]).astype(F32)

time: 776 us -> 716 us (0.923)
  waiting for transfers between devices: 281 us -> 251 us
  local copies, waits for them, and re-layouts: 74.9 us -> 55.8 us
    ppermute x4, waiting for transfers between devices: 25.7 us -> 3.53 us  [sum_scatter(): values = keep + lax.ppermute(give, 'dp', self.route(bit))]
    reduce_scatter x4, waiting for transfers between devices: 33.5 us -> 13.8 us  [sum_lines(): lax.psum_scatter(part, 'dp', scatter_dimension=0, axis_index_groups=lines...]
    ppermute x40, waiting for transfers between devices: 141 us -> 160 us  [the longest x16 141 us: end(): lax.ppermute(give, 'dp', self.route(self.size // 2))]
    cond x115 -> x95, local copies, waits for them, and re-layouts: 23.3 us -> 20.5 us
  transfers between devices with their start and end apart: 68 -> 68, of which waited for: 23 -> 31; matrix products, arithmetic and copies ran while one was open for 22% -> 21% of each run, Pallas kernels for 26% -> 28%
where the time goes in v3:
time: 716 us; the launch traced here: 706 us
  waiting for transfers between devices  251 us (35%)
  Pallas kernels  218 us (30%)
  other arithmetic  112 us (16%)
  local copies, waits for them, and re-layouts  55.8 us (8%)
  starting transfers between devices  51.2 us (7%)
  between operations  15.2 us (2%)
    pallas_call x12, Pallas kernels, call(): pl.pallas_call(kernel, grid_spec=pltpu.PrefetchScalarGridSpec(num_scalar_...  218 us
    ppermute x16, waiting for transfers between devices, end(): lax.ppermute(give, 'dp', self.route(self.size // 2))  141 us
    ppermute x18, waiting for transfers between devices, swap(): return lax.ppermute(block, 'mp', [(0, 1), (1, 0)])  73.6 us
    concatenate x12, other arithmetic, end(): jnp.concatenate([keep, lax.ppermute(give, 'dp', self.route(self.size // 2...  21.5 us
    cond x95, local copies, waits for them, and re-layouts  20.5 us
    concatenate x16, other arithmetic, begin(): jnp.concatenate([keep, lax.ppermute(give, 'dp', self.route(bit))], axis=1)  19.9 us
    ppermute x16, starting transfers between devices, end(): lax.ppermute(give, 'dp', self.route(self.size // 2))  18.1 us
    ppermute x18, starting transfers between devices, swap(): return lax.ppermute(block, 'mp', [(0, 1), (1, 0)])  17.9 us
  transfers between devices with their start and end apart: 68, of which 31 were waited for; matrix products, arithmetic and copies ran while one was open for 21% of the time, Pallas kernels for 28%

profile of v3, /device:TPU:0, one launch (start us, length us, event | category | flops | bytes accessed | tf_op | source)
XLA Modules:
  0.0 705.6 jit_solution(3006936573484797014)
XLA Ops:
  8.1 2.4 collective-permute-start.47
  11.9 2.3 collective-permute-start.48
  14.2 2.8 fusion.103
  30.2 3.6 fusion.77
  35.5 7.2 %collective-permute-done.50 = bf16[4,128,1024]{2,1,0:T(8,128)(2,1)} collective-permute-done((bf16[4,128,1024]{2,1,0:T(8,128)(2,1)S(1)}, bf16[4,128,1024]{2,1,0:T(8,128)(2,1)}, u32[]{:S(2)}, u32[]{:S(2)}) %collective-permute-start.50) | collective-permute-done | bytes 1048608 | tf_op jit(solution)/shard_map/ppermute | solution.py:56
  44.6 2.4 fusion.80.other
  47.0 19.8 %attention_fwd.2 = (bf16[8,128,1024]{2,1,0:T(8,128)(2,1)}, bf16[8,3,8,64,128]{4,3,2,1,0:T(8,128)(2,1)}, f32[8,8,8,128]{3,2,1,0:T(8,128)}, bf16[8,128,512]{2,1,0:...) custom-call(s32[2]{0:T(128)S(1)} %pad_add_fusion.1.info, ...), custom_call_target="tpu_custom_call" | custom-call | flops 429496729600 | bytes 4538369024 | tf_op jit(solution)/shard_map/attention_fwd/pallas_call | solution.py:155
  69.3 2.2 pad_maximum_fusion.28
  71.5 2.5 fusion.74.other
  74.0 19.6 %attention_fwd.3 = (bf16[8,128,1024]{2,1,0:T(8,128)(2,1)}, bf16[8,3,8,64,128]{4,3,2,1,0:T(8,128)(2,1)}, f32[8,8,8,128]{3,2,1,0:T(8,128)}, bf16[8,128,512]{2,1,0:...) custom-call(s32[2]{0:T(128)S(1)} %pad_add_fusion.1.info, ...), custom_call_target="tpu_custom_call" | custom-call | flops 429496729600 | bytes 4538369024 | tf_op jit(solution)/shard_map/attention_fwd/pallas_call | solution.py:155
  102.5 18.2 %collective-permute-done.59 = bf16[4,128,1024]{2,1,0:T(8,128)(2,1)} collective-permute-done((bf16[4,128,1024]{2,1,0:T(8,128)(2,1)S(1)}, bf16[4,128,1024]{2,1,0:T(8,128)(2,1)}, u32[]{:S(2)}, u32[]{:S(2)}) %collective-permute-start.59) | collective-permute-done | bytes 1048608 | tf_op jit(solution)/shard_map/ppermute | solution.py:56
  124.1 67.2 %conditional.4 = (bf16[4,3,256,1408]{3,2,1,0:T(8,128)(2,1)}, bf16[512,1024]{1,0:T(8,128)(2,1)}, bf16[512,1024]{1,0:T(8,128)(2,1)}, bf16[512,1024]{1,0:T(8,128)(2...) conditional(s32[]{:T(128)} %convert_element_type.132, () %tuple.74, ...), branch_computations={%region_2.3_spmd, %region_3.4_spmd} | conditional | flops 2657512062976 | bytes 18158192640 | solution.py:39
  129.6 16.6 %feed_forward.4 = (bf16[512,1408]{1,0:T(8,128)(2,1)}, bf16[2,512,1408]{2,1,0:T(8,128)(2,1)}, f32[512,1024]{1,0:T(8,128)}, f32[512,1024]{1,0:T(8,128)}) custom-call(s32[1]{0:T(128)} %bitcast.5.info, bf16[512,1024]{1,0:T(8,128)(2,1)} %bitcast.rows.refs_2_, bf16[512,1024]{1,0:T(8,128)(2,1)} %get-tuple-element.158.cot.refs_0_, ...), custom_call_target="tpu_custom_call" | custom-call | flops 885837004800 | bytes 7982285312 | tf_op jit(solution)/shard_map/cond/branch_1_fun/feed_forward/pallas_call | solution.py:155
  146.3 2.1 pad_maximum_fusion
  148.4 16.7 %feed_forward.5 = (bf16[512,1408]{1,0:T(8,128)(2,1)}, bf16[2,512,1408]{2,1,0:T(8,128)(2,1)}, f32[512,1024]{1,0:T(8,128)}, f32[512,1024]{1,0:T(8,128)}) custom-call(s32[1]{0:T(128)} %bitcast.5.info, bf16[512,1024]{1,0:T(8,128)(2,1)} %bitcast.4.rows.refs_3_, bf16[512,1024]{1,0:T(8,128)(2,1)} %get-tuple-element.163.cot.refs_1_, ...), custom_call_target="tpu_custom_call" | custom-call | flops 885837004800 | bytes 7982285312 | tf_op jit(solution)/shard_map/cond/branch_1_fun/feed_forward/pallas_call | solution.py:155
  165.2 8.0 %collective-permute-done.2 = bf16[512,1024]{1,0:T(8,128)(2,1)} collective-permute-done((bf16[512,1024]{1,0:T(8,128)(2,1)}, bf16[512,1024]{1,0:T(8,128)(2,1)}, u32[]{:S(2)}, u32[]{:S(2)}) %collective-permute-start.2) | collective-permute-done | bytes 1048608 | tf_op jit(solution)/shard_map/cond/branch_1_fun/ppermute | solution.py:56
  174.5 16.8 %ffn_grad.2 = bf16[4,3,256,1408]{3,2,1,0:T(8,128)(2,1)} custom-call(bf16[512,1024]{1,0:T(8,128)(2,1)} %get-tuple-element.158.cot.refs_0_, bf16[512,1024]{1,0:T(8,128)(2,1)} %get-tuple-element.163.cot.refs_1_, bf16[512,1024]{1,0:T(8,128)(2,1)} %bitcast.rows.refs_2_, bf16[512,1024]{1,0:T(8,128)(2,1)} %bitcast.4.rows.refs_3_, bf16[512,1408]{1,0:T(8,128)(2,1)S(1)} %copy-done.3, ...), custom_call_target="tpu_custom_call" | custom-call | flops 885837004800 | bytes 2149580800 | tf_op jit(solution)/shard_map/cond/branch_1_fun/ffn_grad/pallas_call | solution.py:155
  191.4 159.7 %conditional.5 = (bf16[4,3,256,1408]{3,2,1,0:T(8,128)(2,1)}, f32[4,128,1024]{2,1,0:T(8,128)}, f32[4,128,1024]{2,1,0:T(8,128)}, bf16[4,128,1024]{2,1,0:T(8,128)(2...) conditional(s32[]{:T(128)} %convert_element_type.132, () %tuple.83, ...), branch_computations={%region_5.6_spmd, %region_6.13_spmd} | conditional | flops 2657548763136 | bytes 17908875264 | solution.py:39
  191.6 2.8 constant_dynamic-slice_fusion.4
  201.3 2.1 constant_dynamic-slice_fusion
  208.6 16.6 %feed_forward.6 = (bf16[512,1408]{1,0:T(8,128)(2,1)}, bf16[2,512,1408]{2,1,0:T(8,128)(2,1)}, bf16[512,1024]{1,0:T(8,128)(2,1)}, bf16[512,1024]{1,0:T(8,128)(2,1)}) custom-call(s32[1]{0:T(128)} %bitcast.6.info, bf16[512,1024]{1,0:T(8,128)(2,1)} %get-tuple-element.182.rows.refs_2_, bf16[512,1024]{1,0:T(8,128)(2,1)} %get-tuple-element.183.cot.refs_0_, ...), custom_call_target="tpu_custom_call" | custom-call | flops 885837004800 | bytes 7772570112 | tf_op jit(solution)/shard_map/cond/branch_1_fun/feed_forward/pallas_call | solution.py:155
  225.3 2.8 fusion.16
  228.1 3.7 collective-permute-done.18
  232.1 2.8 pad_maximum_fusion.1
  234.9 13.2 %collective-permute-done.16.rows.refs_3_ = bf16[512,1024]{1,0:T(8,128)(2,1)} collective-permute-done((bf16[512,1024]{1,0:T(8,128)(2,1)}, bf16[512,1024]{1,0:T(8,128)(2,1)}, u32[]{:S(2)}, u32[]{:S(2)}) %collective-permute-start.16) | collective-permute-done | bytes 1048608 | tf_op jit(solution)/shard_map/cond/branch_1_fun/ppermute | solution.py:56
  249.8 16.6 %feed_forward.7 = (bf16[512,1408]{1,0:T(8,128)(2,1)}, bf16[2,512,1408]{2,1,0:T(8,128)(2,1)}, bf16[512,1024]{1,0:T(8,128)(2,1)}, bf16[512,1024]{1,0:T(8,128)(2,1)}) custom-call(s32[1]{0:T(128)} %bitcast.6.info, bf16[512,1024]{1,0:T(8,128)(2,1)} %collective-permute-done.16.rows.refs_3_, bf16[512,1024]{1,0:T(8,128)(2,1)} %collective-permute-done.15.cot.refs_1_, ...), custom_call_target="tpu_custom_call" | custom-call | flops 885837004800 | bytes 7772570112 | tf_op jit(solution)/shard_map/cond/branch_1_fun/feed_forward/pallas_call | solution.py:155
  266.4 5.3 collective-permute-done.20
  271.7 2.7 pad_maximum_fusion.2
  274.4 2.4 add_convert_fusion.1
  281.1 18.2 %ffn_grad.3 = bf16[4,3,256,1408]{3,2,1,0:T(8,128)(2,1)} custom-call(bf16[512,1024]{1,0:T(8,128)(2,1)} %get-tuple-element.183.cot.refs_0_, bf16[512,1024]{1,0:T(8,128)(2,1)} %collective-permute-done.15.cot.refs_1_, bf16[512,1024]{1,0:T(8,128)(2,1)} %get-tuple-element.182.rows.refs_2_, bf16[512,1024]{1,0:T(8,128)(2,1)} %collective-permute-done.16.rows.refs_3_, ...), custom_call_target="tpu_custom_call" | custom-call | flops 885837004800 | bytes 2149580800 | tf_op jit(solution)/shard_map/cond/branch_1_fun/ffn_grad/pallas_call | solution.py:155
  299.3 2.3 add_convert_fusion
  304.8 8.0 %collective-permute-done.25 = bf16[2,1,128,1024]{3,2,1,0:T(8,128)(2,1)S(1)} collective-permute-done((bf16[2,1,128,1024]{3,2,1,0:T(8,128)(2,1)S(1)}, bf16[2,1,128,1024]{3,2,1,0:T(8,128)(2,1)S(1)}, u32[]{:S(2)}, u32[]{:S(2)}) %collective-permute-start.25) | collective-permute-done | bytes 524320 | tf_op jit(solution)/shard_map/cond/branch_1_fun/ppermute | solution.py:106
  316.2 3.9 fusion.96
  320.1 2.4 fusion.98
  327.0 11.6 %collective-permute-done.29 = bf16[1,2,2,128,512]{4,3,1,2,0:T(8,128)(2,1)S(1)} collective-permute-done((bf16[1,2,2,128,512]{4,3,1,2,0:T(8,128)(2,1)S(1)}, bf16[1,2,2,128,512]{4,3,1,2,0:T(8,128)(2,1)S(1)}, u32[]{:S(2)}, u32[]{:S(2)}) %collective-permute-start.29) | collective-permute-done | bytes 524320 | tf_op jit(solution)/shard_map/cond/branch_1_fun/ppermute | solution.py:96
  339.7 9.3 %collective-permute-done.31 = bf16[1,2,2,128,512]{4,3,1,2,0:T(8,128)(2,1)S(1)} collective-permute-done((bf16[1,2,2,128,512]{4,3,1,2,0:T(8,128)(2,1)S(1)}, bf16[1,2,2,128,512]{4,3,1,2,0:T(8,128)(2,1)S(1)}, u32[]{:S(2)}, u32[]{:S(2)}) %collective-permute-start.31) | collective-permute-done | bytes 524320 | tf_op jit(solution)/shard_map/cond/branch_1_fun/ppermute | solution.py:96
  352.1 156.5 %conditional.6 = (bf16[4,2,3,256,512]{4,3,2,1,0:T(8,128)(2,1)}, bf16[4,2,1,256,512]{4,3,2,1,0:T(8,128)(2,1)}, f32[4,128,1024]{2,1,0:T(8,128)}, f32[4,128,1024]{2...) conditional(s32[]{:T(128)} %convert_element_type.132, () %tuple.87, ...), branch_computations={%region_13.14_spmd, %region_14.15_spmd} | conditional | flops 1718001598464 | bytes 11795433472 | solution.py:39
  359.9 24.3 %attention_bwd.2 = (bf16[8,3,128,512]{3,2,1,0:T(8,128)(2,1)}, f32[4,128,1024]{2,1,0:T(8,128)}, bf16[4,128,1024]{2,1,0:T(8,128)(2,1)}) custom-call(s32[2]{0:T(128)S(1)} %get-tuple-element.222.info, bf16[4,128,1024]{2,1,0:T(8,128)(2,1)} %get-tuple-element.228.own, bf16[4,128,1024]{2,1,0:T(8,128)(2,1)} %get-tuple-element.229.other, ...), custom_call_target="tpu_custom_call" | custom-call | flops 429496729600 | bytes 4535092224 | tf_op jit(solution)/shard_map/cond/branch_1_fun/attention_bwd/pallas_call | solution.py:155
  394.2 23.5 %attention_bwd.3 = (bf16[8,3,128,512]{3,2,1,0:T(8,128)(2,1)}, f32[4,128,1024]{2,1,0:T(8,128)}, bf16[4,128,1024]{2,1,0:T(8,128)(2,1)}) custom-call(s32[2]{0:T(128)S(1)} %get-tuple-element.222.info, bf16[4,128,1024]{2,1,0:T(8,128)(2,1)} %get-tuple-element.238.own, bf16[4,128,1024]{2,1,0:T(8,128)(2,1)} %collective-permute-done.6.other, ...), custom_call_target="tpu_custom_call" | custom-call | flops 429496729600 | bytes 4535092224 | tf_op jit(solution)/shard_map/cond/branch_1_fun/attention_bwd/pallas_call | solution.py:155
  417.7 12.1 %collective-permute-done.8 = bf16[1,2,2,3,128,512]{5,4,1,3,2,0:T(8,128)(2,1)} collective-permute-done((bf16[1,2,2,3,128,512]{5,4,1,3,2,0:T(8,128)(2,1)}, bf16[1,2,2,3,128,512]{5,4,1,3,2,0:T(8,128)(2,1)}, u32[]{:S(2)}, u32[]{:S(2)}) %collective-permute-start.8) | collective-permute-done | bytes 1572896 | tf_op jit(solution)/shard_map/cond/branch_1_fun/ppermute | solution.py:96
  429.9 2.1 pad_maximum_fusion.9
  433.1 3.3 collective-permute-done.10
  443.9 29.3 %collective-permute-done.11 = bf16[1,2,2,3,128,512]{5,4,1,3,2,0:T(8,128)(2,1)S(1)} collective-permute-done((bf16[1,2,2,3,128,512]{5,4,1,3,2,0:T(8,128)(2,1)S(1)}, bf16[1,2,2,3,128,512]{5,4,1,3,2,0:T(8,128)(2,1)S(1)}, u32[]{:S(2)}, u32[]{:S(2)}) %collective-permute-start.11) | collective-permute-done | bytes 1572896 | tf_op jit(solution)/shard_map/cond/branch_1_fun/ppermute | solution.py:96
  475.9 21.9 %weight_grad.2 = bf16[4,2,3,256,512]{4,3,2,1,0:T(8,128)(2,1)} custom-call(bf16[2,512,1024]{2,1,0:T(8,128)(2,1)} %get-tuple-element.220.refs_0_, bf16[2,512,1024]{2,1,0:T(8,128)(2,1)} %get-tuple-element.221.refs_1_, bf16[2,3,512,512]{3,2,1,0:T(8,128)(2,1)S(1)} %bitcast.475, bf16[2,3,512,512]{3,2,1,0:T(8,128)(2,1)} %bitcast.493), custom_call_target="tpu_custom_call" | custom-call | flops 644245094400 | bytes 1677721600 | tf_op jit(solution)/shard_map/cond/branch_1_fun/weight_grad/pallas_call | solution.py:155
  497.8 2.1 collective-permute-done.13
  501.3 7.2 %weight_grad.3 = bf16[4,2,1,256,512]{4,3,2,1,0:T(8,128)(2,1)} custom-call(bf16[2,512,1024]{2,1,0:T(8,128)(2,1)S(1)} %bitcast.476, bf16[2,512,1024]{2,1,0:T(8,128)(2,1)S(1)} %bitcast.477, bf16[2,1,512,512]{3,2,1,0:T(8,128)(2,1)} %get-tuple-element.253.refs_2_, bf16[2,1,512,512]{3,2,1,0:T(8,128)(2,1)} %get-tuple-element.254.refs_3_), custom_call_target="tpu_custom_call" | custom-call | flops 214748364800 | bytes 838860800 | tf_op jit(solution)/shard_map/cond/branch_1_fun/weight_grad/pallas_call | solution.py:155
  510.5 142.0 %conditional.7 = (f32[8,64,1408]{2,1,0:T(8,128)}, f32[8,2,64,1408]{3,2,1,0:T(8,128)}, bf16[4,256,1024]{2,1,0:T(8,128)(2,1)}, f32[4,256,1024]{2,1,0:T(8,128)}, f32[4,64]{1,0:T(4,128)S(1)}, /*index=5*/f32[4,64]{1,0:T(4,128)S(1)}) conditional(s32[]{:T(128)} %convert_element_type.132, () %tuple.73, (s32[]{:T(128)}, s32[]{:T(128)}, ...), branch_computations={%region_16.17_spmd, %region_17.24_spmd} | conditional | flops 62505492 | bytes 271007872 | solution.py:39
  510.7 2.2 add_convert_fusion.5
  515.4 2.2 add_convert_fusion.3
  522.8 2.7 constant_dynamic-slice_fusion.16
  531.0 2.5 copy.266
  539.5 7.7 %collective-permute-done.40 = bf16[4,128,1024]{2,1,0:T(8,128)(2,1)} collective-permute-done((bf16[4,128,1024]{2,1,0:T(8,128)(2,1)}, bf16[4,128,1024]{2,1,0:T(8,128)(2,1)}, u32[]{:S(2)}, u32[]{:S(2)}) %collective-permute-start.40) | collective-permute-done | bytes 1048608 | tf_op jit(solution)/shard_map/cond/branch_1_fun/ppermute | solution.py:56
  547.2 19.2 %collective-permute-done.41 = bf16[4,128,1024]{2,1,0:T(8,128)(2,1)} collective-permute-done((bf16[4,128,1024]{2,1,0:T(8,128)(2,1)}, bf16[4,128,1024]{2,1,0:T(8,128)(2,1)}, u32[]{:S(2)}, u32[]{:S(2)}) %collective-permute-start.41) | collective-permute-done | bytes 1048608 | tf_op jit(solution)/shard_map/cond/branch_1_fun/ppermute | solution.py:56
  566.4 4.4 fusion.46
  570.9 4.8 fusion.43
  576.9 2.6 collective-permute-start.43
  582.1 2.0 fusion.60
  586.4 2.4 add_convert_fusion.2
  598.9 2.8 pad_add_fusion
  601.7 20.2 %collective-permute-done.35 = bf16[1,2,3,64,1408]{4,3,2,1,0:T(8,128)(2,1)S(1)} collective-permute-done((bf16[1,2,3,64,1408]{4,3,2,1,0:T(8,128)(2,1)S(1)}, bf16[1,2,3,64,1408]{4,3,2,1,0:T(8,128)(2,1)S(1)}, u32[]{:S(2)}, u32[]{:S(2)}) %collective-permute-start.35) | collective-permute-done | bytes 1081376 | tf_op jit(solution)/shard_map/cond/branch_1_fun/ppermute | solution.py:96
  622.2 22.5 %collective-permute-done.33 = bf16[1,2,3,64,1408]{4,3,2,1,0:T(8,128)(2,1)S(1)} collective-permute-done((bf16[1,2,3,64,1408]{4,3,2,1,0:T(8,128)(2,1)S(1)}, bf16[1,2,3,64,1408]{4,3,2,1,0:T(8,128)(2,1)S(1)}, u32[]{:S(2)}, u32[]{:S(2)}) %collective-permute-start.33) | collective-permute-done | bytes 1081376 | tf_op jit(solution)/shard_map/cond/branch_1_fun/ppermute | solution.py:96
  649.3 3.0 slice.410
  652.5 13.8 %reduce-scatter.9.cloned.1.call-done = bf16[1,2,3,256,512]{4,3,2,1,0:T(8,128)(2,1)} async-done(((bf16[4,2,3,256,512]{4,3,2,1,0:T(8,128)(2,1)}), bf16[1,2,3,256,512]{4,3,2,1,0:T(8,128)(2,1)}) %reduce-scatter.9.cloned.1.call-update) | async-done | bytes 1572880 | tf_op jit(solution)/shard_map/reduce_scatter | solution.py:592
  672.7 23.0 %collective-permute-done.63 = bf16[1,2,2,1,64,512]{5,4,2,3,1,0:T(8,128)(2,1)S(1)} collective-permute-done((bf16[1,2,2,1,64,512]{5,4,2,3,1,0:T(8,128)(2,1)S(1)}, bf16[1,2,2,1,64,512]{5,4,2,3,1,0:T(8,128)(2,1)S(1)}, u32[]{:S(2)}, u32[]{:S(2)}) %collective-permute-start.63) | collective-permute-done | bytes 262176 | tf_op jit(solution)/shard_map/ppermute | solution.py:96
  (398 shorter events, 154.6 us)
Async XLA Ops:
  7.2 343.9 %reduce-scatter.5.cloned.1.call-start = ((), (), s32[]{:S(2)}) async-start(), calls=%async_computation.4 | async-start | bytes 10813440 | tf_op jit(solution)/shard_map/reduce_scatter | solution.py:592
  8.1 16.7 %collective-permute-start.47 = (bf16[4,2,1024]{2,1,0:T(2,128)(2,1)S(1)}, bf16[4,2,1024]{2,1,0:T(2,128)(2,1)S(1)}, u32[]{:S(2)}, u32[]{:S(2)}) collective-permute-start(bf16[4,2,1024]{2,1,0:T(2,128)(2,1)S(1)} %slice.359), channel_id=1, source_target_pairs={{0,2},{2,4},{4,6},{6,8},{8,10},{10,12},{12,14},{14,16},{16,18},{18... | collective-permute-start | bytes 49160 | tf_op jit(solution)/shard_map/ppermute | solution.py:26
  11.9 14.4 %collective-permute-start.48 = (f32[4,1152]{1,0:T(4,128)S(1)}, f32[4,1152]{1,0:T(4,128)S(1)}, u32[]{:S(2)}, u32[]{:S(2)}) collective-permute-start(f32[4,1152]{1,0:T(4,128)S(1)} %pad_maximum_fusion.31), channel_id=1, source_target_pairs={{0,1},{1,0},{2,3},{3,2},{4,5},{5,4},{6,7},{7,6},{8,9},{9,8},{10,11... | collective-permute-start | bytes 55304 | tf_op jit(solution)/shard_map/ppermute | solution.py:56
  17.0 25.7 %collective-permute-start.50 = (bf16[4,128,1024]{2,1,0:T(8,128)(2,1)S(1)}, bf16[4,128,1024]{2,1,0:T(8,128)(2,1)}, u32[]{:S(2)}, u32[]{:S(2)}) collective-permute-start(bf16[4,128,1024]{2,1,0:T(8,128)(2,1)S(1)} %get-tuple-element.364), channel_id=1, source_target_pairs={{0,1},{1,0},{2,3},{3,2},{4,5},{5,4},{6,7},{7,6},{8,9},{9,8},{10,11... | collective-permute-start | bytes 3145736 | tf_op jit(solution)/shard_map/ppermute | solution.py:56
  19.9 7.4 %collective-permute-start.51 = (bf16[2,1,128,1024]{3,2,1,0:T(8,128)(2,1)}, bf16[2,1,128,1024]{3,2,1,0:T(8,128)(2,1)}, u32[]{:S(2)}, u32[]{:S(2)}) collective-permute-start(bf16[2,1,128,1024]{3,2,1,0:T(8,128)(2,1)} %get-tuple-element.589), channel_id=1, source_target_pairs={{0,2},{2,0},{4,6},{6,4},{8,10},{10,8},{12,14},{14,12},{16,18},{18,... | collective-permute-start | bytes 1572872 | tf_op jit(solution)/shard_map/ppermute | solution.py:89
  22.7 11.1 %collective-permute-start.55 = (bf16[2,1,128,1024]{3,2,1,0:T(8,128)(2,1)}, bf16[2,1,128,1024]{3,2,1,0:T(8,128)(2,1)S(1)}, u32[]{:S(2)}, u32[]{:S(2)}) collective-permute-start(bf16[2,1,128,1024]{3,2,1,0:T(8,128)(2,1)} %get-tuple-element.585), channel_id=1, source_target_pairs={{0,2},{2,0},{4,6},{6,4},{8,10},{10,8},{12,14},{14,12},{16,18},{18,... | collective-permute-start | bytes 1572872 | tf_op jit(solution)/shard_map/ppermute | solution.py:89
  24.8 19.8 %collective-permute-start.49 = (bf16[4,2,1024]{2,1,0:T(2,128)(2,1)S(1)}, bf16[4,2,1024]{2,1,0:T(2,128)(2,1)S(1)}, u32[]{:S(2)}, u32[]{:S(2)}) collective-permute-start(bf16[4,2,1024]{2,1,0:T(2,128)(2,1)S(1)} %collective-permute-done.47), channel_id=1, source_target_pairs={{0,1},{1,0},{2,3},{3,2},{4,5},{5,4},{6,7},{7,6},{8,9},{9,8},{10,11... | collective-permute-start | bytes 49160 | tf_op jit(solution)/shard_map/ppermute | solution.py:56
  28.6 14.8 %collective-permute-start.52 = (bf16[1,2,128,1024]{3,2,1,0:T(8,128)(2,1)S(1)}, bf16[1,2,128,1024]{3,2,1,0:T(8,128)(2,1)S(1)}, u32[]{:S(2)}, u32[]{:S(2)}) collective-permute-start(bf16[1,2,128,1024]{3,2,1,0:T(8,128)(2,1)S(1)} %get-tuple-element.588), channel_id=1, source_target_pairs={{0,4},{2,6},{4,0},{6,2},{8,12},{10,14},{12,8},{14,10},{16,20},{18,... | collective-permute-start | bytes 1572872 | tf_op jit(solution)/shard_map/ppermute | solution.py:96
  35.0 34.2 %collective-permute-start.56 = (bf16[1,2,128,1024]{3,2,1,0:T(8,128)(2,1)}, bf16[1,2,128,1024]{3,2,1,0:T(8,128)(2,1)}, u32[]{:S(2)}, u32[]{:S(2)}) collective-permute-start(bf16[1,2,128,1024]{3,2,1,0:T(8,128)(2,1)} %get-tuple-element.584), channel_id=1, source_target_pairs={{0,4},{2,6},{4,0},{6,2},{8,12},{10,14},{12,8},{14,10},{16,20},{18,... | collective-permute-start | bytes 1572872 | tf_op jit(solution)/shard_map/ppermute | solution.py:96
  42.7 28.8 %collective-permute-start.54 = (bf16[4,128,1024]{2,1,0:T(8,128)(2,1)}, bf16[4,128,1024]{2,1,0:T(8,128)(2,1)}, u32[]{:S(2)}, u32[]{:S(2)}) collective-permute-start(bf16[4,128,1024]{2,1,0:T(8,128)(2,1)} %get-tuple-element.371), channel_id=1, source_target_pairs={{0,1},{1,0},{2,3},{3,2},{4,5},{5,4},{6,7},{7,6},{8,9},{9,8},{10,11... | collective-permute-start | bytes 3145736 | tf_op jit(solution)/shard_map/ppermute | solution.py:56
  66.8 26.8 %collective-permute-start.53 = (bf16[4,128,1024]{2,1,0:T(8,128)(2,1)}, bf16[4,128,1024]{2,1,0:T(8,128)(2,1)}, u32[]{:S(2)}, u32[]{:S(2)}) collective-permute-start(bf16[4,128,1024]{2,1,0:T(8,128)(2,1)} %get-tuple-element.369), channel_id=1, source_target_pairs={{0,1},{1,0},{2,3},{3,2},{4,5},{5,4},{6,7},{7,6},{8,9},{9,8},{10,11... | collective-permute-start | bytes 3145736 | tf_op jit(solution)/shard_map/ppermute | solution.py:56
  95.4 25.3 %collective-permute-start.59 = (bf16[4,128,1024]{2,1,0:T(8,128)(2,1)S(1)}, bf16[4,128,1024]{2,1,0:T(8,128)(2,1)}, u32[]{:S(2)}, u32[]{:S(2)}) collective-permute-start(bf16[4,128,1024]{2,1,0:T(8,128)(2,1)S(1)} %get-tuple-element.377), channel_id=1, source_target_pairs={{0,1},{1,0},{2,3},{3,2},{4,5},{5,4},{6,7},{7,6},{8,9},{9,8},{10,11... | collective-permute-start | bytes 3145736 | tf_op jit(solution)/shard_map/ppermute | solution.py:56
  100.8 21.9 %collective-permute-start.58 = (bf16[1,2,128,1024]{3,2,1,0:T(8,128)(2,1)S(1)}, bf16[1,2,128,1024]{3,2,1,0:T(8,128)(2,1)S(1)}, u32[]{:S(2)}, u32[]{:S(2)}) collective-permute-start(bf16[1,2,128,1024]{3,2,1,0:T(8,128)(2,1)S(1)} %get-tuple-element.580), channel_id=1, source_target_pairs={{0,4},{2,6},{4,0},{6,2},{8,12},{10,14},{12,8},{14,10},{16,20},{18,... | collective-permute-start | bytes 1572872 | tf_op jit(solution)/shard_map/ppermute | solution.py:96
  124.8 40.4 %collective-permute-start.3 = (bf16[512,1024]{1,0:T(8,128)(2,1)}, bf16[512,1024]{1,0:T(8,128)(2,1)}, u32[]{:S(2)}, u32[]{:S(2)}) collective-permute-start(bf16[512,1024]{1,0:T(8,128)(2,1)} %bitcast.rows.refs_2_), channel_id=1, source_target_pairs={{0,1},{1,0},{2,3},{3,2},{4,5},{5,4},{6,7},{7,6},{8,9},{9,8},{10,11... | collective-permute-start | bytes 3145736 | tf_op jit(solution)/shard_map/cond/branch_1_fun/ppermute | solution.py:56
  125.1 48.0 %collective-permute-start.2 = (bf16[512,1024]{1,0:T(8,128)(2,1)}, bf16[512,1024]{1,0:T(8,128)(2,1)}, u32[]{:S(2)}, u32[]{:S(2)}) collective-permute-start(bf16[512,1024]{1,0:T(8,128)(2,1)} %get-tuple-element.158.cot.refs_0_), channel_id=1, source_target_pairs={{0,1},{1,0},{2,3},{3,2},{4,5},{5,4},{6,7},{7,6},{8,9},{9,8},{10,11... | collective-permute-start | bytes 3145736 | tf_op jit(solution)/shard_map/cond/branch_1_fun/ppermute | solution.py:56
  128.0 18.3 %collective-permute-start.1 = (bf16[1,2,128,1024]{3,2,1,0:T(8,128)(2,1)}, bf16[1,2,128,1024]{3,2,1,0:T(8,128)(2,1)}, u32[]{:S(2)}, u32[]{:S(2)}) collective-permute-start(bf16[1,2,128,1024]{3,2,1,0:T(8,128)(2,1)} %get-tuple-element.452), channel_id=1, source_target_pairs={{0,4},{2,6},{4,0},{6,2},{8,12},{10,14},{12,8},{14,10},{16,20},{18,... | collective-permute-start | bytes 1572872 | tf_op jit(solution)/shard_map/cond/branch_1_fun/ppermute | solution.py:96
  191.3 317.3 %reduce-scatter.7.cloned.1.call-start = ((), (), s32[]{:S(2)}) async-start(), calls=%async_computation.5 | async-start | bytes 10813440 | tf_op jit(solution)/shard_map/reduce_scatter | solution.py:592
  195.4 10.0 %collective-permute-start.17 = (bf16[2,1,2,128,1024]{4,3,1,2,0:T(8,128)(2,1)}, bf16[2,1,2,128,1024]{4,3,1,2,0:T(8,128)(2,1)S(1)}, u32[]{:S(2)}, u32[]{:S(2)}) collective-permute-start(bf16[2,1,2,128,1024]{4,3,1,2,0:T(8,128)(2,1)} %bitcast.460), channel_id=1, source_target_pairs={{0,2},{2,0},{4,6},{6,4},{8,10},{10,8},{12,14},{14,12},{16,18},{18,... | collective-permute-start | bytes 3145736 | tf_op jit(solution)/shard_map/cond/branch_1_fun/ppermute | solution.py:89
  197.8 124.8 %collective-permute-start.28 = (bf16[2,1,2,128,512]{4,3,1,2,0:T(8,128)(2,1)}, bf16[2,1,2,128,512]{4,3,1,2,0:T(8,128)(2,1)}, u32[]{:S(2)}, u32[]{:S(2)}) collective-permute-start(bf16[2,1,2,128,512]{4,3,1,2,0:T(8,128)(2,1)} %bitcast.464), channel_id=1, source_target_pairs={{0,2},{2,0},{4,6},{6,4},{8,10},{10,8},{12,14},{14,12},{16,18},{18,... | collective-permute-start | bytes 1572872 | tf_op jit(solution)/shard_map/cond/branch_1_fun/ppermute | solution.py:89
  198.8 26.4 %collective-permute-start.19 = (bf16[2,1,2,128,1024]{4,3,1,2,0:T(8,128)(2,1)}, bf16[2,1,2,128,1024]{4,3,1,2,0:T(8,128)(2,1)}, u32[]{:S(2)}, u32[]{:S(2)}) collective-permute-start(bf16[2,1,2,128,1024]{4,3,1,2,0:T(8,128)(2,1)} %bitcast.458), channel_id=1, source_target_pairs={{0,2},{2,0},{4,6},{6,4},{8,10},{10,8},{12,14},{14,12},{16,18},{18,... | collective-permute-start | bytes 3145736 | tf_op jit(solution)/shard_map/cond/branch_1_fun/ppermute | solution.py:89
  199.3 35.6 %collective-permute-start.15 = (bf16[512,1024]{1,0:T(8,128)(2,1)}, bf16[512,1024]{1,0:T(8,128)(2,1)}, u32[]{:S(2)}, u32[]{:S(2)}) collective-permute-start(bf16[512,1024]{1,0:T(8,128)(2,1)} %get-tuple-element.175), channel_id=1, source_target_pairs={{0,1},{1,0},{2,3},{3,2},{4,5},{5,4},{6,7},{7,6},{8,9},{9,8},{10,11... | collective-permute-start | bytes 3145736 | tf_op jit(solution)/shard_map/cond/branch_1_fun/ppermute | solution.py:56
  199.6 48.5 %collective-permute-start.16 = (bf16[512,1024]{1,0:T(8,128)(2,1)}, bf16[512,1024]{1,0:T(8,128)(2,1)}, u32[]{:S(2)}, u32[]{:S(2)}) collective-permute-start(bf16[512,1024]{1,0:T(8,128)(2,1)} %get-tuple-element.177), channel_id=1, source_target_pairs={{0,1},{1,0},{2,3},{3,2},{4,5},{5,4},{6,7},{7,6},{8,9},{9,8},{10,11... | collective-permute-start | bytes 3145736 | tf_op jit(solution)/shard_map/cond/branch_1_fun/ppermute | solution.py:56
  207.0 24.8 %collective-permute-start.18 = (bf16[1,2,2,128,1024]{4,3,1,2,0:T(8,128)(2,1)}, bf16[1,2,2,128,1024]{4,3,1,2,0:T(8,128)(2,1)}, u32[]{:S(2)}, u32[]{:S(2)}) collective-permute-start(bf16[1,2,2,128,1024]{4,3,1,2,0:T(8,128)(2,1)} %get-tuple-element.187), channel_id=1, source_target_pairs={{0,4},{2,6},{4,0},{6,2},{8,12},{10,14},{12,8},{14,10},{16,20},{18,... | collective-permute-start | bytes 3145736 | tf_op jit(solution)/shard_map/cond/branch_1_fun/ppermute | solution.py:96
  225.2 99.1 %collective-permute-start.30 = (bf16[2,1,2,128,512]{4,3,1,2,0:T(8,128)(2,1)}, bf16[2,1,2,128,512]{4,3,1,2,0:T(8,128)(2,1)}, u32[]{:S(2)}, u32[]{:S(2)}) collective-permute-start(bf16[2,1,2,128,512]{4,3,1,2,0:T(8,128)(2,1)} %bitcast.462), channel_id=1, source_target_pairs={{0,2},{2,0},{4,6},{6,4},{8,10},{10,8},{12,14},{14,12},{16,18},{18,... | collective-permute-start | bytes 1572872 | tf_op jit(solution)/shard_map/cond/branch_1_fun/ppermute | solution.py:89
  231.8 42.6 %collective-permute-start.21 = (bf16[512,1024]{1,0:T(8,128)(2,1)}, bf16[512,1024]{1,0:T(8,128)(2,1)}, u32[]{:S(2)}, u32[]{:S(2)}) collective-permute-start(bf16[512,1024]{1,0:T(8,128)(2,1)} %get-tuple-element.197), channel_id=1, source_target_pairs={{0,1},{1,0},{2,3},{3,2},{4,5},{5,4},{6,7},{7,6},{8,9},{9,8},{10,11... | collective-permute-start | bytes 3145736 | tf_op jit(solution)/shard_map/cond/branch_1_fun/ppermute | solution.py:56
  248.1 23.6 %collective-permute-start.20 = (bf16[1,2,2,128,1024]{4,3,1,2,0:T(8,128)(2,1)}, bf16[1,2,2,128,1024]{4,3,1,2,0:T(8,128)(2,1)}, u32[]{:S(2)}, u32[]{:S(2)}) collective-permute-start(bf16[1,2,2,128,1024]{4,3,1,2,0:T(8,128)(2,1)} %get-tuple-element.195), channel_id=1, source_target_pairs={{0,4},{2,6},{4,0},{6,2},{8,12},{10,14},{12,8},{14,10},{16,20},{18,... | collective-permute-start | bytes 3145736 | tf_op jit(solution)/shard_map/cond/branch_1_fun/ppermute | solution.py:96
  266.4 32.9 %collective-permute-start.23 = (bf16[512,1024]{1,0:T(8,128)(2,1)}, bf16[512,1024]{1,0:T(8,128)(2,1)}, u32[]{:S(2)}, u32[]{:S(2)}) collective-permute-start(bf16[512,1024]{1,0:T(8,128)(2,1)} %get-tuple-element.204), channel_id=1, source_target_pairs={{0,1},{1,0},{2,3},{3,2},{4,5},{5,4},{6,7},{7,6},{8,9},{9,8},{10,11... | collective-permute-start | bytes 3145736 | tf_op jit(solution)/shard_map/cond/branch_1_fun/ppermute | solution.py:56
  279.4 19.9 %collective-permute-start.22 = (bf16[2,1,128,1024]{3,2,1,0:T(8,128)(2,1)}, bf16[2,1,128,1024]{3,2,1,0:T(8,128)(2,1)}, u32[]{:S(2)}, u32[]{:S(2)}) collective-permute-start(bf16[2,1,128,1024]{3,2,1,0:T(8,128)(2,1)} %pad_maximum_fusion.7), channel_id=1, source_target_pairs={{0,4},{2,6},{4,0},{6,2},{8,12},{10,14},{12,8},{14,10},{16,20},{18,... | collective-permute-start | bytes 1572872 | tf_op jit(solution)/shard_map/cond/branch_1_fun/ppermute | solution.py:106
  301.8 11.0 %collective-permute-start.25 = (bf16[2,1,128,1024]{3,2,1,0:T(8,128)(2,1)S(1)}, bf16[2,1,128,1024]{3,2,1,0:T(8,128)(2,1)S(1)}, u32[]{:S(2)}, u32[]{:S(2)}) collective-permute-start(bf16[2,1,128,1024]{3,2,1,0:T(8,128)(2,1)S(1)} %pad_maximum_fusion.8), channel_id=1, source_target_pairs={{0,4},{2,6},{4,0},{6,2},{8,12},{10,14},{12,8},{14,10},{16,20},{18,... | collective-permute-start | bytes 1572872 | tf_op jit(solution)/shard_map/cond/branch_1_fun/ppermute | solution.py:106
  304.7 8.3 %collective-permute-start.24 = (bf16[1,2,128,1024]{3,2,1,0:T(8,128)(2,1)S(1)}, bf16[1,2,128,1024]{3,2,1,0:T(8,128)(2,1)S(1)}, u32[]{:S(2)}, u32[]{:S(2)}) collective-permute-start(bf16[1,2,128,1024]{3,2,1,0:T(8,128)(2,1)S(1)} %maximum_bitcast_fusion), channel_id=1, source_target_pairs={{0,2},{2,0},{4,6},{6,4},{8,10},{10,8},{12,14},{14,12},{16,18},{18,... | collective-permute-start | bytes 1572872 | tf_op jit(solution)/shard_map/cond/branch_1_fun/ppermute | solution.py:112
  322.4 28.2 %collective-permute-start.27 = (bf16[4,128,1024]{2,1,0:T(8,128)(2,1)}, bf16[4,128,1024]{2,1,0:T(8,128)(2,1)}, u32[]{:S(2)}, u32[]{:S(2)}) collective-permute-start(bf16[4,128,1024]{2,1,0:T(8,128)(2,1)} %get-tuple-element.643), channel_id=1, source_target_pairs={{0,1},{1,0},{2,3},{3,2},{4,5},{5,4},{6,7},{7,6},{8,9},{9,8},{10,11... | collective-permute-start | bytes 3145736 | tf_op jit(solution)/shard_map/cond/branch_1_fun/ppermute | solution.py:56
  323.7 14.8 %collective-permute-start.29 = (bf16[1,2,2,128,512]{4,3,1,2,0:T(8,128)(2,1)S(1)}, bf16[1,2,2,128,512]{4,3,1,2,0:T(8,128)(2,1)S(1)}, u32[]{:S(2)}, u32[]{:S(2)}) collective-permute-start(bf16[1,2,2,128,512]{4,3,1,2,0:T(8,128)(2,1)S(1)} %get-tuple-element.548), channel_id=1, source_target_pairs={{0,4},{2,6},{4,0},{6,2},{8,12},{10,14},{12,8},{14,10},{16,20},{18,... | collective-permute-start | bytes 1572872 | tf_op jit(solution)/shard_map/cond/branch_1_fun/ppermute | solution.py:96
  325.4 23.5 %collective-permute-start.31 = (bf16[1,2,2,128,512]{4,3,1,2,0:T(8,128)(2,1)S(1)}, bf16[1,2,2,128,512]{4,3,1,2,0:T(8,128)(2,1)S(1)}, u32[]{:S(2)}, u32[]{:S(2)}) collective-permute-start(bf16[1,2,2,128,512]{4,3,1,2,0:T(8,128)(2,1)S(1)} %get-tuple-element.544), channel_id=1, source_target_pairs={{0,4},{2,6},{4,0},{6,2},{8,12},{10,14},{12,8},{14,10},{16,20},{18,... | collective-permute-start | bytes 1572872 | tf_op jit(solution)/shard_map/cond/branch_1_fun/ppermute | solution.py:96
  351.2 301.3 %reduce-scatter.11.cloned.1.call-start = ((), (), s32[]{:S(2)}) async-start(), calls=%async_computation.7 | async-start | bytes 2621440 | tf_op jit(solution)/shard_map/reduce_scatter | solution.py:592
  355.2 2.9 collective-permute-start.4
  355.2 31.4 %collective-permute-start.6 = (bf16[4,128,1024]{2,1,0:T(8,128)(2,1)}, bf16[4,128,1024]{2,1,0:T(8,128)(2,1)}, u32[]{:S(2)}, u32[]{:S(2)}) collective-permute-start(bf16[4,128,1024]{2,1,0:T(8,128)(2,1)} %get-tuple-element.238.own), channel_id=1, source_target_pairs={{0,1},{1,0},{2,3},{3,2},{4,5},{5,4},{6,7},{7,6},{8,9},{9,8},{10,11... | collective-permute-start | bytes 3145736 | tf_op jit(solution)/shard_map/cond/branch_1_fun/ppermute | solution.py:56
  359.6 25.5 %collective-permute-start.5 = (bf16[1,2,2,128,1024]{4,3,1,2,0:T(8,128)(2,1)}, bf16[1,2,2,128,1024]{4,3,1,2,0:T(8,128)(2,1)}, u32[]{:S(2)}, u32[]{:S(2)}) collective-permute-start(bf16[1,2,2,128,1024]{4,3,1,2,0:T(8,128)(2,1)} %get-tuple-element.235), channel_id=1, source_target_pairs={{0,4},{2,6},{4,0},{6,2},{8,12},{10,14},{12,8},{14,10},{16,20},{18,... | collective-permute-start | bytes 3145736 | tf_op jit(solution)/shard_map/cond/branch_1_fun/ppermute | solution.py:96
  387.7 3.5 collective-permute-start.7
  387.8 44.2 %collective-permute-start.9 = (bf16[512,1024]{1,0:T(8,128)(2,1)}, bf16[512,1024]{1,0:T(8,128)(2,1)}, u32[]{:S(2)}, u32[]{:S(2)}) collective-permute-start(bf16[512,1024]{1,0:T(8,128)(2,1)} %get-tuple-element.244), channel_id=1, source_target_pairs={{0,1},{1,0},{2,3},{3,2},{4,5},{5,4},{6,7},{7,6},{8,9},{9,8},{10,11... | collective-permute-start | bytes 3145736 | tf_op jit(solution)/shard_map/cond/branch_1_fun/ppermute | solution.py:56
  393.1 36.8 %collective-permute-start.8 = (bf16[1,2,2,3,128,512]{5,4,1,3,2,0:T(8,128)(2,1)}, bf16[1,2,2,3,128,512]{5,4,1,3,2,0:T(8,128)(2,1)}, u32[]{:S(2)}, u32[]{:S(2)}) collective-permute-start(bf16[1,2,2,3,128,512]{5,4,1,3,2,0:T(8,128)(2,1)} %get-tuple-element.243), channel_id=1, source_target_pairs={{0,4},{2,6},{4,0},{6,2},{8,12},{10,14},{12,8},{14,10},{16,20},{18,... | collective-permute-start | bytes 4718600 | tf_op jit(solution)/shard_map/cond/branch_1_fun/ppermute | solution.py:96
  432.9 3.5 collective-permute-start.10
  436.7 36.5 %collective-permute-start.11 = (bf16[1,2,2,3,128,512]{5,4,1,3,2,0:T(8,128)(2,1)S(1)}, bf16[1,2,2,3,128,512]{5,4,1,3,2,0:T(8,128)(2,1)S(1)}, u32[]{:S(2)}, u32[]{:S(2)}) collective-permute-start(bf16[1,2,2,3,128,512]{5,4,1,3,2,0:T(8,128)(2,1)S(1)} %get-tuple-element.456), channel_id=1, source_target_pairs={{0,4},{2,6},{4,0},{6,2},{8,12},{10,14},{12,8},{14,10},{16,20},{18,... | collective-permute-start | bytes 4718600 | tf_op jit(solution)/shard_map/cond/branch_1_fun/ppermute | solution.py:96
  439.7 2.7 collective-permute-start.12
  439.8 61.6 %collective-permute-start.14 = (bf16[512,1024]{1,0:T(8,128)(2,1)}, bf16[512,1024]{1,0:T(8,128)(2,1)}, u32[]{:S(2)}, u32[]{:S(2)}) collective-permute-start(bf16[512,1024]{1,0:T(8,128)(2,1)} %get-tuple-element.249), channel_id=1, source_target_pairs={{0,1},{1,0},{2,3},{3,2},{4,5},{5,4},{6,7},{7,6},{8,9},{9,8},{10,11... | collective-permute-start | bytes 3145736 | tf_op jit(solution)/shard_map/cond/branch_1_fun/ppermute | solution.py:56
  475.1 24.8 %collective-permute-start.13 = (bf16[1,2,2,128,1024]{4,3,1,2,0:T(8,128)(2,1)}, bf16[1,2,2,128,1024]{4,3,1,2,0:T(8,128)(2,1)}, u32[]{:S(2)}, u32[]{:S(2)}) collective-permute-start(bf16[1,2,2,128,1024]{4,3,1,2,0:T(8,128)(2,1)} %get-tuple-element.248), channel_id=1, source_target_pairs={{0,4},{2,6},{4,0},{6,2},{8,12},{10,14},{12,8},{14,10},{16,20},{18,... | collective-permute-start | bytes 3145736 | tf_op jit(solution)/shard_map/cond/branch_1_fun/ppermute | solution.py:96
  508.7 157.6 %reduce-scatter.9.cloned.1.call-start = ((), (), s32[]{:S(2)}) async-start(), calls=%async_computation.6 | async-start | bytes 7864320 | tf_op jit(solution)/shard_map/reduce_scatter | solution.py:592
  514.6 21.0 %collective-permute-start.36 = (bf16[2,1,128,1024]{3,2,1,0:T(8,128)(2,1)}, bf16[2,1,128,1024]{3,2,1,0:T(8,128)(2,1)}, u32[]{:S(2)}, u32[]{:S(2)}) collective-permute-start(bf16[2,1,128,1024]{3,2,1,0:T(8,128)(2,1)} %pad_maximum_fusion.19), channel_id=1, source_target_pairs={{0,4},{2,6},{4,0},{6,2},{8,12},{10,14},{12,8},{14,10},{16,20},{18,... | collective-permute-start | bytes 1572872 | tf_op jit(solution)/shard_map/cond/branch_1_fun/ppermute | solution.py:106
  519.5 19.0 %collective-permute-start.38 = (bf16[2,1,128,1024]{3,2,1,0:T(8,128)(2,1)}, bf16[2,1,128,1024]{3,2,1,0:T(8,128)(2,1)}, u32[]{:S(2)}, u32[]{:S(2)}) collective-permute-start(bf16[2,1,128,1024]{3,2,1,0:T(8,128)(2,1)} %pad_maximum_fusion.20), channel_id=1, source_target_pairs={{0,4},{2,6},{4,0},{6,2},{8,12},{10,14},{12,8},{14,10},{16,20},{18,... | collective-permute-start | bytes 1572872 | tf_op jit(solution)/shard_map/cond/branch_1_fun/ppermute | solution.py:106
  520.8 26.4 %collective-permute-start.40 = (bf16[4,128,1024]{2,1,0:T(8,128)(2,1)}, bf16[4,128,1024]{2,1,0:T(8,128)(2,1)}, u32[]{:S(2)}, u32[]{:S(2)}) collective-permute-start(bf16[4,128,1024]{2,1,0:T(8,128)(2,1)} %get-tuple-element.279), channel_id=1, source_target_pairs={{0,1},{1,0},{2,3},{3,2},{4,5},{5,4},{6,7},{7,6},{8,9},{9,8},{10,11... | collective-permute-start | bytes 3145736 | tf_op jit(solution)/shard_map/cond/branch_1_fun/ppermute | solution.py:56
  522.4 44.0 %collective-permute-start.41 = (bf16[4,128,1024]{2,1,0:T(8,128)(2,1)}, bf16[4,128,1024]{2,1,0:T(8,128)(2,1)}, u32[]{:S(2)}, u32[]{:S(2)}) collective-permute-start(bf16[4,128,1024]{2,1,0:T(8,128)(2,1)} %get-tuple-element.283), channel_id=1, source_target_pairs={{0,1},{1,0},{2,3},{3,2},{4,5},{5,4},{6,7},{7,6},{8,9},{9,8},{10,11... | collective-permute-start | bytes 3145736 | tf_op jit(solution)/shard_map/cond/branch_1_fun/ppermute | solution.py:56
  526.6 67.0 %collective-permute-start.34 = (bf16[2,1,3,64,1408]{4,3,2,1,0:T(8,128)(2,1)}, bf16[2,1,3,64,1408]{4,3,2,1,0:T(8,128)(2,1)}, u32[]{:S(2)}, u32[]{:S(2)}) collective-permute-start(bf16[2,1,3,64,1408]{4,3,2,1,0:T(8,128)(2,1)} %bitcast.466), channel_id=1, source_target_pairs={{0,2},{2,0},{4,6},{6,4},{8,10},{10,8},{12,14},{14,12},{16,18},{18,... | collective-permute-start | bytes 3244040 | tf_op jit(solution)/shard_map/cond/branch_1_fun/ppermute | solution.py:89
  535.6 60.0 %collective-permute-start.32 = (bf16[2,1,3,64,1408]{4,3,2,1,0:T(8,128)(2,1)}, bf16[2,1,3,64,1408]{4,3,2,1,0:T(8,128)(2,1)}, u32[]{:S(2)}, u32[]{:S(2)}) collective-permute-start(bf16[2,1,3,64,1408]{4,3,2,1,0:T(8,128)(2,1)} %bitcast.508), channel_id=1, source_target_pairs={{0,2},{2,0},{4,6},{6,4},{8,10},{10,8},{12,14},{14,12},{16,18},{18,... | collective-permute-start | bytes 3244040 | tf_op jit(solution)/shard_map/cond/branch_1_fun/ppermute | solution.py:89
  538.4 41.2 %collective-permute-start.37 = (bf16[1,2,128,1024]{3,2,1,0:T(8,128)(2,1)S(1)}, bf16[1,2,128,1024]{3,2,1,0:T(8,128)(2,1)S(1)}, u32[]{:S(2)}, u32[]{:S(2)}) collective-permute-start(bf16[1,2,128,1024]{3,2,1,0:T(8,128)(2,1)S(1)} %maximum_bitcast_fusion.2), channel_id=1, source_target_pairs={{0,2},{2,0},{4,6},{6,4},{8,10},{10,8},{12,14},{14,12},{16,18},{18,... | collective-permute-start | bytes 1572872 | tf_op jit(solution)/shard_map/cond/branch_1_fun/ppermute | solution.py:112
  547.2 34.9 %collective-permute-start.39 = (bf16[1,2,128,1024]{3,2,1,0:T(8,128)(2,1)S(1)}, bf16[1,2,128,1024]{3,2,1,0:T(8,128)(2,1)S(1)}, u32[]{:S(2)}, u32[]{:S(2)}) collective-permute-start(bf16[1,2,128,1024]{3,2,1,0:T(8,128)(2,1)S(1)} %maximum_bitcast_fusion.3), channel_id=1, source_target_pairs={{0,2},{2,0},{4,6},{6,4},{8,10},{10,8},{12,14},{14,12},{16,18},{18,... | collective-permute-start | bytes 1572872 | tf_op jit(solution)/shard_map/cond/branch_1_fun/ppermute | solution.py:112
  576.9 8.2 %collective-permute-start.43 = (f32[2,4,512]{2,1,0:T(4,128)S(1)}, f32[2,4,512]{2,1,0:T(4,128)S(1)}, u32[]{:S(2)}, u32[]{:S(2)}) collective-permute-start(f32[2,4,512]{2,1,0:T(4,128)S(1)} %select_bitcast_fusion), channel_id=1, source_target_pairs={{0,16},{2,18},{4,20},{6,22},{8,24},{10,26},{12,28},{14,30},{16,0},... | collective-permute-start | bytes 49160 | tf_op jit(solution)/shard_map/cond/branch_1_fun/ppermute | solution.py:140
  579.6 19.3 %collective-permute-start.42 = (f32[4,2,1024]{2,1,0:T(2,128)S(1)}, f32[4,2,1024]{2,1,0:T(2,128)S(1)}, u32[]{:S(2)}, u32[]{:S(2)}) collective-permute-start(f32[4,2,1024]{2,1,0:T(2,128)S(1)} %slice_select_fusion), channel_id=1, source_target_pairs={{2,0},{4,2},{6,4},{8,6},{10,8},{12,10},{14,12},{16,14},{18,16},{20... | collective-permute-start | bytes 98312 | tf_op jit(solution)/shard_map/cond/branch_1_fun/ppermute | solution.py:26
  585.9 3.9 collective-permute-start.44
  589.7 3.7 collective-permute-start.45
  595.1 26.7 %collective-permute-start.35 = (bf16[1,2,3,64,1408]{4,3,2,1,0:T(8,128)(2,1)S(1)}, bf16[1,2,3,64,1408]{4,3,2,1,0:T(8,128)(2,1)S(1)}, u32[]{:S(2)}, u32[]{:S(2)}) collective-permute-start(bf16[1,2,3,64,1408]{4,3,2,1,0:T(8,128)(2,1)S(1)} %get-tuple-element.490), channel_id=1, source_target_pairs={{0,4},{2,6},{4,0},{6,2},{8,12},{10,14},{12,8},{14,10},{16,20},{18,... | collective-permute-start | bytes 3244040 | tf_op jit(solution)/shard_map/cond/branch_1_fun/ppermute | solution.py:96
  597.3 47.4 %collective-permute-start.33 = (bf16[1,2,3,64,1408]{4,3,2,1,0:T(8,128)(2,1)S(1)}, bf16[1,2,3,64,1408]{4,3,2,1,0:T(8,128)(2,1)S(1)}, u32[]{:S(2)}, u32[]{:S(2)}) collective-permute-start(bf16[1,2,3,64,1408]{4,3,2,1,0:T(8,128)(2,1)S(1)} %get-tuple-element.482), channel_id=1, source_target_pairs={{0,4},{2,6},{4,0},{6,2},{8,12},{10,14},{12,8},{14,10},{16,20},{18,... | collective-permute-start | bytes 3244040 | tf_op jit(solution)/shard_map/cond/branch_1_fun/ppermute | solution.py:96
  667.9 2.4 collective-permute-start.60
  668.1 3.5 collective-permute-start.62
  670.4 26.4 %collective-permute-start.61 = (bf16[1,2,2,3,64,512]{5,4,3,2,1,0:T(8,128)(2,1)S(1)}, bf16[1,2,2,3,64,512]{5,4,3,2,1,0:T(8,128)(2,1)S(1)}, u32[]{:S(2)}, u32[]{:S(2)}) collective-permute-start(bf16[1,2,2,3,64,512]{5,4,3,2,1,0:T(8,128)(2,1)S(1)} %get-tuple-element.576), channel_id=1, source_target_pairs={{0,4},{2,6},{4,0},{6,2},{8,12},{10,14},{12,8},{14,10},{16,20},{18,... | collective-permute-start | bytes 2359304 | tf_op jit(solution)/shard_map/ppermute | solution.py:96
  671.7 24.0 %collective-permute-start.63 = (bf16[1,2,2,1,64,512]{5,4,2,3,1,0:T(8,128)(2,1)S(1)}, bf16[1,2,2,1,64,512]{5,4,2,3,1,0:T(8,128)(2,1)S(1)}, u32[]{:S(2)}, u32[]{:S(2)}) collective-permute-start(bf16[1,2,2,1,64,512]{5,4,2,3,1,0:T(8,128)(2,1)S(1)} %get-tuple-element.596), channel_id=1, source_target_pairs={{0,4},{2,6},{4,0},{6,2},{8,12},{10,14},{12,8},{14,10},{16,20},{18,... | collective-permute-start | bytes 786440 | tf_op jit(solution)/shard_map/ppermute | solution.py:96
  (70 other events, 548.4 us)
Sparse Core Ops, SparseCore 0:
  191.4 148.1 reduce-scatter.4
  351.3 148.9 reduce-scatter.6
  508.7 44.2 reduce-scatter.10
  555.3 110.9 reduce-scatter.8

commit v4 on v3

--- a/solution.py
+++ b/solution.py
@@ -579,7 +579,9 @@
             if c:
                 other_blocks[c] = tied(step, other_blocks[c])[0]
             other = delayed_chunk(other_lags, other_earlier, other_blocks, c)
-            own, other, cot_own[c] = lax.optimization_barrier((resid[c], other, cot_own[c]))
+            own = resid[c]
+            if c == 0:
+                own, other, cot_own[c] = lax.optimization_barrier((own, other, cot_own[c]))
         *kept, own_part, other_part = attention_fwd(info, own, other, gains, w_qkv, w_out)
         step = own_part
         for held, array in zip((normed_all, qkv, probs, context), kept, strict=True):
@@ -612,12 +614,15 @@
             break
         keep, given = group.begin(normed_f)
         ffn_own.append(group.end(keep, given).reshape(rows, width))
-    def feed(r, step, x_rows, g_rows, beside=()):
+    def feed(r, step, x_rows, g_rows, beside=(), between=()):
         position = jnp.asarray(group.index(r) * size + group.member, jnp.int32)
         kind = F32 if r == 0 or not pair else BF16
         results, moved = [], []
         for c in range(chunks):
             xs, gs = tied(step, x_rows[c], g_rows[c])
+            if between and c:
+                between = [by_position(v)[:, None] for v in tied(step, *between)]
+                xs, *between = lax.optimization_barrier((xs, *between))
             if beside:
                 keep, give = begin_position(beside[c])
                 xs, give = lax.optimization_barrier((xs, give))
@@ -628,7 +633,7 @@
                 step, moved[c] = lax.optimization_barrier((step, moved[c]))
                 result = (step, *result[1:])
             results.append(result)
-        return [list(v) for v in zip(*results, strict=True)], moved
+        return [list(v) for v in zip(*results, strict=True)], moved, list(between)
 
     blocks_of = lambda d_rows: d_rows.astype(BF16).reshape(size, part, width)
 
@@ -642,7 +647,7 @@
         def own_positions(x_rows, last, g_rows):
             last = group.spread(last).reshape(rows, width)
             swapped = [group.swap(g_rows[0]), group.swap(x_rows)]
-            (hidden, d_gate_up, d_own, out_own), _ = feed(0, x_rows, [x_rows, last], g_rows)
+            (hidden, d_gate_up, d_own, out_own), _, _ = feed(0, x_rows, [x_rows, last], g_rows)
             hidden[1], *swapped = lax.optimization_barrier((hidden[1], *swapped))
             grad = ffn_grad(g_rows, [x_rows, last], hidden, d_gate_up, outer)
             return grad, last, swapped, d_own, out_own
@@ -654,7 +659,7 @@
 
         def other_positions(x_first, g_first, x_last, g_last, d_own, normed, held):
             x_rows, g_rows = [x_first, group.swap(x_last)], [g_first, group.swap(g_last)]
-            (hidden, d_gate_up, d_other, out_other), normed = feed(1, x_first, x_rows, g_rows, normed)
+            (hidden, d_gate_up, d_other, out_other), normed, held = feed(1, x_first, x_rows, g_rows, normed, held)
             got = [group.swap(block) for block in d_other]
             hidden[1], got[0] = lax.optimization_barrier((hidden[1], got[0]))
             keep, give = group.begin_back(blocks_of(d_own[0] + got[0].astype(F32)))
@@ -663,13 +668,16 @@
             moved = group.first_back(give)
             grad, moved, got[1] = lax.optimization_barrier((grad, moved, got[1]))
             d_middle, gain_part = back_to_positions(group.end_back(keep, moved), 0)
-            d_last = group.unspread(blocks_of(d_own[1] + got[1].astype(F32)))
+            low = d_middle.astype(BF16)
+            low, got[1] = lax.optimization_barrier((low, got[1]))
+            d_first = group.swap(low)
+            keep, give = group.begin_back(blocks_of(d_own[1] + got[1].astype(F32)))
+            moved, d_first = lax.optimization_barrier((group.first_back(give), d_first))
+            d_last = group.end_back(keep, moved)
             d_late, gain_late = back_to_positions(d_last, 1)
-            held = [by_position(v)[:, None] for v in held]
-            low = d_middle.astype(BF16)
             d_middle = [d_middle, d_late]
             lows = [low, d_late.astype(BF16)]
-            return grad, d_middle, lows, group.swap(low), gain_part + gain_late, out_other, normed, held
+            return grad, d_middle, lows, d_first, gain_part + gain_late, out_other, normed, held
 
         grad, d_middle, d_middle_low, d_first, ffn_gain_part, out_other, normed_rows, context_rows = region(
             item_bounds[0] >= 0,
@@ -692,7 +700,7 @@
         ffn_rows = [[block] for block in group.gather(ffn_own[0])]
         d_parts, out_parts = [], []
         for r in range(mp):
-            (hidden, d_gate_up, d_part, out_part), _ = feed(r, step, ffn_rows[r], cot_rows[r])
+            (hidden, d_gate_up, d_part, out_part), _, _ = feed(r, step, ffn_rows[r], cot_rows[r])
             d_parts.append(d_part[0])
             out_parts.append(out_part)
             step = ffn_grad(cot_rows[r], ffn_rows[r], hidden, d_gate_up, outer)
@@ -707,8 +715,8 @@
         blocks = whole.reshape(whole.shape[:-2] + (size, depth // size, n))
         return group.in_order(group.spread(jnp.moveaxis(blocks, -3, 0)))
 
-    def ffn_grads(sums):
-        done = jnp.stack(group.by_index([finish(v) for v in sums])).astype(F32)
+    def ffn_grads(done):
+        done = jnp.stack(group.by_index(done)).astype(F32)
         done = done.reshape((positions,) + done.shape[2:])
         return done[:, 0], done[:, 1:]
 
@@ -775,13 +783,16 @@
             out_parts[1],
         )
         ffn_sums[1], own_parts[0] = lax.optimization_barrier((ffn_sums[1], own_parts[0]))
-        qkv_part, out_part = tied(ffn_sums[1], qkv_part, out_part)
-        qkv_sums, out_sums = sum_lines(qkv_part), sum_lines(out_part)
+        qkv_sums = sum_lines(tied(ffn_sums[1], qkv_part)[0])
 
         def others(own_parts, other_parts, out_own, sent, middle, d_middle, sums, gain_part):
-            d_normed_a = [group.scatter([own_parts[c], other_parts[c]]) for c in range(chunks)]
+            got = [group.swap(block) for block in other_parts]
+            done = [finish(v) for v in sums]
+            got[1], done[0] = lax.optimization_barrier((got[1], done[0]))
+            done[1], gain_part = lax.optimization_barrier((done[1], gain_part))
+            d_normed_a = [own_parts[c] + got[c].astype(F32) for c in range(chunks)]
             out_rows = [out_own[c] + sent[c].astype(F32) for c in range(chunks)]
-            return ffn_grads(sums), *ends(d_normed_a, out_rows, middle, d_middle, gain_part)
+            return ffn_grads(done), *ends(d_normed_a, out_rows, middle, d_middle, gain_part)
 
         (down_grad, gate_up_grad), mixed, input_grad, attn_gain_grad, ffn_gain_grad = region(
             item_bounds[0] >= 0,
@@ -795,7 +806,8 @@
             ffn_sums,
             ffn_gain_part,
         )
-        qkv_sums, out_sums, attn_gain_grad = lax.optimization_barrier((qkv_sums, out_sums, attn_gain_grad))
+        qkv_sums, out_part, attn_gain_grad = lax.optimization_barrier((qkv_sums, out_part, attn_gain_grad))
+        out_sums = sum_lines(out_part)
     else:
         d_qkv, own_part, _ = attention_bwd(info, *d_middle_two[0], qkv[0], probs[0], w_qkv, w_out)
         d_normed_a = [lax.psum_scatter(own_part, "mp", scatter_dimension=0, tiled=True)]
@@ -803,7 +815,7 @@
         qkv_part = weight_grad(normed_rows, [by_position(d_qkv)], outer)
         out_rows = [group.scatter([out_parts[r][0] for r in range(mp)])]
         qkv_sums, out_sums = sum_lines(qkv_part), sum_lines(out_part)
-        down_grad, gate_up_grad = ffn_grads(ffn_sums)
+        down_grad, gate_up_grad = ffn_grads([finish(v) for v in ffn_sums])
         mixed, input_grad, attn_gain_grad, ffn_gain_grad = ends(
             d_normed_a, out_rows, middle, d_middle, ffn_gain_part
         )

time: 716 us -> 701 us (0.979)
  waiting for transfers between devices: 251 us -> 223 us
  starting transfers between devices: 51.2 us -> 62.8 us
    ppermute x18, waiting for transfers between devices: 73.6 us -> 44 us  [swap(): return lax.ppermute(block, 'mp', [(0, 1), (1, 0)])]
    ppermute x16, waiting for transfers between devices: 141 us -> 112 us  [end(): lax.ppermute(give, 'dp', self.route(self.size // 2))]
    reduce_scatter x4, waiting for transfers between devices: 13.8 us -> 38.4 us  [sum_lines(): lax.psum_scatter(part, 'dp', scatter_dimension=0, axis_index_groups=lines...]
    cond x95 -> x99, local copies, waits for them, and re-layouts: 20.5 us -> 23.6 us
  transfers between devices with their start and end apart: 68 -> 68, of which waited for: 31 -> 31; matrix products, arithmetic and copies ran while one was open for 21% -> 21% of each run, Pallas kernels for 28% -> 29%
where the time goes in v4:
time: 701 us; the launch traced here: 691 us
  waiting for transfers between devices  223 us (32%)
  Pallas kernels  218 us (31%)
  other arithmetic  109 us (16%)
  starting transfers between devices  62.8 us (9%)
  local copies, waits for them, and re-layouts  60.3 us (9%)
  between operations  15.1 us (2%)
    pallas_call x12, Pallas kernels, call(): pl.pallas_call(kernel, grid_spec=pltpu.PrefetchScalarGridSpec(num_scalar_...  218 us
    ppermute x16, waiting for transfers between devices, end(): lax.ppermute(give, 'dp', self.route(self.size // 2))  112 us
    ppermute x18, waiting for transfers between devices, swap(): return lax.ppermute(block, 'mp', [(0, 1), (1, 0)])  44 us
    reduce_scatter x4, waiting for transfers between devices, sum_lines(): lax.psum_scatter(part, 'dp', scatter_dimension=0, axis_index_groups=lines...  38.4 us
    ppermute x18, starting transfers between devices, swap(): return lax.ppermute(block, 'mp', [(0, 1), (1, 0)])  24 us
    cond x99, local copies, waits for them, and re-layouts  23.6 us
    concatenate x12, other arithmetic, end(): jnp.concatenate([keep, lax.ppermute(give, 'dp', self.route(self.size // 2...  21.7 us
    ppermute x16, starting transfers between devices, end(): lax.ppermute(give, 'dp', self.route(self.size // 2))  19.9 us
  transfers between devices with their start and end apart: 68, of which 31 were waited for; matrix products, arithmetic and copies ran while one was open for 21% of the time, Pallas kernels for 29%

profile of v4, /device:TPU:0, one launch (start us, length us, event | category | flops | bytes accessed | tf_op | source)
XLA Modules:
  0.0 690.6 jit_solution(18060374630311902777)
XLA Ops:
  8.1 2.4 collective-permute-start.49
  11.9 2.3 collective-permute-start.50
  14.2 2.8 fusion.103
  30.0 3.6 fusion.77
  33.5 2.5 fusion.91
  36.5 6.2 collective-permute-done.52
  44.3 2.4 fusion.80.other
  46.8 19.8 %attention_fwd.2 = (bf16[8,128,1024]{2,1,0:T(8,128)(2,1)}, bf16[8,3,8,64,128]{4,3,2,1,0:T(8,128)(2,1)}, f32[8,8,8,128]{3,2,1,0:T(8,128)}, bf16[8,128,512]{2,1,0:...) custom-call(s32[2]{0:T(128)S(1)} %pad_add_fusion.1.info, ...), custom_call_target="tpu_custom_call" | custom-call | flops 429496729600 | bytes 4538369024 | tf_op jit(solution)/shard_map/attention_fwd/pallas_call | solution.py:155
  69.3 2.4 fusion.74.other
  71.7 19.6 %attention_fwd.3 = (bf16[8,128,1024]{2,1,0:T(8,128)(2,1)}, bf16[8,3,8,64,128]{4,3,2,1,0:T(8,128)(2,1)}, f32[8,8,8,128]{3,2,1,0:T(8,128)}, bf16[8,128,512]{2,1,0:...) custom-call(s32[2]{0:T(128)S(1)} %pad_add_fusion.1.info, ...), custom_call_target="tpu_custom_call" | custom-call | flops 429496729600 | bytes 4538369024 | tf_op jit(solution)/shard_map/attention_fwd/pallas_call | solution.py:155
  97.9 2.4 pad_maximum_fusion.27
  103.2 16.0 %collective-permute-done.59 = bf16[4,128,1024]{2,1,0:T(8,128)(2,1)} collective-permute-done((bf16[4,128,1024]{2,1,0:T(8,128)(2,1)S(1)}, bf16[4,128,1024]{2,1,0:T(8,128)(2,1)}, u32[]{:S(2)}, u32[]{:S(2)}) %collective-permute-start.59) | collective-permute-done | bytes 1048608 | tf_op jit(solution)/shard_map/ppermute | solution.py:56
  122.7 67.2 %conditional.4 = (bf16[4,3,256,1408]{3,2,1,0:T(8,128)(2,1)}, bf16[512,1024]{1,0:T(8,128)(2,1)}, bf16[512,1024]{1,0:T(8,128)(2,1)}, bf16[512,1024]{1,0:T(8,128)(2...) conditional(s32[]{:T(128)} %convert_element_type.132, () %tuple.82, ...), branch_computations={%region_2.3_spmd, %region_3.4_spmd} | conditional | flops 2657512062976 | bytes 18158192640 | solution.py:39
  128.0 16.6 %feed_forward.4 = (bf16[512,1408]{1,0:T(8,128)(2,1)}, bf16[2,512,1408]{2,1,0:T(8,128)(2,1)}, f32[512,1024]{1,0:T(8,128)}, f32[512,1024]{1,0:T(8,128)}) custom-call(s32[1]{0:T(128)} %bitcast.5.info, bf16[512,1024]{1,0:T(8,128)(2,1)} %bitcast.rows.refs_2_, bf16[512,1024]{1,0:T(8,128)(2,1)} %get-tuple-element.158.cot.refs_0_, ...), custom_call_target="tpu_custom_call" | custom-call | flops 885837004800 | bytes 7982285312 | tf_op jit(solution)/shard_map/cond/branch_1_fun/feed_forward/pallas_call | solution.py:155
  144.6 2.1 pad_maximum_fusion
  146.8 16.8 %feed_forward.5 = (bf16[512,1408]{1,0:T(8,128)(2,1)}, bf16[2,512,1408]{2,1,0:T(8,128)(2,1)}, f32[512,1024]{1,0:T(8,128)}, f32[512,1024]{1,0:T(8,128)}) custom-call(s32[1]{0:T(128)} %bitcast.5.info, bf16[512,1024]{1,0:T(8,128)(2,1)} %bitcast.4.rows.refs_3_, bf16[512,1024]{1,0:T(8,128)(2,1)} %get-tuple-element.163.cot.refs_1_, ...), custom_call_target="tpu_custom_call" | custom-call | flops 885837004800 | bytes 7982285312 | tf_op jit(solution)/shard_map/cond/branch_1_fun/feed_forward/pallas_call | solution.py:155
  163.5 8.2 %collective-permute-done.2 = bf16[512,1024]{1,0:T(8,128)(2,1)} collective-permute-done((bf16[512,1024]{1,0:T(8,128)(2,1)}, bf16[512,1024]{1,0:T(8,128)(2,1)}, u32[]{:S(2)}, u32[]{:S(2)}) %collective-permute-start.2) | collective-permute-done | bytes 1048608 | tf_op jit(solution)/shard_map/cond/branch_1_fun/ppermute | solution.py:56
  173.1 16.8 %ffn_grad.2 = bf16[4,3,256,1408]{3,2,1,0:T(8,128)(2,1)} custom-call(bf16[512,1024]{1,0:T(8,128)(2,1)} %get-tuple-element.158.cot.refs_0_, bf16[512,1024]{1,0:T(8,128)(2,1)} %get-tuple-element.163.cot.refs_1_, bf16[512,1024]{1,0:T(8,128)(2,1)} %bitcast.rows.refs_2_, bf16[512,1024]{1,0:T(8,128)(2,1)} %bitcast.4.rows.refs_3_, bf16[512,1408]{1,0:T(8,128)(2,1)S(1)} %copy-done.3, ...), custom_call_target="tpu_custom_call" | custom-call | flops 885837004800 | bytes 2149580800 | tf_op jit(solution)/shard_map/cond/branch_1_fun/ffn_grad/pallas_call | solution.py:155
  191.4 157.5 %conditional.5 = (bf16[4,3,256,1408]{3,2,1,0:T(8,128)(2,1)}, f32[4,128,1024]{2,1,0:T(8,128)}, f32[4,128,1024]{2,1,0:T(8,128)}, bf16[4,128,1024]{2,1,0:T(8,128)(2...) conditional(s32[]{:T(128)} %convert_element_type.132, () %tuple.80, ...), branch_computations={%region_5.6_spmd, %region_6.13_spmd} | conditional | flops 2657548763136 | bytes 17917280256 | solution.py:39
  200.1 16.5 %feed_forward.6 = (bf16[512,1408]{1,0:T(8,128)(2,1)}, bf16[2,512,1408]{2,1,0:T(8,128)(2,1)}, bf16[512,1024]{1,0:T(8,128)(2,1)}, bf16[512,1024]{1,0:T(8,128)(2,1)}) custom-call(s32[1]{0:T(128)} %bitcast.6.info, bf16[512,1024]{1,0:T(8,128)(2,1)} %get-tuple-element.182.rows.refs_2_, bf16[512,1024]{1,0:T(8,128)(2,1)} %get-tuple-element.183.cot.refs_0_, ...), custom_call_target="tpu_custom_call" | custom-call | flops 885837004800 | bytes 7772570112 | tf_op jit(solution)/shard_map/cond/branch_1_fun/feed_forward/pallas_call | solution.py:155
  216.6 7.9 %collective-permute-done.18 = bf16[1,2,2,128,1024]{4,3,1,2,0:T(8,128)(2,1)} collective-permute-done((bf16[1,2,2,128,1024]{4,3,1,2,0:T(8,128)(2,1)}, bf16[1,2,2,128,1024]{4,3,1,2,0:T(8,128)(2,1)}, u32[]{:S(2)}, u32[]{:S(2)}) %collective-permute-start.18) | collective-permute-done | bytes 1048608 | tf_op jit(solution)/shard_map/cond/branch_1_fun/ppermute | solution.py:96
  224.5 2.8 pad_maximum_fusion.1
  234.2 2.7 fusion.16
  236.9 4.7 collective-permute-done.16.rows.refs_3_
  241.6 2.8 collective-permute-done.22
  245.4 9.4 %collective-permute-done.20 = bf16[1,2,2,128,512]{4,3,1,2,0:T(8,128)(2,1)S(1)} collective-permute-done((bf16[1,2,2,128,512]{4,3,1,2,0:T(8,128)(2,1)S(1)}, bf16[1,2,2,128,512]{4,3,1,2,0:T(8,128)(2,1)S(1)}, u32[]{:S(2)}, u32[]{:S(2)}) %collective-permute-start.20) | collective-permute-done | bytes 524320 | tf_op jit(solution)/shard_map/cond/branch_1_fun/ppermute | solution.py:96
  257.4 16.5 %feed_forward.7 = (bf16[512,1408]{1,0:T(8,128)(2,1)}, bf16[2,512,1408]{2,1,0:T(8,128)(2,1)}, bf16[512,1024]{1,0:T(8,128)(2,1)}, bf16[512,1024]{1,0:T(8,128)(2,1)}) custom-call(s32[1]{0:T(128)} %bitcast.6.info, bf16[512,1024]{1,0:T(8,128)(2,1)} %collective-permute-done.16.rows.refs_3_, bf16[512,1024]{1,0:T(8,128)(2,1)} %collective-permute-done.15.cot.refs_1_, ...), custom_call_target="tpu_custom_call" | custom-call | flops 885837004800 | bytes 7772570112 | tf_op jit(solution)/shard_map/cond/branch_1_fun/feed_forward/pallas_call | solution.py:155
  275.5 5.2 collective-permute-done.24
  280.7 2.8 pad_maximum_fusion.2
  283.4 2.3 add_convert_fusion.1
  289.9 18.1 %ffn_grad.3 = bf16[4,3,256,1408]{3,2,1,0:T(8,128)(2,1)} custom-call(bf16[512,1024]{1,0:T(8,128)(2,1)} %get-tuple-element.183.cot.refs_0_, bf16[512,1024]{1,0:T(8,128)(2,1)} %collective-permute-done.15.cot.refs_1_, bf16[512,1024]{1,0:T(8,128)(2,1)} %get-tuple-element.182.rows.refs_2_, bf16[512,1024]{1,0:T(8,128)(2,1)} %collective-permute-done.16.rows.refs_3_, ...), custom_call_target="tpu_custom_call" | custom-call | flops 885837004800 | bytes 2149580800 | tf_op jit(solution)/shard_map/cond/branch_1_fun/ffn_grad/pallas_call | solution.py:155
  309.1 2.6 multiply_reduce_fusion
  314.3 2.4 fusion.98
  318.4 2.2 add_convert_fusion
  321.3 13.6 %collective-permute-done.29 = bf16[2,1,128,1024]{3,2,1,0:T(8,128)(2,1)S(1)} collective-permute-done((bf16[2,1,128,1024]{3,2,1,0:T(8,128)(2,1)S(1)}, bf16[2,1,128,1024]{3,2,1,0:T(8,128)(2,1)S(1)}, u32[]{:S(2)}, u32[]{:S(2)}) %collective-permute-start.29) | collective-permute-done | bytes 524320 | tf_op jit(solution)/shard_map/cond/branch_1_fun/ppermute | solution.py:106
  334.9 7.7 %collective-permute-done.30 = bf16[4,128,1024]{2,1,0:T(8,128)(2,1)} collective-permute-done((bf16[4,128,1024]{2,1,0:T(8,128)(2,1)}, bf16[4,128,1024]{2,1,0:T(8,128)(2,1)}, u32[]{:S(2)}, u32[]{:S(2)}) %collective-permute-start.30) | collective-permute-done | bytes 1048608 | tf_op jit(solution)/shard_map/cond/branch_1_fun/ppermute | solution.py:56
  346.1 2.4 fusion.96
  349.9 156.6 %conditional.6 = (bf16[4,2,3,256,512]{4,3,2,1,0:T(8,128)(2,1)}, bf16[4,2,1,256,512]{4,3,2,1,0:T(8,128)(2,1)}, f32[4,128,1024]{2,1,0:T(8,128)}, f32[4,128,1024]{2...) conditional(s32[]{:T(128)} %convert_element_type.132, () %tuple.79, ...), branch_computations={%region_13.14_spmd, %region_14.15_spmd} | conditional | flops 1718001598464 | bytes 11795433472 | solution.py:39
  357.9 24.3 %attention_bwd.2 = (bf16[8,3,128,512]{3,2,1,0:T(8,128)(2,1)}, f32[4,128,1024]{2,1,0:T(8,128)}, bf16[4,128,1024]{2,1,0:T(8,128)(2,1)}) custom-call(s32[2]{0:T(128)S(1)} %get-tuple-element.231.info, bf16[4,128,1024]{2,1,0:T(8,128)(2,1)} %get-tuple-element.237.own, bf16[4,128,1024]{2,1,0:T(8,128)(2,1)} %get-tuple-element.238.other, ...), custom_call_target="tpu_custom_call" | custom-call | flops 429496729600 | bytes 4535092224 | tf_op jit(solution)/shard_map/cond/branch_1_fun/attention_bwd/pallas_call | solution.py:155
  392.2 23.5 %attention_bwd.3 = (bf16[8,3,128,512]{3,2,1,0:T(8,128)(2,1)}, f32[4,128,1024]{2,1,0:T(8,128)}, bf16[4,128,1024]{2,1,0:T(8,128)(2,1)}) custom-call(s32[2]{0:T(128)S(1)} %get-tuple-element.231.info, bf16[4,128,1024]{2,1,0:T(8,128)(2,1)} %get-tuple-element.247.own, bf16[4,128,1024]{2,1,0:T(8,128)(2,1)} %collective-permute-done.6.other, ...), custom_call_target="tpu_custom_call" | custom-call | flops 429496729600 | bytes 4535092224 | tf_op jit(solution)/shard_map/cond/branch_1_fun/attention_bwd/pallas_call | solution.py:155
  415.6 12.2 %collective-permute-done.8 = bf16[1,2,2,3,128,512]{5,4,1,3,2,0:T(8,128)(2,1)} collective-permute-done((bf16[1,2,2,3,128,512]{5,4,1,3,2,0:T(8,128)(2,1)}, bf16[1,2,2,3,128,512]{5,4,1,3,2,0:T(8,128)(2,1)}, u32[]{:S(2)}, u32[]{:S(2)}) %collective-permute-start.8) | collective-permute-done | bytes 1572896 | tf_op jit(solution)/shard_map/cond/branch_1_fun/ppermute | solution.py:96
  427.8 2.0 pad_maximum_fusion.9
  431.0 3.3 collective-permute-done.10
  441.9 29.2 %collective-permute-done.11 = bf16[1,2,2,3,128,512]{5,4,1,3,2,0:T(8,128)(2,1)S(1)} collective-permute-done((bf16[1,2,2,3,128,512]{5,4,1,3,2,0:T(8,128)(2,1)S(1)}, bf16[1,2,2,3,128,512]{5,4,1,3,2,0:T(8,128)(2,1)S(1)}, u32[]{:S(2)}, u32[]{:S(2)}) %collective-permute-start.11) | collective-permute-done | bytes 1572896 | tf_op jit(solution)/shard_map/cond/branch_1_fun/ppermute | solution.py:96
  473.9 21.9 %weight_grad.2 = bf16[4,2,3,256,512]{4,3,2,1,0:T(8,128)(2,1)} custom-call(bf16[2,512,1024]{2,1,0:T(8,128)(2,1)} %get-tuple-element.229.refs_0_, bf16[2,512,1024]{2,1,0:T(8,128)(2,1)} %get-tuple-element.230.refs_1_, bf16[2,3,512,512]{3,2,1,0:T(8,128)(2,1)S(1)} %bitcast.495, bf16[2,3,512,512]{3,2,1,0:T(8,128)(2,1)} %bitcast.513), custom_call_target="tpu_custom_call" | custom-call | flops 644245094400 | bytes 1677721600 | tf_op jit(solution)/shard_map/cond/branch_1_fun/weight_grad/pallas_call | solution.py:155
  495.7 2.1 collective-permute-done.13
  499.3 7.2 %weight_grad.3 = bf16[4,2,1,256,512]{4,3,2,1,0:T(8,128)(2,1)} custom-call(bf16[2,512,1024]{2,1,0:T(8,128)(2,1)S(1)} %bitcast.496, bf16[2,512,1024]{2,1,0:T(8,128)(2,1)S(1)} %bitcast.497, bf16[2,1,512,512]{3,2,1,0:T(8,128)(2,1)} %get-tuple-element.262.refs_2_, bf16[2,1,512,512]{3,2,1,0:T(8,128)(2,1)} %get-tuple-element.263.refs_3_), custom_call_target="tpu_custom_call" | custom-call | flops 214748364800 | bytes 838860800 | tf_op jit(solution)/shard_map/cond/branch_1_fun/weight_grad/pallas_call | solution.py:155
  508.4 116.3 %conditional.7 = (f32[8,64,1408]{2,1,0:T(8,128)}, f32[8,2,64,1408]{3,2,1,0:T(8,128)}, bf16[4,256,1024]{2,1,0:T(8,128)(2,1)}, f32[4,256,1024]{2,1,0:T(8,128)}, f32[4,64]{1,0:T(4,128)S(1)}, /*index=5*/f32[4,64]{1,0:T(4,128)S(1)}) conditional(s32[]{:T(128)} %convert_element_type.132, () %tuple.78, (s32[]{:T(128)}, bf16[4,128,1024]{2,1,0:T(8,128)(2,1)}, ...), branch_computations={%region_16.17_spmd, %region_17.24_spmd} | conditional | flops 62505492 | bytes 322650304 | solution.py:39
  508.6 2.2 add_convert_fusion.5
  513.4 2.7 add_convert_fusion.3
  521.4 2.7 constant_dynamic-slice_fusion.18
  529.5 2.4 copy.264
  546.5 21.1 %collective-permute-done.34 = bf16[1,2,3,64,1408]{4,3,2,1,0:T(8,128)(2,1)S(1)} collective-permute-done((bf16[1,2,3,64,1408]{4,3,2,1,0:T(8,128)(2,1)S(1)}, bf16[1,2,3,64,1408]{4,3,2,1,0:T(8,128)(2,1)S(1)}, u32[]{:S(2)}, u32[]{:S(2)}) %collective-permute-start.34) | collective-permute-done | bytes 1081376 | tf_op jit(solution)/shard_map/cond/branch_1_fun/ppermute | solution.py:96
  569.1 4.4 fusion.46
  573.5 16.7 %collective-permute-done.36 = bf16[1,2,3,64,1408]{4,3,2,1,0:T(8,128)(2,1)S(1)} collective-permute-done((bf16[1,2,3,64,1408]{4,3,2,1,0:T(8,128)(2,1)S(1)}, bf16[1,2,3,64,1408]{4,3,2,1,0:T(8,128)(2,1)S(1)}, u32[]{:S(2)}, u32[]{:S(2)}) %collective-permute-start.36) | collective-permute-done | bytes 1081376 | tf_op jit(solution)/shard_map/cond/branch_1_fun/ppermute | solution.py:96
  591.6 2.6 collective-permute-start.43
  596.4 3.4 copy-done.11
  603.2 4.6 fusion.43
  612.8 5.9 slice.408
  621.7 2.8 pad_add_fusion
  626.4 2.7 collective-permute-start.60
  631.1 2.2 collective-permute-start.61
  633.3 38.3 %reduce-scatter.11.cloned.1.call-done = bf16[1,2,1,256,512]{4,3,2,1,0:T(8,128)(2,1)} async-done(((bf16[4,2,1,256,512]{4,3,2,1,0:T(8,128)(2,1)}), bf16[1,2,1,256,512]{4,3,2,1,0:T(8,128)(2,1)}) %reduce-scatter.11.cloned.1.call-update) | async-done | bytes 524304 | tf_op jit(solution)/shard_map/reduce_scatter | solution.py:594
  678.0 4.8 collective-permute-done.63
  (408 shorter events, 162.9 us)
Async XLA Ops:
  7.2 341.8 %reduce-scatter.5.cloned.1.call-start = ((), (), s32[]{:S(2)}) async-start(), calls=%async_computation.4 | async-start | bytes 10813440 | tf_op jit(solution)/shard_map/reduce_scatter | solution.py:594
  8.1 16.6 %collective-permute-start.49 = (bf16[4,2,1024]{2,1,0:T(2,128)(2,1)S(1)}, bf16[4,2,1024]{2,1,0:T(2,128)(2,1)S(1)}, u32[]{:S(2)}, u32[]{:S(2)}) collective-permute-start(bf16[4,2,1024]{2,1,0:T(2,128)(2,1)S(1)} %slice.362), channel_id=1, source_target_pairs={{0,2},{2,4},{4,6},{6,8},{8,10},{10,12},{12,14},{14,16},{16,18},{18... | collective-permute-start | bytes 49160 | tf_op jit(solution)/shard_map/ppermute | solution.py:26
  11.9 14.4 %collective-permute-start.50 = (f32[4,1152]{1,0:T(4,128)S(1)}, f32[4,1152]{1,0:T(4,128)S(1)}, u32[]{:S(2)}, u32[]{:S(2)}) collective-permute-start(f32[4,1152]{1,0:T(4,128)S(1)} %pad_maximum_fusion.31), channel_id=1, source_target_pairs={{0,1},{1,0},{2,3},{3,2},{4,5},{5,4},{6,7},{7,6},{8,9},{9,8},{10,11... | collective-permute-start | bytes 55304 | tf_op jit(solution)/shard_map/ppermute | solution.py:56
  17.0 25.7 %collective-permute-start.52 = (bf16[4,128,1024]{2,1,0:T(8,128)(2,1)S(1)}, bf16[4,128,1024]{2,1,0:T(8,128)(2,1)}, u32[]{:S(2)}, u32[]{:S(2)}) collective-permute-start(bf16[4,128,1024]{2,1,0:T(8,128)(2,1)S(1)} %get-tuple-element.374), channel_id=1, source_target_pairs={{0,1},{1,0},{2,3},{3,2},{4,5},{5,4},{6,7},{7,6},{8,9},{9,8},{10,11... | collective-permute-start | bytes 3145736 | tf_op jit(solution)/shard_map/ppermute | solution.py:56
  19.9 13.6 %collective-permute-start.47 = (bf16[2,1,128,1024]{3,2,1,0:T(8,128)(2,1)}, bf16[2,1,128,1024]{3,2,1,0:T(8,128)(2,1)}, u32[]{:S(2)}, u32[]{:S(2)}) collective-permute-start(bf16[2,1,128,1024]{3,2,1,0:T(8,128)(2,1)} %get-tuple-element.590), channel_id=1, source_target_pairs={{0,2},{2,0},{4,6},{6,4},{8,10},{10,8},{12,14},{14,12},{16,18},{18,... | collective-permute-start | bytes 1572872 | tf_op jit(solution)/shard_map/ppermute | solution.py:89
  22.7 4.5 collective-permute-start.53
  24.7 19.6 %collective-permute-start.51 = (bf16[4,2,1024]{2,1,0:T(2,128)(2,1)S(1)}, bf16[4,2,1024]{2,1,0:T(2,128)(2,1)S(1)}, u32[]{:S(2)}, u32[]{:S(2)}) collective-permute-start(bf16[4,2,1024]{2,1,0:T(2,128)(2,1)S(1)} %collective-permute-done.49), channel_id=1, source_target_pairs={{0,1},{1,0},{2,3},{3,2},{4,5},{5,4},{6,7},{7,6},{8,9},{9,8},{10,11... | collective-permute-start | bytes 49160 | tf_op jit(solution)/shard_map/ppermute | solution.py:56
  28.3 14.8 %collective-permute-start.54 = (bf16[1,2,128,1024]{3,2,1,0:T(8,128)(2,1)S(1)}, bf16[1,2,128,1024]{3,2,1,0:T(8,128)(2,1)S(1)}, u32[]{:S(2)}, u32[]{:S(2)}) collective-permute-start(bf16[1,2,128,1024]{3,2,1,0:T(8,128)(2,1)S(1)} %get-tuple-element.585), channel_id=1, source_target_pairs={{0,4},{2,6},{4,0},{6,2},{8,12},{10,14},{12,8},{14,10},{16,20},{18,... | collective-permute-start | bytes 1572872 | tf_op jit(solution)/shard_map/ppermute | solution.py:96
  36.0 61.9 %collective-permute-start.48 = (bf16[1,2,128,1024]{3,2,1,0:T(8,128)(2,1)}, bf16[1,2,128,1024]{3,2,1,0:T(8,128)(2,1)}, u32[]{:S(2)}, u32[]{:S(2)}) collective-permute-start(bf16[1,2,128,1024]{3,2,1,0:T(8,128)(2,1)} %get-tuple-element.589), channel_id=1, source_target_pairs={{0,4},{2,6},{4,0},{6,2},{8,12},{10,14},{12,8},{14,10},{16,20},{18,... | collective-permute-start | bytes 1572872 | tf_op jit(solution)/shard_map/ppermute | solution.py:96
  42.7 26.5 %collective-permute-start.56 = (bf16[4,128,1024]{2,1,0:T(8,128)(2,1)}, bf16[4,128,1024]{2,1,0:T(8,128)(2,1)}, u32[]{:S(2)}, u32[]{:S(2)}) collective-permute-start(bf16[4,128,1024]{2,1,0:T(8,128)(2,1)} %get-tuple-element.380), channel_id=1, source_target_pairs={{0,1},{1,0},{2,3},{3,2},{4,5},{5,4},{6,7},{7,6},{8,9},{9,8},{10,11... | collective-permute-start | bytes 3145736 | tf_op jit(solution)/shard_map/ppermute | solution.py:56
  66.6 25.9 %collective-permute-start.55 = (bf16[4,128,1024]{2,1,0:T(8,128)(2,1)}, bf16[4,128,1024]{2,1,0:T(8,128)(2,1)}, u32[]{:S(2)}, u32[]{:S(2)}) collective-permute-start(bf16[4,128,1024]{2,1,0:T(8,128)(2,1)} %get-tuple-element.378), channel_id=1, source_target_pairs={{0,1},{1,0},{2,3},{3,2},{4,5},{5,4},{6,7},{7,6},{8,9},{9,8},{10,11... | collective-permute-start | bytes 3145736 | tf_op jit(solution)/shard_map/ppermute | solution.py:56
  94.2 25.0 %collective-permute-start.59 = (bf16[4,128,1024]{2,1,0:T(8,128)(2,1)S(1)}, bf16[4,128,1024]{2,1,0:T(8,128)(2,1)}, u32[]{:S(2)}, u32[]{:S(2)}) collective-permute-start(bf16[4,128,1024]{2,1,0:T(8,128)(2,1)S(1)} %get-tuple-element.384), channel_id=1, source_target_pairs={{0,1},{1,0},{2,3},{3,2},{4,5},{5,4},{6,7},{7,6},{8,9},{9,8},{10,11... | collective-permute-start | bytes 3145736 | tf_op jit(solution)/shard_map/ppermute | solution.py:56
  97.3 3.0 collective-permute-start.57
  101.4 19.8 %collective-permute-start.58 = (bf16[1,2,128,1024]{3,2,1,0:T(8,128)(2,1)S(1)}, bf16[1,2,128,1024]{3,2,1,0:T(8,128)(2,1)S(1)}, u32[]{:S(2)}, u32[]{:S(2)}) collective-permute-start(bf16[1,2,128,1024]{3,2,1,0:T(8,128)(2,1)S(1)} %get-tuple-element.581), channel_id=1, source_target_pairs={{0,4},{2,6},{4,0},{6,2},{8,12},{10,14},{12,8},{14,10},{16,20},{18,... | collective-permute-start | bytes 1572872 | tf_op jit(solution)/shard_map/ppermute | solution.py:96
  123.3 2.2 collective-permute-start
  123.3 40.2 %collective-permute-start.3 = (bf16[512,1024]{1,0:T(8,128)(2,1)}, bf16[512,1024]{1,0:T(8,128)(2,1)}, u32[]{:S(2)}, u32[]{:S(2)}) collective-permute-start(bf16[512,1024]{1,0:T(8,128)(2,1)} %bitcast.rows.refs_2_), channel_id=1, source_target_pairs={{0,1},{1,0},{2,3},{3,2},{4,5},{5,4},{6,7},{7,6},{8,9},{9,8},{10,11... | collective-permute-start | bytes 3145736 | tf_op jit(solution)/shard_map/cond/branch_1_fun/ppermute | solution.py:56
  125.1 46.6 %collective-permute-start.2 = (bf16[512,1024]{1,0:T(8,128)(2,1)}, bf16[512,1024]{1,0:T(8,128)(2,1)}, u32[]{:S(2)}, u32[]{:S(2)}) collective-permute-start(bf16[512,1024]{1,0:T(8,128)(2,1)} %get-tuple-element.158.cot.refs_0_), channel_id=1, source_target_pairs={{0,1},{1,0},{2,3},{3,2},{4,5},{5,4},{6,7},{7,6},{8,9},{9,8},{10,11... | collective-permute-start | bytes 3145736 | tf_op jit(solution)/shard_map/cond/branch_1_fun/ppermute | solution.py:56
  126.5 18.1 %collective-permute-start.1 = (bf16[1,2,128,1024]{3,2,1,0:T(8,128)(2,1)}, bf16[1,2,128,1024]{3,2,1,0:T(8,128)(2,1)}, u32[]{:S(2)}, u32[]{:S(2)}) collective-permute-start(bf16[1,2,128,1024]{3,2,1,0:T(8,128)(2,1)} %get-tuple-element.457), channel_id=1, source_target_pairs={{0,4},{2,6},{4,0},{6,2},{8,12},{10,14},{12,8},{14,10},{16,20},{18,... | collective-permute-start | bytes 1572872 | tf_op jit(solution)/shard_map/cond/branch_1_fun/ppermute | solution.py:96
  189.8 316.7 %reduce-scatter.7.cloned.1.call-start = ((), (), s32[]{:S(2)}) async-start(), calls=%async_computation.5 | async-start | bytes 10813440 | tf_op jit(solution)/shard_map/reduce_scatter | solution.py:594
  192.8 4.3 collective-permute-start.17
  192.8 44.0 %collective-permute-start.15 = (bf16[512,1024]{1,0:T(8,128)(2,1)}, bf16[512,1024]{1,0:T(8,128)(2,1)}, u32[]{:S(2)}, u32[]{:S(2)}) collective-permute-start(bf16[512,1024]{1,0:T(8,128)(2,1)} %get-tuple-element.175), channel_id=1, source_target_pairs={{0,1},{1,0},{2,3},{3,2},{4,5},{5,4},{6,7},{7,6},{8,9},{9,8},{10,11... | collective-permute-start | bytes 3145736 | tf_op jit(solution)/shard_map/cond/branch_1_fun/ppermute | solution.py:56
  194.5 47.0 %collective-permute-start.16 = (bf16[512,1024]{1,0:T(8,128)(2,1)}, bf16[512,1024]{1,0:T(8,128)(2,1)}, u32[]{:S(2)}, u32[]{:S(2)}) collective-permute-start(bf16[512,1024]{1,0:T(8,128)(2,1)} %get-tuple-element.177), channel_id=1, source_target_pairs={{0,1},{1,0},{2,3},{3,2},{4,5},{5,4},{6,7},{7,6},{8,9},{9,8},{10,11... | collective-permute-start | bytes 3145736 | tf_op jit(solution)/shard_map/cond/branch_1_fun/ppermute | solution.py:56
  197.0 35.3 %collective-permute-start.23 = (bf16[2,1,2,128,1024]{4,3,1,2,0:T(8,128)(2,1)}, bf16[2,1,2,128,1024]{4,3,1,2,0:T(8,128)(2,1)}, u32[]{:S(2)}, u32[]{:S(2)}) collective-permute-start(bf16[2,1,2,128,1024]{4,3,1,2,0:T(8,128)(2,1)} %bitcast.478), channel_id=1, source_target_pairs={{0,2},{2,0},{4,6},{6,4},{8,10},{10,8},{12,14},{14,12},{16,18},{18,... | collective-permute-start | bytes 3145736 | tf_op jit(solution)/shard_map/cond/branch_1_fun/ppermute | solution.py:89
  198.6 25.9 %collective-permute-start.18 = (bf16[1,2,2,128,1024]{4,3,1,2,0:T(8,128)(2,1)}, bf16[1,2,2,128,1024]{4,3,1,2,0:T(8,128)(2,1)}, u32[]{:S(2)}, u32[]{:S(2)}) collective-permute-start(bf16[1,2,2,128,1024]{4,3,1,2,0:T(8,128)(2,1)} %get-tuple-element.187), channel_id=1, source_target_pairs={{0,4},{2,6},{4,0},{6,2},{8,12},{10,14},{12,8},{14,10},{16,20},{18,... | collective-permute-start | bytes 3145736 | tf_op jit(solution)/shard_map/cond/branch_1_fun/ppermute | solution.py:96
  228.7 2.4 collective-permute-start.19
  229.5 14.8 %collective-permute-start.22 = (bf16[1,2,2,128,512]{4,3,1,2,0:T(8,128)(2,1)S(1)}, bf16[1,2,2,128,512]{4,3,1,2,0:T(8,128)(2,1)S(1)}, u32[]{:S(2)}, u32[]{:S(2)}) collective-permute-start(bf16[1,2,2,128,512]{4,3,1,2,0:T(8,128)(2,1)S(1)} %get-tuple-element.555), channel_id=1, source_target_pairs={{0,4},{2,6},{4,0},{6,2},{8,12},{10,14},{12,8},{14,10},{16,20},{18,... | collective-permute-start | bytes 1572872 | tf_op jit(solution)/shard_map/cond/branch_1_fun/ppermute | solution.py:96
  231.2 23.6 %collective-permute-start.20 = (bf16[1,2,2,128,512]{4,3,1,2,0:T(8,128)(2,1)S(1)}, bf16[1,2,2,128,512]{4,3,1,2,0:T(8,128)(2,1)S(1)}, u32[]{:S(2)}, u32[]{:S(2)}) collective-permute-start(bf16[1,2,2,128,512]{4,3,1,2,0:T(8,128)(2,1)S(1)} %get-tuple-element.559), channel_id=1, source_target_pairs={{0,4},{2,6},{4,0},{6,2},{8,12},{10,14},{12,8},{14,10},{16,20},{18,... | collective-permute-start | bytes 1572872 | tf_op jit(solution)/shard_map/cond/branch_1_fun/ppermute | solution.py:96
  232.4 51.0 %collective-permute-start.25 = (bf16[512,1024]{1,0:T(8,128)(2,1)}, bf16[512,1024]{1,0:T(8,128)(2,1)}, u32[]{:S(2)}, u32[]{:S(2)}) collective-permute-start(bf16[512,1024]{1,0:T(8,128)(2,1)} %get-tuple-element.202), channel_id=1, source_target_pairs={{0,1},{1,0},{2,3},{3,2},{4,5},{5,4},{6,7},{7,6},{8,9},{9,8},{10,11... | collective-permute-start | bytes 3145736 | tf_op jit(solution)/shard_map/cond/branch_1_fun/ppermute | solution.py:56
  255.9 24.8 %collective-permute-start.24 = (bf16[1,2,2,128,1024]{4,3,1,2,0:T(8,128)(2,1)}, bf16[1,2,2,128,1024]{4,3,1,2,0:T(8,128)(2,1)}, u32[]{:S(2)}, u32[]{:S(2)}) collective-permute-start(bf16[1,2,2,128,1024]{4,3,1,2,0:T(8,128)(2,1)} %get-tuple-element.200), channel_id=1, source_target_pairs={{0,4},{2,6},{4,0},{6,2},{8,12},{10,14},{12,8},{14,10},{16,20},{18,... | collective-permute-start | bytes 3145736 | tf_op jit(solution)/shard_map/cond/branch_1_fun/ppermute | solution.py:96
  273.9 34.1 %collective-permute-start.27 = (bf16[512,1024]{1,0:T(8,128)(2,1)}, bf16[512,1024]{1,0:T(8,128)(2,1)}, u32[]{:S(2)}, u32[]{:S(2)}) collective-permute-start(bf16[512,1024]{1,0:T(8,128)(2,1)} %get-tuple-element.209), channel_id=1, source_target_pairs={{0,1},{1,0},{2,3},{3,2},{4,5},{5,4},{6,7},{7,6},{8,9},{9,8},{10,11... | collective-permute-start | bytes 3145736 | tf_op jit(solution)/shard_map/cond/branch_1_fun/ppermute | solution.py:56
  288.4 19.6 %collective-permute-start.26 = (bf16[2,1,128,1024]{3,2,1,0:T(8,128)(2,1)}, bf16[2,1,128,1024]{3,2,1,0:T(8,128)(2,1)}, u32[]{:S(2)}, u32[]{:S(2)}) collective-permute-start(bf16[2,1,128,1024]{3,2,1,0:T(8,128)(2,1)} %pad_maximum_fusion.7), channel_id=1, source_target_pairs={{0,4},{2,6},{4,0},{6,2},{8,12},{10,14},{12,8},{14,10},{16,20},{18,... | collective-permute-start | bytes 1572872 | tf_op jit(solution)/shard_map/cond/branch_1_fun/ppermute | solution.py:106
  309.0 2.7 collective-permute-start.28
  316.7 25.9 %collective-permute-start.30 = (bf16[4,128,1024]{2,1,0:T(8,128)(2,1)}, bf16[4,128,1024]{2,1,0:T(8,128)(2,1)}, u32[]{:S(2)}, u32[]{:S(2)}) collective-permute-start(bf16[4,128,1024]{2,1,0:T(8,128)(2,1)} %get-tuple-element.644), channel_id=1, source_target_pairs={{0,1},{1,0},{2,3},{3,2},{4,5},{5,4},{6,7},{7,6},{8,9},{9,8},{10,11... | collective-permute-start | bytes 3145736 | tf_op jit(solution)/shard_map/cond/branch_1_fun/ppermute | solution.py:56
  320.8 14.1 %collective-permute-start.29 = (bf16[2,1,128,1024]{3,2,1,0:T(8,128)(2,1)S(1)}, bf16[2,1,128,1024]{3,2,1,0:T(8,128)(2,1)S(1)}, u32[]{:S(2)}, u32[]{:S(2)}) collective-permute-start(bf16[2,1,128,1024]{3,2,1,0:T(8,128)(2,1)S(1)} %pad_maximum_fusion.8), channel_id=1, source_target_pairs={{0,4},{2,6},{4,0},{6,2},{8,12},{10,14},{12,8},{14,10},{16,20},{18,... | collective-permute-start | bytes 1572872 | tf_op jit(solution)/shard_map/cond/branch_1_fun/ppermute | solution.py:106
  349.0 275.7 %reduce-scatter.9.cloned.1.call-start = ((), (), s32[]{:S(2)}) async-start(), calls=%async_computation.6 | async-start | bytes 7864320 | tf_op jit(solution)/shard_map/reduce_scatter | solution.py:594
  353.0 2.9 collective-permute-start.4
  353.2 31.3 %collective-permute-start.6 = (bf16[4,128,1024]{2,1,0:T(8,128)(2,1)}, bf16[4,128,1024]{2,1,0:T(8,128)(2,1)}, u32[]{:S(2)}, u32[]{:S(2)}) collective-permute-start(bf16[4,128,1024]{2,1,0:T(8,128)(2,1)} %get-tuple-element.247.own), channel_id=1, source_target_pairs={{0,1},{1,0},{2,3},{3,2},{4,5},{5,4},{6,7},{7,6},{8,9},{9,8},{10,11... | collective-permute-start | bytes 3145736 | tf_op jit(solution)/shard_map/cond/branch_1_fun/ppermute | solution.py:56
  357.4 25.5 %collective-permute-start.5 = (bf16[1,2,2,128,1024]{4,3,1,2,0:T(8,128)(2,1)}, bf16[1,2,2,128,1024]{4,3,1,2,0:T(8,128)(2,1)}, u32[]{:S(2)}, u32[]{:S(2)}) collective-permute-start(bf16[1,2,2,128,1024]{4,3,1,2,0:T(8,128)(2,1)} %get-tuple-element.244), channel_id=1, source_target_pairs={{0,4},{2,6},{4,0},{6,2},{8,12},{10,14},{12,8},{14,10},{16,20},{18,... | collective-permute-start | bytes 3145736 | tf_op jit(solution)/shard_map/cond/branch_1_fun/ppermute | solution.py:96
  385.6 3.5 collective-permute-start.7
  385.7 44.2 %collective-permute-start.9 = (bf16[512,1024]{1,0:T(8,128)(2,1)}, bf16[512,1024]{1,0:T(8,128)(2,1)}, u32[]{:S(2)}, u32[]{:S(2)}) collective-permute-start(bf16[512,1024]{1,0:T(8,128)(2,1)} %get-tuple-element.253), channel_id=1, source_target_pairs={{0,1},{1,0},{2,3},{3,2},{4,5},{5,4},{6,7},{7,6},{8,9},{9,8},{10,11... | collective-permute-start | bytes 3145736 | tf_op jit(solution)/shard_map/cond/branch_1_fun/ppermute | solution.py:56
  391.1 36.8 %collective-permute-start.8 = (bf16[1,2,2,3,128,512]{5,4,1,3,2,0:T(8,128)(2,1)}, bf16[1,2,2,3,128,512]{5,4,1,3,2,0:T(8,128)(2,1)}, u32[]{:S(2)}, u32[]{:S(2)}) collective-permute-start(bf16[1,2,2,3,128,512]{5,4,1,3,2,0:T(8,128)(2,1)} %get-tuple-element.252), channel_id=1, source_target_pairs={{0,4},{2,6},{4,0},{6,2},{8,12},{10,14},{12,8},{14,10},{16,20},{18,... | collective-permute-start | bytes 4718600 | tf_op jit(solution)/shard_map/cond/branch_1_fun/ppermute | solution.py:96
  430.9 3.5 collective-permute-start.10
  434.6 36.5 %collective-permute-start.11 = (bf16[1,2,2,3,128,512]{5,4,1,3,2,0:T(8,128)(2,1)S(1)}, bf16[1,2,2,3,128,512]{5,4,1,3,2,0:T(8,128)(2,1)S(1)}, u32[]{:S(2)}, u32[]{:S(2)}) collective-permute-start(bf16[1,2,2,3,128,512]{5,4,1,3,2,0:T(8,128)(2,1)S(1)} %get-tuple-element.461), channel_id=1, source_target_pairs={{0,4},{2,6},{4,0},{6,2},{8,12},{10,14},{12,8},{14,10},{16,20},{18,... | collective-permute-start | bytes 4718600 | tf_op jit(solution)/shard_map/cond/branch_1_fun/ppermute | solution.py:96
  437.7 2.7 collective-permute-start.12
  437.8 61.5 %collective-permute-start.14 = (bf16[512,1024]{1,0:T(8,128)(2,1)}, bf16[512,1024]{1,0:T(8,128)(2,1)}, u32[]{:S(2)}, u32[]{:S(2)}) collective-permute-start(bf16[512,1024]{1,0:T(8,128)(2,1)} %get-tuple-element.258), channel_id=1, source_target_pairs={{0,1},{1,0},{2,3},{3,2},{4,5},{5,4},{6,7},{7,6},{8,9},{9,8},{10,11... | collective-permute-start | bytes 3145736 | tf_op jit(solution)/shard_map/cond/branch_1_fun/ppermute | solution.py:56
  473.0 24.8 %collective-permute-start.13 = (bf16[1,2,2,128,1024]{4,3,1,2,0:T(8,128)(2,1)}, bf16[1,2,2,128,1024]{4,3,1,2,0:T(8,128)(2,1)}, u32[]{:S(2)}, u32[]{:S(2)}) collective-permute-start(bf16[1,2,2,128,1024]{4,3,1,2,0:T(8,128)(2,1)} %get-tuple-element.257), channel_id=1, source_target_pairs={{0,4},{2,6},{4,0},{6,2},{8,12},{10,14},{12,8},{14,10},{16,20},{18,... | collective-permute-start | bytes 3145736 | tf_op jit(solution)/shard_map/cond/branch_1_fun/ppermute | solution.py:96
  506.6 165.0 %reduce-scatter.11.cloned.1.call-start = ((), (), s32[]{:S(2)}) async-start(), calls=%async_computation.7 | async-start | bytes 2621440 | tf_op jit(solution)/shard_map/reduce_scatter | solution.py:594
  512.5 21.7 %collective-permute-start.37 = (bf16[2,1,128,1024]{3,2,1,0:T(8,128)(2,1)}, bf16[2,1,128,1024]{3,2,1,0:T(8,128)(2,1)}, u32[]{:S(2)}, u32[]{:S(2)}) collective-permute-start(bf16[2,1,128,1024]{3,2,1,0:T(8,128)(2,1)} %pad_maximum_fusion.19), channel_id=1, source_target_pairs={{0,4},{2,6},{4,0},{6,2},{8,12},{10,14},{12,8},{14,10},{16,20},{18,... | collective-permute-start | bytes 1572872 | tf_op jit(solution)/shard_map/cond/branch_1_fun/ppermute | solution.py:106
  517.9 18.4 %collective-permute-start.39 = (bf16[2,1,128,1024]{3,2,1,0:T(8,128)(2,1)}, bf16[2,1,128,1024]{3,2,1,0:T(8,128)(2,1)}, u32[]{:S(2)}, u32[]{:S(2)}) collective-permute-start(bf16[2,1,128,1024]{3,2,1,0:T(8,128)(2,1)} %pad_maximum_fusion.20), channel_id=1, source_target_pairs={{0,4},{2,6},{4,0},{6,2},{8,12},{10,14},{12,8},{14,10},{16,20},{18,... | collective-permute-start | bytes 1572872 | tf_op jit(solution)/shard_map/cond/branch_1_fun/ppermute | solution.py:106
  519.4 48.8 %collective-permute-start.32 = (bf16[4,128,1024]{2,1,0:T(8,128)(2,1)}, bf16[4,128,1024]{2,1,0:T(8,128)(2,1)}, u32[]{:S(2)}, u32[]{:S(2)}) collective-permute-start(bf16[4,128,1024]{2,1,0:T(8,128)(2,1)} %get-tuple-element.271), channel_id=1, source_target_pairs={{0,1},{1,0},{2,3},{3,2},{4,5},{5,4},{6,7},{7,6},{8,9},{9,8},{10,11... | collective-permute-start | bytes 3145736 | tf_op jit(solution)/shard_map/cond/branch_1_fun/ppermute | solution.py:56
  521.0 47.3 %collective-permute-start.41 = (bf16[4,128,1024]{2,1,0:T(8,128)(2,1)}, bf16[4,128,1024]{2,1,0:T(8,128)(2,1)}, u32[]{:S(2)}, u32[]{:S(2)}) collective-permute-start(bf16[4,128,1024]{2,1,0:T(8,128)(2,1)} %get-tuple-element.292), channel_id=1, source_target_pairs={{0,1},{1,0},{2,3},{3,2},{4,5},{5,4},{6,7},{7,6},{8,9},{9,8},{10,11... | collective-permute-start | bytes 3145736 | tf_op jit(solution)/shard_map/cond/branch_1_fun/ppermute | solution.py:56
  525.2 14.1 %collective-permute-start.33 = (bf16[2,1,3,64,1408]{4,3,2,1,0:T(8,128)(2,1)}, bf16[2,1,3,64,1408]{4,3,2,1,0:T(8,128)(2,1)}, u32[]{:S(2)}, u32[]{:S(2)}) collective-permute-start(bf16[2,1,3,64,1408]{4,3,2,1,0:T(8,128)(2,1)} %bitcast.488), channel_id=1, source_target_pairs={{0,2},{2,0},{4,6},{6,4},{8,10},{10,8},{12,14},{14,12},{16,18},{18,... | collective-permute-start | bytes 3244040 | tf_op jit(solution)/shard_map/cond/branch_1_fun/ppermute | solution.py:89
  536.3 8.4 %collective-permute-start.35 = (bf16[2,1,3,64,1408]{4,3,2,1,0:T(8,128)(2,1)}, bf16[2,1,3,64,1408]{4,3,2,1,0:T(8,128)(2,1)S(1)}, u32[]{:S(2)}, u32[]{:S(2)}) collective-permute-start(bf16[2,1,3,64,1408]{4,3,2,1,0:T(8,128)(2,1)} %bitcast.528), channel_id=1, source_target_pairs={{0,2},{2,0},{4,6},{6,4},{8,10},{10,8},{12,14},{14,12},{16,18},{18,... | collective-permute-start | bytes 3244040 | tf_op jit(solution)/shard_map/cond/branch_1_fun/ppermute | solution.py:89
  538.1 3.4 collective-permute-start.40
  540.8 26.8 %collective-permute-start.34 = (bf16[1,2,3,64,1408]{4,3,2,1,0:T(8,128)(2,1)S(1)}, bf16[1,2,3,64,1408]{4,3,2,1,0:T(8,128)(2,1)S(1)}, u32[]{:S(2)}, u32[]{:S(2)}) collective-permute-start(bf16[1,2,3,64,1408]{4,3,2,1,0:T(8,128)(2,1)S(1)} %get-tuple-element.487), channel_id=1, source_target_pairs={{0,4},{2,6},{4,0},{6,2},{8,12},{10,14},{12,8},{14,10},{16,20},{18,... | collective-permute-start | bytes 3244040 | tf_op jit(solution)/shard_map/cond/branch_1_fun/ppermute | solution.py:96
  545.0 45.2 %collective-permute-start.36 = (bf16[1,2,3,64,1408]{4,3,2,1,0:T(8,128)(2,1)S(1)}, bf16[1,2,3,64,1408]{4,3,2,1,0:T(8,128)(2,1)S(1)}, u32[]{:S(2)}, u32[]{:S(2)}) collective-permute-start(bf16[1,2,3,64,1408]{4,3,2,1,0:T(8,128)(2,1)S(1)} %get-tuple-element.495), channel_id=1, source_target_pairs={{0,4},{2,6},{4,0},{6,2},{8,12},{10,14},{12,8},{14,10},{16,20},{18,... | collective-permute-start | bytes 3244040 | tf_op jit(solution)/shard_map/cond/branch_1_fun/ppermute | solution.py:96
  591.6 10.0 %collective-permute-start.43 = (f32[2,4,512]{2,1,0:T(4,128)S(1)}, f32[2,4,512]{2,1,0:T(4,128)S(1)}, u32[]{:S(2)}, u32[]{:S(2)}) collective-permute-start(f32[2,4,512]{2,1,0:T(4,128)S(1)} %select_bitcast_fusion.10), channel_id=1, source_target_pairs={{0,16},{2,18},{4,20},{6,22},{8,24},{10,26},{12,28},{14,30},{16,0},... | collective-permute-start | bytes 49160 | tf_op jit(solution)/shard_map/cond/branch_1_fun/ppermute | solution.py:140
  602.4 5.5 collective-permute-start.44
  607.9 3.7 collective-permute-start.45
  611.7 8.2 %collective-permute-start.46 = (f32[2,4,64]{2,1,0:T(4,128)S(1)}, f32[2,4,64]{2,1,0:T(4,128)S(1)}, u32[]{:S(2)}, u32[]{:S(2)}) collective-permute-start(f32[2,4,64]{2,1,0:T(4,128)S(1)} %bitcast.544), channel_id=1, source_target_pairs={{0,2},{2,0},{4,6},{6,4},{8,10},{10,8},{12,14},{14,12},{16,18},{18,... | collective-permute-start | bytes 6152 | tf_op jit(solution)/shard_map/cond/branch_1_fun/ppermute | solution.py:140
  618.7 3.1 collective-permute-start.42
  626.4 4.6 collective-permute-start.60
  631.1 44.8 %collective-permute-start.61 = (bf16[1,2,2,3,64,512]{5,4,3,2,1,0:T(8,128)(2,1)S(1)}, bf16[1,2,2,3,64,512]{5,4,3,2,1,0:T(8,128)(2,1)S(1)}, u32[]{:S(2)}, u32[]{:S(2)}) collective-permute-start(bf16[1,2,2,3,64,512]{5,4,3,2,1,0:T(8,128)(2,1)S(1)} %get-tuple-element.577), channel_id=1, source_target_pairs={{0,4},{2,6},{4,0},{6,2},{8,12},{10,14},{12,8},{14,10},{16,20},{18,... | collective-permute-start | bytes 2359304 | tf_op jit(solution)/shard_map/ppermute | solution.py:96
  674.4 8.4 %collective-permute-start.63 = (bf16[1,2,2,1,64,512]{5,4,2,3,1,0:T(8,128)(2,1)S(1)}, bf16[1,2,2,1,64,512]{5,4,2,3,1,0:T(8,128)(2,1)S(1)}, u32[]{:S(2)}, u32[]{:S(2)}) collective-permute-start(bf16[1,2,2,1,64,512]{5,4,2,3,1,0:T(8,128)(2,1)S(1)} %get-tuple-element.597), channel_id=1, source_target_pairs={{0,4},{2,6},{4,0},{6,2},{8,12},{10,14},{12,8},{14,10},{16,20},{18,... | collective-permute-start | bytes 786440 | tf_op jit(solution)/shard_map/ppermute | solution.py:96
  (73 other events, 551.2 us)
Sparse Core Ops, SparseCore 0:
  190.0 149.1 reduce-scatter.4
  349.1 148.9 reduce-scatter.6
  506.7 111.6 reduce-scatter.8
  624.9 46.6 reduce-scatter.10

commit v5 on v4

--- a/solution.py
+++ b/solution.py
@@ -387,7 +387,7 @@
 def ffn(position, rows, cot, w_gate_up, w_down, kind):
     count, width = rows.shape
     units = w_down.shape[2]
-    block = min(count, 256)
+    block = min(count, 512)
     row = lambda i, info: (i, 0)
     return call(
         ffn_kernel,
@@ -533,13 +533,15 @@
 
     own_blocks = [frames_in[:, c * part : (c + 1) * part] for c in range(chunks)]
     rows = size * part
-    *own_blocks, late_cotangent = lax.optimization_barrier((*own_blocks, cotangent))
+    *own_blocks, late_cotangent, last_two, own_gain = lax.optimization_barrier(
+        (*own_blocks, cotangent, frames_in[:, frames - 2 :, :], attn_gain)
+    )
     cot_chunks = [late_cotangent[:, c * part : (c + 1) * part] for c in range(chunks)]
-    earlier = shift_frames(frames_in[:, frames - 2 :, :], 1)
+    earlier = shift_frames(last_two, 1)
     resid = [delayed_chunk(delays, earlier, own_blocks, c) for c in range(chunks)]
     if pair:
         small = jnp.concatenate(
-            [attn_gain, jnp.broadcast_to(delays.astype(F32)[:, None], (local_pos, LANES))], axis=1
+            [own_gain, jnp.broadcast_to(delays.astype(F32)[:, None], (local_pos, LANES))], axis=1
         )
         small = group.swap(small)
         other_blocks = []

time: 701 us -> 699 us (level)
  transfers between devices with their start and end apart: 68 -> 68, of which waited for: 31 -> 32; matrix products, arithmetic and copies ran while one was open for 21% -> 21% of each run, Pallas kernels for 29% -> 29%
where the time goes in v5:
time: 699 us; the launch traced here: 689 us
  waiting for transfers between devices  224 us (32%)
  Pallas kernels  216 us (31%)
  other arithmetic  108 us (15%)
  starting transfers between devices  63.3 us (9%)
  local copies, waits for them, and re-layouts  60.4 us (9%)
  between operations  15.3 us (2%)
    pallas_call x12, Pallas kernels, call(): pl.pallas_call(kernel, grid_spec=pltpu.PrefetchScalarGridSpec(num_scalar_...  216 us
    ppermute x16, waiting for transfers between devices, end(): lax.ppermute(give, 'dp', self.route(self.size // 2))  113 us
    ppermute x18, waiting for transfers between devices, swap(): return lax.ppermute(block, 'mp', [(0, 1), (1, 0)])  43.6 us
    reduce_scatter x4, waiting for transfers between devices, sum_lines(): lax.psum_scatter(part, 'dp', scatter_dimension=0, axis_index_groups=lines...  38.3 us
    cond x99, local copies, waits for them, and re-layouts  23.6 us
    ppermute x18, starting transfers between devices, swap(): return lax.ppermute(block, 'mp', [(0, 1), (1, 0)])  22.9 us
    concatenate x12, other arithmetic, end(): jnp.concatenate([keep, lax.ppermute(give, 'dp', self.route(self.size // 2...  21.6 us
    ppermute x16, starting transfers between devices, end(): lax.ppermute(give, 'dp', self.route(self.size // 2))  21.4 us
  transfers between devices with their start and end apart: 68, of which 32 were waited for; matrix products, arithmetic and copies ran while one was open for 21% of the time, Pallas kernels for 29%

profile of v5, /device:TPU:0, one launch (start us, length us, event | category | flops | bytes accessed | tf_op | source)
XLA Modules:
  0.0 688.8 jit_solution(1094068191328909892)
XLA Ops:
  8.1 2.8 fusion.103
  10.9 2.3 collective-permute-start.49
  13.3 2.4 collective-permute-start.50
  28.8 3.6 fusion.77
  32.4 2.5 fusion.91
  35.3 6.1 collective-permute-done.52
  43.1 2.4 fusion.80.other
  45.6 19.8 %attention_fwd.2 = (bf16[8,128,1024]{2,1,0:T(8,128)(2,1)}, bf16[8,3,8,64,128]{4,3,2,1,0:T(8,128)(2,1)}, f32[8,8,8,128]{3,2,1,0:T(8,128)}, bf16[8,128,512]{2,1,0:...) custom-call(s32[2]{0:T(128)S(1)} %pad_add_fusion.1.info, ...), custom_call_target="tpu_custom_call" | custom-call | flops 429496729600 | bytes 4538369024 | tf_op jit(solution)/shard_map/attention_fwd/pallas_call | solution.py:155
  68.0 2.4 fusion.74.other
  70.5 19.6 %attention_fwd.3 = (bf16[8,128,1024]{2,1,0:T(8,128)(2,1)}, bf16[8,3,8,64,128]{4,3,2,1,0:T(8,128)(2,1)}, f32[8,8,8,128]{3,2,1,0:T(8,128)}, bf16[8,128,512]{2,1,0:...) custom-call(s32[2]{0:T(128)S(1)} %pad_add_fusion.1.info, ...), custom_call_target="tpu_custom_call" | custom-call | flops 429496729600 | bytes 4538369024 | tf_op jit(solution)/shard_map/attention_fwd/pallas_call | solution.py:155
  96.6 2.4 pad_maximum_fusion.27
  101.9 15.7 %collective-permute-done.59 = bf16[4,128,1024]{2,1,0:T(8,128)(2,1)} collective-permute-done((bf16[4,128,1024]{2,1,0:T(8,128)(2,1)S(1)}, bf16[4,128,1024]{2,1,0:T(8,128)(2,1)}, u32[]{:S(2)}, u32[]{:S(2)}) %collective-permute-start.59) | collective-permute-done | bytes 1048608 | tf_op jit(solution)/shard_map/ppermute | solution.py:56
  121.1 67.0 %conditional.4 = (bf16[4,3,256,1408]{3,2,1,0:T(8,128)(2,1)}, bf16[512,1024]{1,0:T(8,128)(2,1)}, bf16[512,1024]{1,0:T(8,128)(2,1)}, bf16[512,1024]{1,0:T(8,128)(2...) conditional(s32[]{:T(128)} %convert_element_type.132, () %tuple.82, ...), branch_computations={%region_2.3_spmd, %region_3.4_spmd} | conditional | flops 2657512062976 | bytes 18158192640 | solution.py:39
  126.6 16.1 %feed_forward.4 = (bf16[512,1408]{1,0:T(8,128)(2,1)}, bf16[2,512,1408]{2,1,0:T(8,128)(2,1)}, f32[512,1024]{1,0:T(8,128)}, f32[512,1024]{1,0:T(8,128)}) custom-call(s32[1]{0:T(128)} %bitcast.5.info, bf16[512,1024]{1,0:T(8,128)(2,1)} %bitcast.rows.refs_2_, bf16[512,1024]{1,0:T(8,128)(2,1)} %get-tuple-element.158.cot.refs_0_, ...), custom_call_target="tpu_custom_call" | custom-call | flops 885837004800 | bytes 7982285312 | tf_op jit(solution)/shard_map/cond/branch_1_fun/feed_forward/pallas_call | solution.py:155
  142.7 2.1 pad_maximum_fusion
  144.8 16.6 %feed_forward.5 = (bf16[512,1408]{1,0:T(8,128)(2,1)}, bf16[2,512,1408]{2,1,0:T(8,128)(2,1)}, f32[512,1024]{1,0:T(8,128)}, f32[512,1024]{1,0:T(8,128)}) custom-call(s32[1]{0:T(128)} %bitcast.5.info, bf16[512,1024]{1,0:T(8,128)(2,1)} %bitcast.4.rows.refs_3_, bf16[512,1024]{1,0:T(8,128)(2,1)} %get-tuple-element.163.cot.refs_1_, ...), custom_call_target="tpu_custom_call" | custom-call | flops 885837004800 | bytes 7982285312 | tf_op jit(solution)/shard_map/cond/branch_1_fun/feed_forward/pallas_call | solution.py:155
  161.4 8.4 %collective-permute-done.2 = bf16[512,1024]{1,0:T(8,128)(2,1)} collective-permute-done((bf16[512,1024]{1,0:T(8,128)(2,1)}, bf16[512,1024]{1,0:T(8,128)(2,1)}, u32[]{:S(2)}, u32[]{:S(2)}) %collective-permute-start.2) | collective-permute-done | bytes 1048608 | tf_op jit(solution)/shard_map/cond/branch_1_fun/ppermute | solution.py:56
  171.2 16.8 %ffn_grad.2 = bf16[4,3,256,1408]{3,2,1,0:T(8,128)(2,1)} custom-call(bf16[512,1024]{1,0:T(8,128)(2,1)} %get-tuple-element.158.cot.refs_0_, bf16[512,1024]{1,0:T(8,128)(2,1)} %get-tuple-element.163.cot.refs_1_, bf16[512,1024]{1,0:T(8,128)(2,1)} %bitcast.rows.refs_2_, bf16[512,1024]{1,0:T(8,128)(2,1)} %bitcast.4.rows.refs_3_, bf16[512,1408]{1,0:T(8,128)(2,1)S(1)} %copy-done.3, ...), custom_call_target="tpu_custom_call" | custom-call | flops 885837004800 | bytes 2149580800 | tf_op jit(solution)/shard_map/cond/branch_1_fun/ffn_grad/pallas_call | solution.py:155
  189.7 157.3 %conditional.5 = (bf16[4,3,256,1408]{3,2,1,0:T(8,128)(2,1)}, f32[4,128,1024]{2,1,0:T(8,128)}, f32[4,128,1024]{2,1,0:T(8,128)}, bf16[4,128,1024]{2,1,0:T(8,128)(2...) conditional(s32[]{:T(128)} %convert_element_type.132, () %tuple.80, ...), branch_computations={%region_5.6_spmd, %region_6.13_spmd} | conditional | flops 2657548763136 | bytes 17917280256 | solution.py:39
  198.7 15.7 %feed_forward.6 = (bf16[512,1408]{1,0:T(8,128)(2,1)}, bf16[2,512,1408]{2,1,0:T(8,128)(2,1)}, bf16[512,1024]{1,0:T(8,128)(2,1)}, bf16[512,1024]{1,0:T(8,128)(2,1)}) custom-call(s32[1]{0:T(128)} %bitcast.6.info, bf16[512,1024]{1,0:T(8,128)(2,1)} %get-tuple-element.182.rows.refs_2_, bf16[512,1024]{1,0:T(8,128)(2,1)} %get-tuple-element.183.cot.refs_0_, ...), custom_call_target="tpu_custom_call" | custom-call | flops 885837004800 | bytes 7772570112 | tf_op jit(solution)/shard_map/cond/branch_1_fun/feed_forward/pallas_call | solution.py:155
  214.4 8.4 %collective-permute-done.18 = bf16[1,2,2,128,1024]{4,3,1,2,0:T(8,128)(2,1)} collective-permute-done((bf16[1,2,2,128,1024]{4,3,1,2,0:T(8,128)(2,1)}, bf16[1,2,2,128,1024]{4,3,1,2,0:T(8,128)(2,1)}, u32[]{:S(2)}, u32[]{:S(2)}) %collective-permute-start.18) | collective-permute-done | bytes 1048608 | tf_op jit(solution)/shard_map/cond/branch_1_fun/ppermute | solution.py:96
  222.9 2.8 pad_maximum_fusion.1
  232.6 2.7 fusion.16
  235.2 4.4 collective-permute-done.16.rows.refs_3_
  239.7 3.0 collective-permute-done.22
  243.8 9.4 %collective-permute-done.20 = bf16[1,2,2,128,512]{4,3,1,2,0:T(8,128)(2,1)S(1)} collective-permute-done((bf16[1,2,2,128,512]{4,3,1,2,0:T(8,128)(2,1)S(1)}, bf16[1,2,2,128,512]{4,3,1,2,0:T(8,128)(2,1)S(1)}, u32[]{:S(2)}, u32[]{:S(2)}) %collective-permute-start.20) | collective-permute-done | bytes 524320 | tf_op jit(solution)/shard_map/cond/branch_1_fun/ppermute | solution.py:96
  256.0 16.3 %feed_forward.7 = (bf16[512,1408]{1,0:T(8,128)(2,1)}, bf16[2,512,1408]{2,1,0:T(8,128)(2,1)}, bf16[512,1024]{1,0:T(8,128)(2,1)}, bf16[512,1024]{1,0:T(8,128)(2,1)}) custom-call(s32[1]{0:T(128)} %bitcast.6.info, bf16[512,1024]{1,0:T(8,128)(2,1)} %collective-permute-done.16.rows.refs_3_, bf16[512,1024]{1,0:T(8,128)(2,1)} %collective-permute-done.15.cot.refs_1_, ...), custom_call_target="tpu_custom_call" | custom-call | flops 885837004800 | bytes 7772570112 | tf_op jit(solution)/shard_map/cond/branch_1_fun/feed_forward/pallas_call | solution.py:155
  273.8 5.2 collective-permute-done.24
  279.0 2.8 pad_maximum_fusion.2
  281.8 2.3 add_convert_fusion.1
  288.4 17.9 %ffn_grad.3 = bf16[4,3,256,1408]{3,2,1,0:T(8,128)(2,1)} custom-call(bf16[512,1024]{1,0:T(8,128)(2,1)} %get-tuple-element.183.cot.refs_0_, bf16[512,1024]{1,0:T(8,128)(2,1)} %collective-permute-done.15.cot.refs_1_, bf16[512,1024]{1,0:T(8,128)(2,1)} %get-tuple-element.182.rows.refs_2_, bf16[512,1024]{1,0:T(8,128)(2,1)} %collective-permute-done.16.rows.refs_3_, ...), custom_call_target="tpu_custom_call" | custom-call | flops 885837004800 | bytes 2149580800 | tf_op jit(solution)/shard_map/cond/branch_1_fun/ffn_grad/pallas_call | solution.py:155
  307.4 2.6 multiply_reduce_fusion
  312.7 2.4 fusion.98
  316.6 2.2 add_convert_fusion
  319.4 13.6 %collective-permute-done.29 = bf16[2,1,128,1024]{3,2,1,0:T(8,128)(2,1)S(1)} collective-permute-done((bf16[2,1,128,1024]{3,2,1,0:T(8,128)(2,1)S(1)}, bf16[2,1,128,1024]{3,2,1,0:T(8,128)(2,1)S(1)}, u32[]{:S(2)}, u32[]{:S(2)}) %collective-permute-start.29) | collective-permute-done | bytes 524320 | tf_op jit(solution)/shard_map/cond/branch_1_fun/ppermute | solution.py:106
  333.0 7.9 %collective-permute-done.30 = bf16[4,128,1024]{2,1,0:T(8,128)(2,1)} collective-permute-done((bf16[4,128,1024]{2,1,0:T(8,128)(2,1)}, bf16[4,128,1024]{2,1,0:T(8,128)(2,1)}, u32[]{:S(2)}, u32[]{:S(2)}) %collective-permute-start.30) | collective-permute-done | bytes 1048608 | tf_op jit(solution)/shard_map/cond/branch_1_fun/ppermute | solution.py:56
  344.5 2.4 fusion.96
  348.0 156.5 %conditional.6 = (bf16[4,2,3,256,512]{4,3,2,1,0:T(8,128)(2,1)}, bf16[4,2,1,256,512]{4,3,2,1,0:T(8,128)(2,1)}, f32[4,128,1024]{2,1,0:T(8,128)}, f32[4,128,1024]{2...) conditional(s32[]{:T(128)} %convert_element_type.132, () %tuple.79, ...), branch_computations={%region_13.14_spmd, %region_14.15_spmd} | conditional | flops 1718001598464 | bytes 11795433472 | solution.py:39
  355.8 24.3 %attention_bwd.2 = (bf16[8,3,128,512]{3,2,1,0:T(8,128)(2,1)}, f32[4,128,1024]{2,1,0:T(8,128)}, bf16[4,128,1024]{2,1,0:T(8,128)(2,1)}) custom-call(s32[2]{0:T(128)S(1)} %get-tuple-element.231.info, bf16[4,128,1024]{2,1,0:T(8,128)(2,1)} %get-tuple-element.237.own, bf16[4,128,1024]{2,1,0:T(8,128)(2,1)} %get-tuple-element.238.other, ...), custom_call_target="tpu_custom_call" | custom-call | flops 429496729600 | bytes 4535092224 | tf_op jit(solution)/shard_map/cond/branch_1_fun/attention_bwd/pallas_call | solution.py:155
  390.2 23.4 %attention_bwd.3 = (bf16[8,3,128,512]{3,2,1,0:T(8,128)(2,1)}, f32[4,128,1024]{2,1,0:T(8,128)}, bf16[4,128,1024]{2,1,0:T(8,128)(2,1)}) custom-call(s32[2]{0:T(128)S(1)} %get-tuple-element.231.info, bf16[4,128,1024]{2,1,0:T(8,128)(2,1)} %get-tuple-element.247.own, bf16[4,128,1024]{2,1,0:T(8,128)(2,1)} %collective-permute-done.6.other, ...), custom_call_target="tpu_custom_call" | custom-call | flops 429496729600 | bytes 4535092224 | tf_op jit(solution)/shard_map/cond/branch_1_fun/attention_bwd/pallas_call | solution.py:155
  413.7 12.2 %collective-permute-done.8 = bf16[1,2,2,3,128,512]{5,4,1,3,2,0:T(8,128)(2,1)} collective-permute-done((bf16[1,2,2,3,128,512]{5,4,1,3,2,0:T(8,128)(2,1)}, bf16[1,2,2,3,128,512]{5,4,1,3,2,0:T(8,128)(2,1)}, u32[]{:S(2)}, u32[]{:S(2)}) %collective-permute-start.8) | collective-permute-done | bytes 1572896 | tf_op jit(solution)/shard_map/cond/branch_1_fun/ppermute | solution.py:96
  425.9 2.0 pad_maximum_fusion.9
  429.0 3.3 collective-permute-done.10
  440.0 29.1 %collective-permute-done.11 = bf16[1,2,2,3,128,512]{5,4,1,3,2,0:T(8,128)(2,1)S(1)} collective-permute-done((bf16[1,2,2,3,128,512]{5,4,1,3,2,0:T(8,128)(2,1)S(1)}, bf16[1,2,2,3,128,512]{5,4,1,3,2,0:T(8,128)(2,1)S(1)}, u32[]{:S(2)}, u32[]{:S(2)}) %collective-permute-start.11) | collective-permute-done | bytes 1572896 | tf_op jit(solution)/shard_map/cond/branch_1_fun/ppermute | solution.py:96
  472.0 21.9 %weight_grad.2 = bf16[4,2,3,256,512]{4,3,2,1,0:T(8,128)(2,1)} custom-call(bf16[2,512,1024]{2,1,0:T(8,128)(2,1)} %get-tuple-element.229.refs_0_, bf16[2,512,1024]{2,1,0:T(8,128)(2,1)} %get-tuple-element.230.refs_1_, bf16[2,3,512,512]{3,2,1,0:T(8,128)(2,1)S(1)} %bitcast.495, bf16[2,3,512,512]{3,2,1,0:T(8,128)(2,1)} %bitcast.513), custom_call_target="tpu_custom_call" | custom-call | flops 644245094400 | bytes 1677721600 | tf_op jit(solution)/shard_map/cond/branch_1_fun/weight_grad/pallas_call | solution.py:155
  493.8 2.0 collective-permute-done.13
  497.3 7.2 %weight_grad.3 = bf16[4,2,1,256,512]{4,3,2,1,0:T(8,128)(2,1)} custom-call(bf16[2,512,1024]{2,1,0:T(8,128)(2,1)S(1)} %bitcast.496, bf16[2,512,1024]{2,1,0:T(8,128)(2,1)S(1)} %bitcast.497, bf16[2,1,512,512]{3,2,1,0:T(8,128)(2,1)} %get-tuple-element.262.refs_2_, bf16[2,1,512,512]{3,2,1,0:T(8,128)(2,1)} %get-tuple-element.263.refs_3_), custom_call_target="tpu_custom_call" | custom-call | flops 214748364800 | bytes 838860800 | tf_op jit(solution)/shard_map/cond/branch_1_fun/weight_grad/pallas_call | solution.py:155
  506.4 116.4 %conditional.7 = (f32[8,64,1408]{2,1,0:T(8,128)}, f32[8,2,64,1408]{3,2,1,0:T(8,128)}, bf16[4,256,1024]{2,1,0:T(8,128)(2,1)}, f32[4,256,1024]{2,1,0:T(8,128)}, f32[4,64]{1,0:T(4,128)S(1)}, /*index=5*/f32[4,64]{1,0:T(4,128)S(1)}) conditional(s32[]{:T(128)} %convert_element_type.132, () %tuple.78, (s32[]{:T(128)}, bf16[4,128,1024]{2,1,0:T(8,128)(2,1)}, ...), branch_computations={%region_16.17_spmd, %region_17.24_spmd} | conditional | flops 62505492 | bytes 322650304 | solution.py:39
  506.6 2.2 add_convert_fusion.5
  511.4 2.6 add_convert_fusion.3
  519.4 2.7 constant_dynamic-slice_fusion.18
  527.5 2.4 copy.264
  544.5 21.1 %collective-permute-done.34 = bf16[1,2,3,64,1408]{4,3,2,1,0:T(8,128)(2,1)S(1)} collective-permute-done((bf16[1,2,3,64,1408]{4,3,2,1,0:T(8,128)(2,1)S(1)}, bf16[1,2,3,64,1408]{4,3,2,1,0:T(8,128)(2,1)S(1)}, u32[]{:S(2)}, u32[]{:S(2)}) %collective-permute-start.34) | collective-permute-done | bytes 1081376 | tf_op jit(solution)/shard_map/cond/branch_1_fun/ppermute | solution.py:96
  567.1 4.4 fusion.46
  571.5 16.7 %collective-permute-done.36 = bf16[1,2,3,64,1408]{4,3,2,1,0:T(8,128)(2,1)S(1)} collective-permute-done((bf16[1,2,3,64,1408]{4,3,2,1,0:T(8,128)(2,1)S(1)}, bf16[1,2,3,64,1408]{4,3,2,1,0:T(8,128)(2,1)S(1)}, u32[]{:S(2)}, u32[]{:S(2)}) %collective-permute-start.36) | collective-permute-done | bytes 1081376 | tf_op jit(solution)/shard_map/cond/branch_1_fun/ppermute | solution.py:96
  589.6 2.7 collective-permute-start.43
  594.4 3.4 copy-done.11
  601.3 4.6 fusion.43
  610.8 5.9 slice.408
  619.8 2.8 pad_add_fusion
  624.5 2.7 collective-permute-start.60
  629.2 2.1 collective-permute-start.61
  631.3 38.2 %reduce-scatter.11.cloned.1.call-done = bf16[1,2,1,256,512]{4,3,2,1,0:T(8,128)(2,1)} async-done(((bf16[4,2,1,256,512]{4,3,2,1,0:T(8,128)(2,1)}), bf16[1,2,1,256,512]{4,3,2,1,0:T(8,128)(2,1)}) %reduce-scatter.11.cloned.1.call-update) | async-done | bytes 524304 | tf_op jit(solution)/shard_map/reduce_scatter | solution.py:596
  675.9 4.8 collective-permute-done.63
  (408 shorter events, 162.8 us)
Async XLA Ops:
  7.2 339.8 %reduce-scatter.5.cloned.1.call-start = ((), (), s32[]{:S(2)}) async-start(), calls=%async_computation.4 | async-start | bytes 10813440 | tf_op jit(solution)/shard_map/reduce_scatter | solution.py:596
  10.9 12.6 %collective-permute-start.49 = (bf16[4,2,1024]{2,1,0:T(2,128)(2,1)S(1)}, bf16[4,2,1024]{2,1,0:T(2,128)(2,1)S(1)}, u32[]{:S(2)}, u32[]{:S(2)}) collective-permute-start(bf16[4,2,1024]{2,1,0:T(2,128)(2,1)S(1)} %slice.359), channel_id=1, source_target_pairs={{0,2},{2,4},{4,6},{6,8},{8,10},{10,12},{12,14},{14,16},{16,18},{18... | collective-permute-start | bytes 49160 | tf_op jit(solution)/shard_map/ppermute | solution.py:26
  13.3 11.8 %collective-permute-start.50 = (f32[4,1152]{1,0:T(4,128)S(1)}, f32[4,1152]{1,0:T(4,128)S(1)}, u32[]{:S(2)}, u32[]{:S(2)}) collective-permute-start(f32[4,1152]{1,0:T(4,128)S(1)} %pad_maximum_fusion.31), channel_id=1, source_target_pairs={{0,1},{1,0},{2,3},{3,2},{4,5},{5,4},{6,7},{7,6},{8,9},{9,8},{10,11... | collective-permute-start | bytes 55304 | tf_op jit(solution)/shard_map/ppermute | solution.py:56
  15.7 25.7 %collective-permute-start.52 = (bf16[4,128,1024]{2,1,0:T(8,128)(2,1)S(1)}, bf16[4,128,1024]{2,1,0:T(8,128)(2,1)}, u32[]{:S(2)}, u32[]{:S(2)}) collective-permute-start(bf16[4,128,1024]{2,1,0:T(8,128)(2,1)S(1)} %get-tuple-element.377), channel_id=1, source_target_pairs={{0,1},{1,0},{2,3},{3,2},{4,5},{5,4},{6,7},{7,6},{8,9},{9,8},{10,11... | collective-permute-start | bytes 3145736 | tf_op jit(solution)/shard_map/ppermute | solution.py:56
  18.9 13.5 %collective-permute-start.47 = (bf16[2,1,128,1024]{3,2,1,0:T(8,128)(2,1)}, bf16[2,1,128,1024]{3,2,1,0:T(8,128)(2,1)}, u32[]{:S(2)}, u32[]{:S(2)}) collective-permute-start(bf16[2,1,128,1024]{3,2,1,0:T(8,128)(2,1)} %get-tuple-element.594), channel_id=1, source_target_pairs={{0,2},{2,0},{4,6},{6,4},{8,10},{10,8},{12,14},{14,12},{16,18},{18,... | collective-permute-start | bytes 1572872 | tf_op jit(solution)/shard_map/ppermute | solution.py:89
  21.5 4.5 collective-permute-start.53
  23.5 19.6 %collective-permute-start.51 = (bf16[4,2,1024]{2,1,0:T(2,128)(2,1)S(1)}, bf16[4,2,1024]{2,1,0:T(2,128)(2,1)S(1)}, u32[]{:S(2)}, u32[]{:S(2)}) collective-permute-start(bf16[4,2,1024]{2,1,0:T(2,128)(2,1)S(1)} %collective-permute-done.49), channel_id=1, source_target_pairs={{0,1},{1,0},{2,3},{3,2},{4,5},{5,4},{6,7},{7,6},{8,9},{9,8},{10,11... | collective-permute-start | bytes 49160 | tf_op jit(solution)/shard_map/ppermute | solution.py:56
  27.2 14.8 %collective-permute-start.54 = (bf16[1,2,128,1024]{3,2,1,0:T(8,128)(2,1)S(1)}, bf16[1,2,128,1024]{3,2,1,0:T(8,128)(2,1)S(1)}, u32[]{:S(2)}, u32[]{:S(2)}) collective-permute-start(bf16[1,2,128,1024]{3,2,1,0:T(8,128)(2,1)S(1)} %get-tuple-element.589), channel_id=1, source_target_pairs={{0,4},{2,6},{4,0},{6,2},{8,12},{10,14},{12,8},{14,10},{16,20},{18,... | collective-permute-start | bytes 1572872 | tf_op jit(solution)/shard_map/ppermute | solution.py:96
  34.8 61.7 %collective-permute-start.48 = (bf16[1,2,128,1024]{3,2,1,0:T(8,128)(2,1)}, bf16[1,2,128,1024]{3,2,1,0:T(8,128)(2,1)}, u32[]{:S(2)}, u32[]{:S(2)}) collective-permute-start(bf16[1,2,128,1024]{3,2,1,0:T(8,128)(2,1)} %get-tuple-element.593), channel_id=1, source_target_pairs={{0,4},{2,6},{4,0},{6,2},{8,12},{10,14},{12,8},{14,10},{16,20},{18,... | collective-permute-start | bytes 1572872 | tf_op jit(solution)/shard_map/ppermute | solution.py:96
  41.4 26.6 %collective-permute-start.56 = (bf16[4,128,1024]{2,1,0:T(8,128)(2,1)}, bf16[4,128,1024]{2,1,0:T(8,128)(2,1)}, u32[]{:S(2)}, u32[]{:S(2)}) collective-permute-start(bf16[4,128,1024]{2,1,0:T(8,128)(2,1)} %get-tuple-element.384), channel_id=1, source_target_pairs={{0,1},{1,0},{2,3},{3,2},{4,5},{5,4},{6,7},{7,6},{8,9},{9,8},{10,11... | collective-permute-start | bytes 3145736 | tf_op jit(solution)/shard_map/ppermute | solution.py:56
  65.4 25.7 %collective-permute-start.55 = (bf16[4,128,1024]{2,1,0:T(8,128)(2,1)}, bf16[4,128,1024]{2,1,0:T(8,128)(2,1)}, u32[]{:S(2)}, u32[]{:S(2)}) collective-permute-start(bf16[4,128,1024]{2,1,0:T(8,128)(2,1)} %get-tuple-element.382), channel_id=1, source_target_pairs={{0,1},{1,0},{2,3},{3,2},{4,5},{5,4},{6,7},{7,6},{8,9},{9,8},{10,11... | collective-permute-start | bytes 3145736 | tf_op jit(solution)/shard_map/ppermute | solution.py:56
  92.8 24.8 %collective-permute-start.59 = (bf16[4,128,1024]{2,1,0:T(8,128)(2,1)S(1)}, bf16[4,128,1024]{2,1,0:T(8,128)(2,1)}, u32[]{:S(2)}, u32[]{:S(2)}) collective-permute-start(bf16[4,128,1024]{2,1,0:T(8,128)(2,1)S(1)} %get-tuple-element.388), channel_id=1, source_target_pairs={{0,1},{1,0},{2,3},{3,2},{4,5},{5,4},{6,7},{7,6},{8,9},{9,8},{10,11... | collective-permute-start | bytes 3145736 | tf_op jit(solution)/shard_map/ppermute | solution.py:56
  96.0 3.0 collective-permute-start.57
  100.1 19.6 %collective-permute-start.58 = (bf16[1,2,128,1024]{3,2,1,0:T(8,128)(2,1)S(1)}, bf16[1,2,128,1024]{3,2,1,0:T(8,128)(2,1)S(1)}, u32[]{:S(2)}, u32[]{:S(2)}) collective-permute-start(bf16[1,2,128,1024]{3,2,1,0:T(8,128)(2,1)S(1)} %get-tuple-element.585), channel_id=1, source_target_pairs={{0,4},{2,6},{4,0},{6,2},{8,12},{10,14},{12,8},{14,10},{16,20},{18,... | collective-permute-start | bytes 1572872 | tf_op jit(solution)/shard_map/ppermute | solution.py:96
  121.4 2.2 collective-permute-start
  121.5 40.0 %collective-permute-start.3 = (bf16[512,1024]{1,0:T(8,128)(2,1)}, bf16[512,1024]{1,0:T(8,128)(2,1)}, u32[]{:S(2)}, u32[]{:S(2)}) collective-permute-start(bf16[512,1024]{1,0:T(8,128)(2,1)} %bitcast.rows.refs_2_), channel_id=1, source_target_pairs={{0,1},{1,0},{2,3},{3,2},{4,5},{5,4},{6,7},{7,6},{8,9},{9,8},{10,11... | collective-permute-start | bytes 3145736 | tf_op jit(solution)/shard_map/cond/branch_1_fun/ppermute | solution.py:56
  123.3 46.6 %collective-permute-start.2 = (bf16[512,1024]{1,0:T(8,128)(2,1)}, bf16[512,1024]{1,0:T(8,128)(2,1)}, u32[]{:S(2)}, u32[]{:S(2)}) collective-permute-start(bf16[512,1024]{1,0:T(8,128)(2,1)} %get-tuple-element.158.cot.refs_0_), channel_id=1, source_target_pairs={{0,1},{1,0},{2,3},{3,2},{4,5},{5,4},{6,7},{7,6},{8,9},{9,8},{10,11... | collective-permute-start | bytes 3145736 | tf_op jit(solution)/shard_map/cond/branch_1_fun/ppermute | solution.py:56
  124.6 18.0 %collective-permute-start.1 = (bf16[1,2,128,1024]{3,2,1,0:T(8,128)(2,1)}, bf16[1,2,128,1024]{3,2,1,0:T(8,128)(2,1)}, u32[]{:S(2)}, u32[]{:S(2)}) collective-permute-start(bf16[1,2,128,1024]{3,2,1,0:T(8,128)(2,1)} %get-tuple-element.461), channel_id=1, source_target_pairs={{0,4},{2,6},{4,0},{6,2},{8,12},{10,14},{12,8},{14,10},{16,20},{18,... | collective-permute-start | bytes 1572872 | tf_op jit(solution)/shard_map/cond/branch_1_fun/ppermute | solution.py:96
  188.1 316.4 %reduce-scatter.7.cloned.1.call-start = ((), (), s32[]{:S(2)}) async-start(), calls=%async_computation.5 | async-start | bytes 10813440 | tf_op jit(solution)/shard_map/reduce_scatter | solution.py:596
  190.9 4.3 collective-permute-start.17
  190.9 44.3 %collective-permute-start.15 = (bf16[512,1024]{1,0:T(8,128)(2,1)}, bf16[512,1024]{1,0:T(8,128)(2,1)}, u32[]{:S(2)}, u32[]{:S(2)}) collective-permute-start(bf16[512,1024]{1,0:T(8,128)(2,1)} %get-tuple-element.175), channel_id=1, source_target_pairs={{0,1},{1,0},{2,3},{3,2},{4,5},{5,4},{6,7},{7,6},{8,9},{9,8},{10,11... | collective-permute-start | bytes 3145736 | tf_op jit(solution)/shard_map/cond/branch_1_fun/ppermute | solution.py:56
  192.7 47.0 %collective-permute-start.16 = (bf16[512,1024]{1,0:T(8,128)(2,1)}, bf16[512,1024]{1,0:T(8,128)(2,1)}, u32[]{:S(2)}, u32[]{:S(2)}) collective-permute-start(bf16[512,1024]{1,0:T(8,128)(2,1)} %get-tuple-element.177), channel_id=1, source_target_pairs={{0,1},{1,0},{2,3},{3,2},{4,5},{5,4},{6,7},{7,6},{8,9},{9,8},{10,11... | collective-permute-start | bytes 3145736 | tf_op jit(solution)/shard_map/cond/branch_1_fun/ppermute | solution.py:56
  195.1 35.8 %collective-permute-start.23 = (bf16[2,1,2,128,1024]{4,3,1,2,0:T(8,128)(2,1)}, bf16[2,1,2,128,1024]{4,3,1,2,0:T(8,128)(2,1)}, u32[]{:S(2)}, u32[]{:S(2)}) collective-permute-start(bf16[2,1,2,128,1024]{4,3,1,2,0:T(8,128)(2,1)} %bitcast.478), channel_id=1, source_target_pairs={{0,2},{2,0},{4,6},{6,4},{8,10},{10,8},{12,14},{14,12},{16,18},{18,... | collective-permute-start | bytes 3145736 | tf_op jit(solution)/shard_map/cond/branch_1_fun/ppermute | solution.py:89
  196.7 26.1 %collective-permute-start.18 = (bf16[1,2,2,128,1024]{4,3,1,2,0:T(8,128)(2,1)}, bf16[1,2,2,128,1024]{4,3,1,2,0:T(8,128)(2,1)}, u32[]{:S(2)}, u32[]{:S(2)}) collective-permute-start(bf16[1,2,2,128,1024]{4,3,1,2,0:T(8,128)(2,1)} %get-tuple-element.187), channel_id=1, source_target_pairs={{0,4},{2,6},{4,0},{6,2},{8,12},{10,14},{12,8},{14,10},{16,20},{18,... | collective-permute-start | bytes 3145736 | tf_op jit(solution)/shard_map/cond/branch_1_fun/ppermute | solution.py:96
  227.0 2.7 collective-permute-start.19
  227.9 14.8 %collective-permute-start.22 = (bf16[1,2,2,128,512]{4,3,1,2,0:T(8,128)(2,1)S(1)}, bf16[1,2,2,128,512]{4,3,1,2,0:T(8,128)(2,1)S(1)}, u32[]{:S(2)}, u32[]{:S(2)}) collective-permute-start(bf16[1,2,2,128,512]{4,3,1,2,0:T(8,128)(2,1)S(1)} %get-tuple-element.559), channel_id=1, source_target_pairs={{0,4},{2,6},{4,0},{6,2},{8,12},{10,14},{12,8},{14,10},{16,20},{18,... | collective-permute-start | bytes 1572872 | tf_op jit(solution)/shard_map/cond/branch_1_fun/ppermute | solution.py:96
  229.8 23.4 %collective-permute-start.20 = (bf16[1,2,2,128,512]{4,3,1,2,0:T(8,128)(2,1)S(1)}, bf16[1,2,2,128,512]{4,3,1,2,0:T(8,128)(2,1)S(1)}, u32[]{:S(2)}, u32[]{:S(2)}) collective-permute-start(bf16[1,2,2,128,512]{4,3,1,2,0:T(8,128)(2,1)S(1)} %get-tuple-element.563), channel_id=1, source_target_pairs={{0,4},{2,6},{4,0},{6,2},{8,12},{10,14},{12,8},{14,10},{16,20},{18,... | collective-permute-start | bytes 1572872 | tf_op jit(solution)/shard_map/cond/branch_1_fun/ppermute | solution.py:96
  231.0 50.8 %collective-permute-start.25 = (bf16[512,1024]{1,0:T(8,128)(2,1)}, bf16[512,1024]{1,0:T(8,128)(2,1)}, u32[]{:S(2)}, u32[]{:S(2)}) collective-permute-start(bf16[512,1024]{1,0:T(8,128)(2,1)} %get-tuple-element.202), channel_id=1, source_target_pairs={{0,1},{1,0},{2,3},{3,2},{4,5},{5,4},{6,7},{7,6},{8,9},{9,8},{10,11... | collective-permute-start | bytes 3145736 | tf_op jit(solution)/shard_map/cond/branch_1_fun/ppermute | solution.py:56
  254.2 24.8 %collective-permute-start.24 = (bf16[1,2,2,128,1024]{4,3,1,2,0:T(8,128)(2,1)}, bf16[1,2,2,128,1024]{4,3,1,2,0:T(8,128)(2,1)}, u32[]{:S(2)}, u32[]{:S(2)}) collective-permute-start(bf16[1,2,2,128,1024]{4,3,1,2,0:T(8,128)(2,1)} %get-tuple-element.200), channel_id=1, source_target_pairs={{0,4},{2,6},{4,0},{6,2},{8,12},{10,14},{12,8},{14,10},{16,20},{18,... | collective-permute-start | bytes 3145736 | tf_op jit(solution)/shard_map/cond/branch_1_fun/ppermute | solution.py:96
  272.3 34.0 %collective-permute-start.27 = (bf16[512,1024]{1,0:T(8,128)(2,1)}, bf16[512,1024]{1,0:T(8,128)(2,1)}, u32[]{:S(2)}, u32[]{:S(2)}) collective-permute-start(bf16[512,1024]{1,0:T(8,128)(2,1)} %get-tuple-element.209), channel_id=1, source_target_pairs={{0,1},{1,0},{2,3},{3,2},{4,5},{5,4},{6,7},{7,6},{8,9},{9,8},{10,11... | collective-permute-start | bytes 3145736 | tf_op jit(solution)/shard_map/cond/branch_1_fun/ppermute | solution.py:56
  286.7 19.6 %collective-permute-start.26 = (bf16[2,1,128,1024]{3,2,1,0:T(8,128)(2,1)}, bf16[2,1,128,1024]{3,2,1,0:T(8,128)(2,1)}, u32[]{:S(2)}, u32[]{:S(2)}) collective-permute-start(bf16[2,1,128,1024]{3,2,1,0:T(8,128)(2,1)} %pad_maximum_fusion.7), channel_id=1, source_target_pairs={{0,4},{2,6},{4,0},{6,2},{8,12},{10,14},{12,8},{14,10},{16,20},{18,... | collective-permute-start | bytes 1572872 | tf_op jit(solution)/shard_map/cond/branch_1_fun/ppermute | solution.py:106
  307.4 2.7 collective-permute-start.28
  315.0 25.9 %collective-permute-start.30 = (bf16[4,128,1024]{2,1,0:T(8,128)(2,1)}, bf16[4,128,1024]{2,1,0:T(8,128)(2,1)}, u32[]{:S(2)}, u32[]{:S(2)}) collective-permute-start(bf16[4,128,1024]{2,1,0:T(8,128)(2,1)} %get-tuple-element.648), channel_id=1, source_target_pairs={{0,1},{1,0},{2,3},{3,2},{4,5},{5,4},{6,7},{7,6},{8,9},{9,8},{10,11... | collective-permute-start | bytes 3145736 | tf_op jit(solution)/shard_map/cond/branch_1_fun/ppermute | solution.py:56
  318.9 14.1 %collective-permute-start.29 = (bf16[2,1,128,1024]{3,2,1,0:T(8,128)(2,1)S(1)}, bf16[2,1,128,1024]{3,2,1,0:T(8,128)(2,1)S(1)}, u32[]{:S(2)}, u32[]{:S(2)}) collective-permute-start(bf16[2,1,128,1024]{3,2,1,0:T(8,128)(2,1)S(1)} %pad_maximum_fusion.8), channel_id=1, source_target_pairs={{0,4},{2,6},{4,0},{6,2},{8,12},{10,14},{12,8},{14,10},{16,20},{18,... | collective-permute-start | bytes 1572872 | tf_op jit(solution)/shard_map/cond/branch_1_fun/ppermute | solution.py:106
  347.1 275.8 %reduce-scatter.9.cloned.1.call-start = ((), (), s32[]{:S(2)}) async-start(), calls=%async_computation.6 | async-start | bytes 7864320 | tf_op jit(solution)/shard_map/reduce_scatter | solution.py:596
  351.1 2.9 collective-permute-start.4
  351.2 31.3 %collective-permute-start.6 = (bf16[4,128,1024]{2,1,0:T(8,128)(2,1)}, bf16[4,128,1024]{2,1,0:T(8,128)(2,1)}, u32[]{:S(2)}, u32[]{:S(2)}) collective-permute-start(bf16[4,128,1024]{2,1,0:T(8,128)(2,1)} %get-tuple-element.247.own), channel_id=1, source_target_pairs={{0,1},{1,0},{2,3},{3,2},{4,5},{5,4},{6,7},{7,6},{8,9},{9,8},{10,11... | collective-permute-start | bytes 3145736 | tf_op jit(solution)/shard_map/cond/branch_1_fun/ppermute | solution.py:56
  355.5 25.5 %collective-permute-start.5 = (bf16[1,2,2,128,1024]{4,3,1,2,0:T(8,128)(2,1)}, bf16[1,2,2,128,1024]{4,3,1,2,0:T(8,128)(2,1)}, u32[]{:S(2)}, u32[]{:S(2)}) collective-permute-start(bf16[1,2,2,128,1024]{4,3,1,2,0:T(8,128)(2,1)} %get-tuple-element.244), channel_id=1, source_target_pairs={{0,4},{2,6},{4,0},{6,2},{8,12},{10,14},{12,8},{14,10},{16,20},{18,... | collective-permute-start | bytes 3145736 | tf_op jit(solution)/shard_map/cond/branch_1_fun/ppermute | solution.py:96
  383.7 3.5 collective-permute-start.7
  383.8 44.2 %collective-permute-start.9 = (bf16[512,1024]{1,0:T(8,128)(2,1)}, bf16[512,1024]{1,0:T(8,128)(2,1)}, u32[]{:S(2)}, u32[]{:S(2)}) collective-permute-start(bf16[512,1024]{1,0:T(8,128)(2,1)} %get-tuple-element.253), channel_id=1, source_target_pairs={{0,1},{1,0},{2,3},{3,2},{4,5},{5,4},{6,7},{7,6},{8,9},{9,8},{10,11... | collective-permute-start | bytes 3145736 | tf_op jit(solution)/shard_map/cond/branch_1_fun/ppermute | solution.py:56
  389.1 36.8 %collective-permute-start.8 = (bf16[1,2,2,3,128,512]{5,4,1,3,2,0:T(8,128)(2,1)}, bf16[1,2,2,3,128,512]{5,4,1,3,2,0:T(8,128)(2,1)}, u32[]{:S(2)}, u32[]{:S(2)}) collective-permute-start(bf16[1,2,2,3,128,512]{5,4,1,3,2,0:T(8,128)(2,1)} %get-tuple-element.252), channel_id=1, source_target_pairs={{0,4},{2,6},{4,0},{6,2},{8,12},{10,14},{12,8},{14,10},{16,20},{18,... | collective-permute-start | bytes 4718600 | tf_op jit(solution)/shard_map/cond/branch_1_fun/ppermute | solution.py:96
  428.9 3.5 collective-permute-start.10
  432.6 36.5 %collective-permute-start.11 = (bf16[1,2,2,3,128,512]{5,4,1,3,2,0:T(8,128)(2,1)S(1)}, bf16[1,2,2,3,128,512]{5,4,1,3,2,0:T(8,128)(2,1)S(1)}, u32[]{:S(2)}, u32[]{:S(2)}) collective-permute-start(bf16[1,2,2,3,128,512]{5,4,1,3,2,0:T(8,128)(2,1)S(1)} %get-tuple-element.465), channel_id=1, source_target_pairs={{0,4},{2,6},{4,0},{6,2},{8,12},{10,14},{12,8},{14,10},{16,20},{18,... | collective-permute-start | bytes 4718600 | tf_op jit(solution)/shard_map/cond/branch_1_fun/ppermute | solution.py:96
  435.7 2.7 collective-permute-start.12
  435.8 61.5 %collective-permute-start.14 = (bf16[512,1024]{1,0:T(8,128)(2,1)}, bf16[512,1024]{1,0:T(8,128)(2,1)}, u32[]{:S(2)}, u32[]{:S(2)}) collective-permute-start(bf16[512,1024]{1,0:T(8,128)(2,1)} %get-tuple-element.258), channel_id=1, source_target_pairs={{0,1},{1,0},{2,3},{3,2},{4,5},{5,4},{6,7},{7,6},{8,9},{9,8},{10,11... | collective-permute-start | bytes 3145736 | tf_op jit(solution)/shard_map/cond/branch_1_fun/ppermute | solution.py:56
  471.1 24.8 %collective-permute-start.13 = (bf16[1,2,2,128,1024]{4,3,1,2,0:T(8,128)(2,1)}, bf16[1,2,2,128,1024]{4,3,1,2,0:T(8,128)(2,1)}, u32[]{:S(2)}, u32[]{:S(2)}) collective-permute-start(bf16[1,2,2,128,1024]{4,3,1,2,0:T(8,128)(2,1)} %get-tuple-element.257), channel_id=1, source_target_pairs={{0,4},{2,6},{4,0},{6,2},{8,12},{10,14},{12,8},{14,10},{16,20},{18,... | collective-permute-start | bytes 3145736 | tf_op jit(solution)/shard_map/cond/branch_1_fun/ppermute | solution.py:96
  504.6 165.0 %reduce-scatter.11.cloned.1.call-start = ((), (), s32[]{:S(2)}) async-start(), calls=%async_computation.7 | async-start | bytes 2621440 | tf_op jit(solution)/shard_map/reduce_scatter | solution.py:596
  510.5 21.6 %collective-permute-start.37 = (bf16[2,1,128,1024]{3,2,1,0:T(8,128)(2,1)}, bf16[2,1,128,1024]{3,2,1,0:T(8,128)(2,1)}, u32[]{:S(2)}, u32[]{:S(2)}) collective-permute-start(bf16[2,1,128,1024]{3,2,1,0:T(8,128)(2,1)} %pad_maximum_fusion.19), channel_id=1, source_target_pairs={{0,4},{2,6},{4,0},{6,2},{8,12},{10,14},{12,8},{14,10},{16,20},{18,... | collective-permute-start | bytes 1572872 | tf_op jit(solution)/shard_map/cond/branch_1_fun/ppermute | solution.py:106
  515.9 18.4 %collective-permute-start.39 = (bf16[2,1,128,1024]{3,2,1,0:T(8,128)(2,1)}, bf16[2,1,128,1024]{3,2,1,0:T(8,128)(2,1)}, u32[]{:S(2)}, u32[]{:S(2)}) collective-permute-start(bf16[2,1,128,1024]{3,2,1,0:T(8,128)(2,1)} %pad_maximum_fusion.20), channel_id=1, source_target_pairs={{0,4},{2,6},{4,0},{6,2},{8,12},{10,14},{12,8},{14,10},{16,20},{18,... | collective-permute-start | bytes 1572872 | tf_op jit(solution)/shard_map/cond/branch_1_fun/ppermute | solution.py:106
  517.4 48.8 %collective-permute-start.32 = (bf16[4,128,1024]{2,1,0:T(8,128)(2,1)}, bf16[4,128,1024]{2,1,0:T(8,128)(2,1)}, u32[]{:S(2)}, u32[]{:S(2)}) collective-permute-start(bf16[4,128,1024]{2,1,0:T(8,128)(2,1)} %get-tuple-element.271), channel_id=1, source_target_pairs={{0,1},{1,0},{2,3},{3,2},{4,5},{5,4},{6,7},{7,6},{8,9},{9,8},{10,11... | collective-permute-start | bytes 3145736 | tf_op jit(solution)/shard_map/cond/branch_1_fun/ppermute | solution.py:56
  518.9 47.4 %collective-permute-start.41 = (bf16[4,128,1024]{2,1,0:T(8,128)(2,1)}, bf16[4,128,1024]{2,1,0:T(8,128)(2,1)}, u32[]{:S(2)}, u32[]{:S(2)}) collective-permute-start(bf16[4,128,1024]{2,1,0:T(8,128)(2,1)} %get-tuple-element.292), channel_id=1, source_target_pairs={{0,1},{1,0},{2,3},{3,2},{4,5},{5,4},{6,7},{7,6},{8,9},{9,8},{10,11... | collective-permute-start | bytes 3145736 | tf_op jit(solution)/shard_map/cond/branch_1_fun/ppermute | solution.py:56
  523.2 14.1 %collective-permute-start.33 = (bf16[2,1,3,64,1408]{4,3,2,1,0:T(8,128)(2,1)}, bf16[2,1,3,64,1408]{4,3,2,1,0:T(8,128)(2,1)}, u32[]{:S(2)}, u32[]{:S(2)}) collective-permute-start(bf16[2,1,3,64,1408]{4,3,2,1,0:T(8,128)(2,1)} %bitcast.488), channel_id=1, source_target_pairs={{0,2},{2,0},{4,6},{6,4},{8,10},{10,8},{12,14},{14,12},{16,18},{18,... | collective-permute-start | bytes 3244040 | tf_op jit(solution)/shard_map/cond/branch_1_fun/ppermute | solution.py:89
  534.4 8.4 %collective-permute-start.35 = (bf16[2,1,3,64,1408]{4,3,2,1,0:T(8,128)(2,1)}, bf16[2,1,3,64,1408]{4,3,2,1,0:T(8,128)(2,1)S(1)}, u32[]{:S(2)}, u32[]{:S(2)}) collective-permute-start(bf16[2,1,3,64,1408]{4,3,2,1,0:T(8,128)(2,1)} %bitcast.528), channel_id=1, source_target_pairs={{0,2},{2,0},{4,6},{6,4},{8,10},{10,8},{12,14},{14,12},{16,18},{18,... | collective-permute-start | bytes 3244040 | tf_op jit(solution)/shard_map/cond/branch_1_fun/ppermute | solution.py:89
  536.1 3.5 collective-permute-start.40
  538.8 26.8 %collective-permute-start.34 = (bf16[1,2,3,64,1408]{4,3,2,1,0:T(8,128)(2,1)S(1)}, bf16[1,2,3,64,1408]{4,3,2,1,0:T(8,128)(2,1)S(1)}, u32[]{:S(2)}, u32[]{:S(2)}) collective-permute-start(bf16[1,2,3,64,1408]{4,3,2,1,0:T(8,128)(2,1)S(1)} %get-tuple-element.491), channel_id=1, source_target_pairs={{0,4},{2,6},{4,0},{6,2},{8,12},{10,14},{12,8},{14,10},{16,20},{18,... | collective-permute-start | bytes 3244040 | tf_op jit(solution)/shard_map/cond/branch_1_fun/ppermute | solution.py:96
  543.1 45.1 %collective-permute-start.36 = (bf16[1,2,3,64,1408]{4,3,2,1,0:T(8,128)(2,1)S(1)}, bf16[1,2,3,64,1408]{4,3,2,1,0:T(8,128)(2,1)S(1)}, u32[]{:S(2)}, u32[]{:S(2)}) collective-permute-start(bf16[1,2,3,64,1408]{4,3,2,1,0:T(8,128)(2,1)S(1)} %get-tuple-element.499), channel_id=1, source_target_pairs={{0,4},{2,6},{4,0},{6,2},{8,12},{10,14},{12,8},{14,10},{16,20},{18,... | collective-permute-start | bytes 3244040 | tf_op jit(solution)/shard_map/cond/branch_1_fun/ppermute | solution.py:96
  589.6 10.1 %collective-permute-start.43 = (f32[2,4,512]{2,1,0:T(4,128)S(1)}, f32[2,4,512]{2,1,0:T(4,128)S(1)}, u32[]{:S(2)}, u32[]{:S(2)}) collective-permute-start(f32[2,4,512]{2,1,0:T(4,128)S(1)} %select_bitcast_fusion.10), channel_id=1, source_target_pairs={{0,16},{2,18},{4,20},{6,22},{8,24},{10,26},{12,28},{14,30},{16,0},... | collective-permute-start | bytes 49160 | tf_op jit(solution)/shard_map/cond/branch_1_fun/ppermute | solution.py:140
  600.4 5.5 collective-permute-start.44
  606.0 3.7 collective-permute-start.45
  609.8 8.2 %collective-permute-start.46 = (f32[2,4,64]{2,1,0:T(4,128)S(1)}, f32[2,4,64]{2,1,0:T(4,128)S(1)}, u32[]{:S(2)}, u32[]{:S(2)}) collective-permute-start(f32[2,4,64]{2,1,0:T(4,128)S(1)} %bitcast.544), channel_id=1, source_target_pairs={{0,2},{2,0},{4,6},{6,4},{8,10},{10,8},{12,14},{14,12},{16,18},{18,... | collective-permute-start | bytes 6152 | tf_op jit(solution)/shard_map/cond/branch_1_fun/ppermute | solution.py:140
  616.7 3.1 collective-permute-start.42
  624.5 4.6 collective-permute-start.60
  629.2 44.6 %collective-permute-start.61 = (bf16[1,2,2,3,64,512]{5,4,3,2,1,0:T(8,128)(2,1)S(1)}, bf16[1,2,2,3,64,512]{5,4,3,2,1,0:T(8,128)(2,1)S(1)}, u32[]{:S(2)}, u32[]{:S(2)}) collective-permute-start(bf16[1,2,2,3,64,512]{5,4,3,2,1,0:T(8,128)(2,1)S(1)} %get-tuple-element.581), channel_id=1, source_target_pairs={{0,4},{2,6},{4,0},{6,2},{8,12},{10,14},{12,8},{14,10},{16,20},{18,... | collective-permute-start | bytes 2359304 | tf_op jit(solution)/shard_map/ppermute | solution.py:96
  672.3 8.4 %collective-permute-start.63 = (bf16[1,2,2,1,64,512]{5,4,2,3,1,0:T(8,128)(2,1)S(1)}, bf16[1,2,2,1,64,512]{5,4,2,3,1,0:T(8,128)(2,1)S(1)}, u32[]{:S(2)}, u32[]{:S(2)}) collective-permute-start(bf16[1,2,2,1,64,512]{5,4,2,3,1,0:T(8,128)(2,1)S(1)} %get-tuple-element.601), channel_id=1, source_target_pairs={{0,4},{2,6},{4,0},{6,2},{8,12},{10,14},{12,8},{14,10},{16,20},{18,... | collective-permute-start | bytes 786440 | tf_op jit(solution)/shard_map/ppermute | solution.py:96
  (73 other events, 549.5 us)
Sparse Core Ops, SparseCore 0:
  188.3 149.4 reduce-scatter.4
  347.2 148.8 reduce-scatter.6
  504.7 111.5 reduce-scatter.8
  623.0 46.5 reduce-scatter.10
